TPU v7x, 32 devices: a whole 2x2x4 slice. The times are simulated.
32 devices in a mesh: space: 16 (over z, x, core), sub: 2 (over y).
Axes of the slice: x: 2, y: 2, z: 4, core: 2. Of those that a mesh axis runs over, the one named last changes fastest.
Arguments:
- positions: float32 [3, 32, 4, 3, 128], P(None, 'space', 'sub'), may hold values from 0 to 1
- charges: float32 [32, 4, 3, 128], P('space', 'sub'), may hold values from -0.6 to 0.6
- counts: int32 [32, 4, 3], P('space', 'sub'), may hold values from 64 to 128
Outputs:
- forces: float32 [3, 32, 4, 3, 128], P(None, 'space', 'sub')
Inputs may be any that keep to these rules, and one draw needn't show every extreme that they name: `counts`: slots 0 to count - 1 of a cell hold atoms; the others are padding.
All inputs are finite; a program needn't handle non-finite values.
Results may differ from a plain program's by a relative error of at most 0.0003.
Values sent between devices are 32-bit elements; how exact they have to be, the bound alone decides.
No kernel may reach another device: no remote copies, remote signals or barrier semaphores. Data moves between devices by JAX's collectives and lax.ppermute only.
A program may use at most 64 MiB of HBM per device.

v0:
```python
import math

import jax
import jax.numpy as jnp
from jax import lax
from jax.sharding import PartitionSpec as P

POINTS = 4
REACH = 4


SOFT_SQUARE = 0.0625
SPLIT_RATE = 0.8
FINE_WIDTHS = (1.0, 2.0)
FINE_WEIGHTS = (2.0, 0.5)
COARSE_FRACTIONS = (8.0, 4.0)
COARSE_WEIGHTS = (4.0, 2.0)
HIGHEST = lax.Precision.HIGHEST


def extended_2(value, sides, width):
    for axis, dim in sides:
        size, length = (lax.axis_size(axis), value.shape[dim])
        up = [(i, (i + 1) % size) for i in range(size)]
        down = [(j, i) for i, j in up]
        last = lax.slice_in_dim(value, length - width, length, axis=dim)
        first = lax.slice_in_dim(value, 0, width, axis=dim)
        before = lax.ppermute(last, axis, up)
        after = lax.ppermute(first, axis, down)
        value = jnp.concatenate([before, value, after], axis=dim)
    return value


def pair_force(own_pos, own_charge, other_pos, other_charge, offset_vec):
    shifted = own_pos - offset_vec.reshape((3,) + (1,) * (own_pos.ndim - 1))
    spread = shifted[..., :, None] - other_pos[..., None, :]
    square = jnp.sum(spread * spread, axis=0) + SOFT_SQUARE
    length = jnp.sqrt(square)
    factor = jax.scipy.special.erfc(SPLIT_RATE * length) / (square * length)
    factor = (
        factor
        + 2.0
        * SPLIT_RATE
        / math.sqrt(math.pi)
        * jnp.exp(-SPLIT_RATE * SPLIT_RATE * square)
        / square
    )
    stacked = jnp.concatenate([other_charge[None], other_charge[None] * other_pos], axis=0)
    moments = jnp.einsum("...ab,c...b->c...a", factor, stacked, precision=HIGHEST)
    return own_charge * (shifted * moments[0][None] - moments[1:])


def spline(shifted):
    magnitude = jnp.abs(shifted)
    inner = (4.0 - 6.0 * magnitude * magnitude + 3.0 * magnitude * magnitude * magnitude) / 6.0
    outer = (2.0 - magnitude) * (2.0 - magnitude) * (2.0 - magnitude) / 6.0
    return jnp.where(magnitude < 1.0, inner, jnp.where(magnitude < 2.0, outer, 0.0))


def spline_slope(shifted):
    magnitude = jnp.abs(shifted)
    inner = (9.0 * magnitude * magnitude - 12.0 * magnitude) / 6.0
    outer = -(2.0 - magnitude) * (2.0 - magnitude) / 2.0
    return jnp.sign(shifted) * jnp.where(
        magnitude < 1.0, inner, jnp.where(magnitude < 2.0, outer, 0.0)
    )


def spline_tables(fraction):
    offsets = lax.iota(jnp.int32, POINTS + 3).astype(jnp.float32) - 1.0
    shifted = POINTS * fraction[..., None] - offsets
    return (spline(shifted), spline_slope(shifted))


def make_boxes(coords, charged):
    weight_x = spline_tables(coords[0])[0]
    weight_y = spline_tables(coords[1])[0]
    weight_z = spline_tables(coords[2])[0]
    first = (charged[..., None] * weight_x)[..., :, None] * weight_y[..., None, :]
    return jnp.einsum("...aef,...ag->...efg", first, weight_z, precision=HIGHEST)


def placement_table():
    shape = (POINTS + 3, POINTS, 3)
    entry = lax.broadcasted_iota(jnp.int32, shape, 0)
    inside = lax.broadcasted_iota(jnp.int32, shape, 1)
    which = lax.broadcasted_iota(jnp.int32, shape, 2)
    return (entry - 1 == (which - 1) * POINTS + inside).astype(jnp.float32)


def pick_table(cells, length, first, period):
    shape = (cells, POINTS + 3, length)
    cell_idx = lax.broadcasted_iota(jnp.int32, shape, 0)
    entry = lax.broadcasted_iota(jnp.int32, shape, 1)
    point = lax.broadcasted_iota(jnp.int32, shape, 2)
    return (jnp.mod(POINTS * cell_idx + first + entry, period) == point).astype(jnp.float32)


def gauss_matrix(length, width, first_row, rows):
    row_idx = first_row + lax.broadcasted_iota(jnp.int32, (rows, length), 0)
    col_idx = lax.broadcasted_iota(jnp.int32, (rows, length), 1)
    dist = jnp.mod(row_idx - col_idx, length)
    dist = jnp.minimum(dist, length - dist).astype(jnp.float32)
    return jnp.exp(-dist * dist / (2.0 * width * width))


def taps_for(width):
    return [math.exp(-(step * step) / (2.0 * width * width)) for step in range(-REACH, REACH + 1)]


def long_forces(coords, charged, point_box):
    weight_x, slope_x = spline_tables(coords[0])
    weight_y, slope_y = spline_tables(coords[1])
    weight_z, slope_z = spline_tables(coords[2])
    along_z = jnp.einsum("xyzag,xyzefg->xyzaef", weight_z, point_box, precision=HIGHEST)
    sloped_z = jnp.einsum("xyzag,xyzefg->xyzaef", slope_z, point_box, precision=HIGHEST)
    force_x = jnp.einsum("xyzae,xyzaf,xyzaef->xyza", slope_x, weight_y, along_z, precision=HIGHEST)
    force_y = jnp.einsum("xyzae,xyzaf,xyzaef->xyza", weight_x, slope_y, along_z, precision=HIGHEST)
    force_z = jnp.einsum(
        "xyzae,xyzaf,xyzaef->xyza", weight_x, weight_y, sloped_z, precision=HIGHEST
    )
    return -POINTS * charged * jnp.stack([force_x, force_y, force_z])


def short_forces(packed, beside_all):
    extended = jnp.concatenate(
        [beside_all[:, :, :, -1:], beside_all, beside_all[:, :, :, :1]], axis=3
    )

    def add_offset(offset, total):
        start_x = offset // 9
        start_y = offset // 3 % 3
        start_z = offset % 3
        nearby = lax.dynamic_slice(extended, (0, start_x, start_y, start_z, 0), packed.shape)
        offset_vec = jnp.stack([start_x, start_y, start_z]).astype(jnp.float32) - 1.0
        return total + pair_force(packed[:3], packed[3], nearby[:3], nearby[3], offset_vec)

    return lax.fori_loop(0, 27, add_offset, jnp.zeros((3,) + packed.shape[1:], jnp.float32))


def body(positions, charges, counts):
    live_mask = (lax.broadcasted_iota(jnp.int32, charges.shape, 3) < counts[..., None]).astype(
        jnp.float32
    )
    charged = charges * live_mask
    packed = jnp.concatenate([positions, charged[None]], axis=0)
    beside_all = extended_2(packed, (("space", 1), ("sub", 2)), 1)
    brick_x, brick_y, brick_z = (charges.shape[0], charges.shape[1], charges.shape[2])
    short = short_forces(packed, beside_all)
    boxes = make_boxes(beside_all[:3], beside_all[3])
    table = placement_table()
    placed_x = sum(
        (
            jnp.einsum(
                "XYZefg,ej->XYZjfg",
                boxes[2 - which : 2 - which + brick_x],
                table[:, :, which],
                precision=HIGHEST,
            )
            for which in range(3)
        )
    )
    placed_y = sum(
        (
            jnp.einsum(
                "XYZjfg,fl->XYZjlg",
                placed_x[:, 2 - which : 2 - which + brick_y],
                table[:, :, which],
                precision=HIGHEST,
            )
            for which in range(3)
        )
    )
    placed_z = sum(
        (
            jnp.einsum(
                "XYZjlg,gm->XYZjlm",
                jnp.roll(placed_y, which - 1, axis=2),
                table[:, :, which],
                precision=HIGHEST,
            )
            for which in range(3)
        )
    )
    local_x, local_y, local_z = (POINTS * brick_x, POINTS * brick_y, POINTS * brick_z)
    charge_grid = placed_z.transpose(0, 3, 1, 4, 2, 5).reshape(local_x, local_y, local_z)
    margin_grid = extended_2(charge_grid, (("space", 0), ("sub", 1)), REACH + 2)
    rows_x, rows_y = (local_x + 4, local_y + 4)
    fine = jnp.zeros((rows_x, rows_y, local_z), jnp.float32)
    for width, weight in zip(FINE_WIDTHS, FINE_WEIGHTS):
        taps = taps_for(width)
        section = sum(
            (
                taps[step + REACH]
                * lax.slice_in_dim(margin_grid, REACH + step, REACH + step + rows_x, axis=0)
                for step in range(-REACH, REACH + 1)
            )
        )
        section = sum(
            (
                taps[step + REACH]
                * lax.slice_in_dim(section, REACH + step, REACH + step + rows_y, axis=1)
                for step in range(-REACH, REACH + 1)
            )
        )
        section = sum(
            (
                taps[step + REACH] * jnp.roll(section, -step, axis=2)
                for step in range(-REACH, REACH + 1)
            )
        )
        fine = fine + weight * section
    coarse_charge = (
        charge_grid.reshape(local_x // 2, 2, local_y // 2, 2, local_z // 2, 2).sum(axis=(1, 3, 5))
        * 0.125
    )
    coarse_x, coarse_y, coarse_z = (local_x // 2, local_y // 2, local_z // 2)
    total_x = coarse_x * lax.axis_size("space")
    total_y = coarse_y * lax.axis_size("sub")
    first_x = lax.axis_index("space") * coarse_x - 1
    first_y = lax.axis_index("sub") * coarse_y - 1
    matrices_x = [
        gauss_matrix(total_x, total_x / fraction, first_x, coarse_x + 2)
        for fraction in COARSE_FRACTIONS
    ]
    matrices_y = [
        gauss_matrix(total_y, total_y / fraction, first_y, coarse_y + 2)
        for fraction in COARSE_FRACTIONS
    ]
    matrices_z = [
        gauss_matrix(coarse_z, coarse_z / fraction, 0, coarse_z) for fraction in COARSE_FRACTIONS
    ]
    rows_sub = lax.all_gather(coarse_charge, "sub", axis=1, tiled=True)
    whole = lax.all_gather(rows_sub, "space", axis=0, tiled=True)
    contracted = []
    for number in range(2):
        section = jnp.einsum("ri,ijk->rjk", matrices_x[number], whole, precision=HIGHEST)
        contracted.append(jnp.einsum("sj,rjk->rsk", matrices_y[number], section, precision=HIGHEST))
    coarse = jnp.zeros((coarse_x + 2, coarse_y + 2, coarse_z), jnp.float32)
    for number in range(2):
        coarse = coarse + COARSE_WEIGHTS[number] * jnp.einsum(
            "tk,rsk->rst", matrices_z[number], contracted[number], precision=HIGHEST
        )
    lifted = jnp.repeat(jnp.repeat(jnp.repeat(coarse, 2, axis=0), 2, axis=1), 2, axis=2)
    potential = fine + lifted
    pick_x = pick_table(brick_x, rows_x, 1, rows_x)
    pick_y = pick_table(brick_y, rows_y, 1, rows_y)
    pick_z = pick_table(brick_z, local_z, -1, local_z)
    point_box = jnp.einsum("Xei,ijk->Xejk", pick_x, potential, precision=HIGHEST)
    point_box = jnp.einsum("Yfj,Xejk->XYefk", pick_y, point_box, precision=HIGHEST)
    point_box = jnp.einsum("Zgk,XYefk->XYZefg", pick_z, point_box, precision=HIGHEST)
    return short + long_forces(positions, charged, point_box)


def solution(mesh):
    in_specs = (
        P(None, "space", "sub", None, None),
        P("space", "sub", None, None),
        P("space", "sub", None),
    )
    out_specs = P(None, "space", "sub", None, None)
    return jax.shard_map(body, mesh=mesh, in_specs=in_specs, out_specs=out_specs, check_vma=False)
```

profile of v0, /device:TPU:0, one launch (start us, length us, event | category | flops | bytes accessed | tf_op | source)
XLA Modules:
  0.0 197.8 jit_solution(11479206783595300274)
XLA Ops:
  2.8 5.0 %collective-permute-start.1 = (f32[4,1,2,3,128]{4,2,3,1,0:T(2,128)S(1)}, f32[4,1,2,3,128]{4,2,3,1,0:T(2,128)S(1)}, u32[]{:S(2)}, u32[]{:S(2)}) collective-permute-start(f32[4,1,2,3,128]{4,2,3,1,0:T(2,128)S(1)} %get-tuple-element.288), channel_id=1, source_target_pairs={{2,0},{4,2},{6,4},{8,6},{10,8},{12,10},{14,12},{16,14},{18,16},{20... | collective-permute-start | bytes 36872 | tf_op jit(solution)/shard_map/ppermute | solution.py:29
  10.0 2.0 %collective-permute-start.2 = (f32[4,4,1,3,128]{4,2,3,1,0:T(1,128)S(1)}, f32[4,4,1,3,128]{4,2,3,1,0:T(1,128)S(1)}, u32[]{:S(2)}, u32[]{:S(2)}) collective-permute-start(f32[4,4,1,3,128]{4,2,3,1,0:T(1,128)S(1)} %get-tuple-element.285), channel_id=1, source_target_pairs={{0,1},{1,0},{2,3},{3,2},{4,5},{5,4},{6,7},{7,6},{8,9},{9,8},{10,11... | collective-permute-start | bytes 73736 | tf_op jit(solution)/shard_map/ppermute | solution.py:28
  14.0 1.8 collective-permute-done.3
  16.3 2.6 %fusion.85 = f32[4,4,3,7,7,7]{5,4,3,2,1,0:T(8,128)S(1)} fusion(f32[4,4,3,128,7]{3,4,2,1,0:T(8,128)S(1)} %get-tuple-element.301, f32[4,4,3,128,7]{3,4,2,1,0:T(8,128)S(1)} %get-tuple-element.300, f32[4,4,3,128]{3,2,1,0:T(4,128)S(1)} %copy.215, f32[7]{0:T(128)S(1)} %convert_add_fusion), kind=kOutput, calls=%fused_computation.102 | convolution fusion | flops 26363904 | bytes 434524 | tf_op jit(solution)/shard_map/...aef,...ag->...efg/dot_general | solution.py:80
  22.9 4.4 %all_gather.6 = f32[4,8,6]{2,0,1:T(4,128)S(1)} all-gather(f32[4,4,6]{2,0,1:T(4,128)S(1)} %copy.224), channel_id=1, replica_groups=mesh['space'=16,'sub'=2] {'sub'}, dimensions={1}, use_global_device_ids=true | all-gather | bytes 1152 | tf_op jit(solution)/shard_map/all_gather | solution.py:233
  27.3 19.6 %all_gather.7 = f32[64,8,6]{2,1,0:T(8,128)S(1)} all-gather(f32[4,8,6]{2,1,0:T(8,128)S(1)} %copy.225), channel_id=1, replica_groups=mesh['space'=16,'sub'=2] {'space'}, dimensions={0}, use_global_device_ids=true | all-gather | bytes 13056 | tf_op jit(solution)/shard_map/all_gather | solution.py:234
  49.5 4.1 %collective-permute-start.5 = (f32[6,8,12]{1,0,2:T(8,128)S(1)}, f32[6,8,12]{1,0,2:T(8,128)S(1)}, u32[]{:S(2)}, u32[]{:S(2)}) collective-permute-start(f32[6,8,12]{1,0,2:T(8,128)S(1)} %get-tuple-element.284), channel_id=1, source_target_pairs={{2,0},{4,2},{6,4},{8,6},{10,8},{12,10},{14,12},{16,14},{18,16},{20... | collective-permute-start | bytes 6920 | tf_op jit(solution)/shard_map/ppermute | solution.py:29
  53.7 130.5 %while.17 = (s32[]{:T(128)}, f32[3,2,2,3,128]{4,0,3,2,1:T(4,128)S(1)}, f32[1,2,2,3,128]{4,3,2,1,0:T(4,128)S(1)}, f32[3,2,2,3,128]{4,0,3,2,1:T(4,128)S(1)}, f32[4...) while((s32[]{:T(128)}, ...), condition=%wide.region_2.3_spmd.clone, body=%wide.region_0.2_spmd.clone.sunk | while | flops 24422448 | bytes 2021951 | solution.py:138
  54.0 0.8 multiply_reduce_fusion.7
  54.9 3.5 %convolution_bitcast_fusion.7 = f32[4,2,2,3,128]{4,0,3,2,1:T(4,128)S(1)} fusion(f32[2,2,3,128,128]{4,3,2,1,0:T(8,128)S(1)} %multiply_reduce_fusion.7, f32[3,2,2,3,128]{4,0,3,2,1:T(4,128)S(1)} %copy_multiply_fusion.2, f32[1,2,2,3,128]{4,0,3,2,1:T(1,128)S(1)} %copy.343), kind=kOutput, calls=%fused_computation.4.clone.1 | convolution fusion | flops 22812672 | bytes 835584 | tf_op jit(solution)/shard_map/while/body/eval_jaxpr/...ab,c...b->c...a/dot_general | solution.py:49
  58.8 0.8 multiply_reduce_fusion.7
  59.8 3.5 %convolution_bitcast_fusion.7 = f32[4,2,2,3,128]{4,0,3,2,1:T(4,128)S(1)} fusion(f32[2,2,3,128,128]{4,3,2,1,0:T(8,128)S(1)} %multiply_reduce_fusion.7, f32[3,2,2,3,128]{4,0,3,2,1:T(4,128)S(1)} %copy_multiply_fusion.2, f32[1,2,2,3,128]{4,0,3,2,1:T(1,128)S(1)} %copy.343), kind=kOutput, calls=%fused_computation.4.clone.1 | convolution fusion | flops 22812672 | bytes 835584 | tf_op jit(solution)/shard_map/while/body/eval_jaxpr/...ab,c...b->c...a/dot_general | solution.py:49
  63.7 0.8 multiply_reduce_fusion.7
  64.6 3.5 %convolution_bitcast_fusion.7 = f32[4,2,2,3,128]{4,0,3,2,1:T(4,128)S(1)} fusion(f32[2,2,3,128,128]{4,3,2,1,0:T(8,128)S(1)} %multiply_reduce_fusion.7, f32[3,2,2,3,128]{4,0,3,2,1:T(4,128)S(1)} %copy_multiply_fusion.2, f32[1,2,2,3,128]{4,0,3,2,1:T(1,128)S(1)} %copy.343), kind=kOutput, calls=%fused_computation.4.clone.1 | convolution fusion | flops 22812672 | bytes 835584 | tf_op jit(solution)/shard_map/while/body/eval_jaxpr/...ab,c...b->c...a/dot_general | solution.py:49
  68.5 0.8 multiply_reduce_fusion.7
  69.4 3.5 %convolution_bitcast_fusion.7 = f32[4,2,2,3,128]{4,0,3,2,1:T(4,128)S(1)} fusion(f32[2,2,3,128,128]{4,3,2,1,0:T(8,128)S(1)} %multiply_reduce_fusion.7, f32[3,2,2,3,128]{4,0,3,2,1:T(4,128)S(1)} %copy_multiply_fusion.2, f32[1,2,2,3,128]{4,0,3,2,1:T(1,128)S(1)} %copy.343), kind=kOutput, calls=%fused_computation.4.clone.1 | convolution fusion | flops 22812672 | bytes 835584 | tf_op jit(solution)/shard_map/while/body/eval_jaxpr/...ab,c...b->c...a/dot_general | solution.py:49
  73.3 0.8 multiply_reduce_fusion.7
  74.3 3.5 %convolution_bitcast_fusion.7 = f32[4,2,2,3,128]{4,0,3,2,1:T(4,128)S(1)} fusion(f32[2,2,3,128,128]{4,3,2,1,0:T(8,128)S(1)} %multiply_reduce_fusion.7, f32[3,2,2,3,128]{4,0,3,2,1:T(4,128)S(1)} %copy_multiply_fusion.2, f32[1,2,2,3,128]{4,0,3,2,1:T(1,128)S(1)} %copy.343), kind=kOutput, calls=%fused_computation.4.clone.1 | convolution fusion | flops 22812672 | bytes 835584 | tf_op jit(solution)/shard_map/while/body/eval_jaxpr/...ab,c...b->c...a/dot_general | solution.py:49
  79.1 3.5 %convolution_bitcast_fusion.7 = f32[4,2,2,3,128]{4,0,3,2,1:T(4,128)S(1)} fusion(f32[2,2,3,128,128]{4,3,2,1,0:T(8,128)S(1)} %multiply_reduce_fusion.7, f32[3,2,2,3,128]{4,0,3,2,1:T(4,128)S(1)} %copy_multiply_fusion.2, f32[1,2,2,3,128]{4,0,3,2,1:T(1,128)S(1)} %copy.343), kind=kOutput, calls=%fused_computation.4.clone.1 | convolution fusion | flops 22812672 | bytes 835584 | tf_op jit(solution)/shard_map/while/body/eval_jaxpr/...ab,c...b->c...a/dot_general | solution.py:49
  83.9 3.5 %convolution_bitcast_fusion.7 = f32[4,2,2,3,128]{4,0,3,2,1:T(4,128)S(1)} fusion(f32[2,2,3,128,128]{4,3,2,1,0:T(8,128)S(1)} %multiply_reduce_fusion.7, f32[3,2,2,3,128]{4,0,3,2,1:T(4,128)S(1)} %copy_multiply_fusion.2, f32[1,2,2,3,128]{4,0,3,2,1:T(1,128)S(1)} %copy.343), kind=kOutput, calls=%fused_computation.4.clone.1 | convolution fusion | flops 22812672 | bytes 835584 | tf_op jit(solution)/shard_map/while/body/eval_jaxpr/...ab,c...b->c...a/dot_general | solution.py:49
  88.8 3.5 %convolution_bitcast_fusion.7 = f32[4,2,2,3,128]{4,0,3,2,1:T(4,128)S(1)} fusion(f32[2,2,3,128,128]{4,3,2,1,0:T(8,128)S(1)} %multiply_reduce_fusion.7, f32[3,2,2,3,128]{4,0,3,2,1:T(4,128)S(1)} %copy_multiply_fusion.2, f32[1,2,2,3,128]{4,0,3,2,1:T(1,128)S(1)} %copy.343), kind=kOutput, calls=%fused_computation.4.clone.1 | convolution fusion | flops 22812672 | bytes 835584 | tf_op jit(solution)/shard_map/while/body/eval_jaxpr/...ab,c...b->c...a/dot_general | solution.py:49
  93.6 3.5 %convolution_bitcast_fusion.7 = f32[4,2,2,3,128]{4,0,3,2,1:T(4,128)S(1)} fusion(f32[2,2,3,128,128]{4,3,2,1,0:T(8,128)S(1)} %multiply_reduce_fusion.7, f32[3,2,2,3,128]{4,0,3,2,1:T(4,128)S(1)} %copy_multiply_fusion.2, f32[1,2,2,3,128]{4,0,3,2,1:T(1,128)S(1)} %copy.343), kind=kOutput, calls=%fused_computation.4.clone.1 | convolution fusion | flops 22812672 | bytes 835584 | tf_op jit(solution)/shard_map/while/body/eval_jaxpr/...ab,c...b->c...a/dot_general | solution.py:49
  97.5 0.8 multiply_reduce_fusion.7
  98.4 3.5 %convolution_bitcast_fusion.7 = f32[4,2,2,3,128]{4,0,3,2,1:T(4,128)S(1)} fusion(f32[2,2,3,128,128]{4,3,2,1,0:T(8,128)S(1)} %multiply_reduce_fusion.7, f32[3,2,2,3,128]{4,0,3,2,1:T(4,128)S(1)} %copy_multiply_fusion.2, f32[1,2,2,3,128]{4,0,3,2,1:T(1,128)S(1)} %copy.343), kind=kOutput, calls=%fused_computation.4.clone.1 | convolution fusion | flops 22812672 | bytes 835584 | tf_op jit(solution)/shard_map/while/body/eval_jaxpr/...ab,c...b->c...a/dot_general | solution.py:49
  103.3 3.5 %convolution_bitcast_fusion.7 = f32[4,2,2,3,128]{4,0,3,2,1:T(4,128)S(1)} fusion(f32[2,2,3,128,128]{4,3,2,1,0:T(8,128)S(1)} %multiply_reduce_fusion.7, f32[3,2,2,3,128]{4,0,3,2,1:T(4,128)S(1)} %copy_multiply_fusion.2, f32[1,2,2,3,128]{4,0,3,2,1:T(1,128)S(1)} %copy.343), kind=kOutput, calls=%fused_computation.4.clone.1 | convolution fusion | flops 22812672 | bytes 835584 | tf_op jit(solution)/shard_map/while/body/eval_jaxpr/...ab,c...b->c...a/dot_general | solution.py:49
  107.2 0.8 multiply_reduce_fusion.7
  108.1 3.5 %convolution_bitcast_fusion.7 = f32[4,2,2,3,128]{4,0,3,2,1:T(4,128)S(1)} fusion(f32[2,2,3,128,128]{4,3,2,1,0:T(8,128)S(1)} %multiply_reduce_fusion.7, f32[3,2,2,3,128]{4,0,3,2,1:T(4,128)S(1)} %copy_multiply_fusion.2, f32[1,2,2,3,128]{4,0,3,2,1:T(1,128)S(1)} %copy.343), kind=kOutput, calls=%fused_computation.4.clone.1 | convolution fusion | flops 22812672 | bytes 835584 | tf_op jit(solution)/shard_map/while/body/eval_jaxpr/...ab,c...b->c...a/dot_general | solution.py:49
  112.9 3.5 %convolution_bitcast_fusion.7 = f32[4,2,2,3,128]{4,0,3,2,1:T(4,128)S(1)} fusion(f32[2,2,3,128,128]{4,3,2,1,0:T(8,128)S(1)} %multiply_reduce_fusion.7, f32[3,2,2,3,128]{4,0,3,2,1:T(4,128)S(1)} %copy_multiply_fusion.2, f32[1,2,2,3,128]{4,0,3,2,1:T(1,128)S(1)} %copy.343), kind=kOutput, calls=%fused_computation.4.clone.1 | convolution fusion | flops 22812672 | bytes 835584 | tf_op jit(solution)/shard_map/while/body/eval_jaxpr/...ab,c...b->c...a/dot_general | solution.py:49
  116.9 0.8 multiply_reduce_fusion.7
  117.8 3.5 %convolution_bitcast_fusion.7 = f32[4,2,2,3,128]{4,0,3,2,1:T(4,128)S(1)} fusion(f32[2,2,3,128,128]{4,3,2,1,0:T(8,128)S(1)} %multiply_reduce_fusion.7, f32[3,2,2,3,128]{4,0,3,2,1:T(4,128)S(1)} %copy_multiply_fusion.2, f32[1,2,2,3,128]{4,0,3,2,1:T(1,128)S(1)} %copy.343), kind=kOutput, calls=%fused_computation.4.clone.1 | convolution fusion | flops 22812672 | bytes 835584 | tf_op jit(solution)/shard_map/while/body/eval_jaxpr/...ab,c...b->c...a/dot_general | solution.py:49
  122.6 3.5 %convolution_bitcast_fusion.7 = f32[4,2,2,3,128]{4,0,3,2,1:T(4,128)S(1)} fusion(f32[2,2,3,128,128]{4,3,2,1,0:T(8,128)S(1)} %multiply_reduce_fusion.7, f32[3,2,2,3,128]{4,0,3,2,1:T(4,128)S(1)} %copy_multiply_fusion.2, f32[1,2,2,3,128]{4,0,3,2,1:T(1,128)S(1)} %copy.343), kind=kOutput, calls=%fused_computation.4.clone.1 | convolution fusion | flops 22812672 | bytes 835584 | tf_op jit(solution)/shard_map/while/body/eval_jaxpr/...ab,c...b->c...a/dot_general | solution.py:49
  126.5 0.8 multiply_reduce_fusion.7
  127.4 3.5 %convolution_bitcast_fusion.7 = f32[4,2,2,3,128]{4,0,3,2,1:T(4,128)S(1)} fusion(f32[2,2,3,128,128]{4,3,2,1,0:T(8,128)S(1)} %multiply_reduce_fusion.7, f32[3,2,2,3,128]{4,0,3,2,1:T(4,128)S(1)} %copy_multiply_fusion.2, f32[1,2,2,3,128]{4,0,3,2,1:T(1,128)S(1)} %copy.343), kind=kOutput, calls=%fused_computation.4.clone.1 | convolution fusion | flops 22812672 | bytes 835584 | tf_op jit(solution)/shard_map/while/body/eval_jaxpr/...ab,c...b->c...a/dot_general | solution.py:49
  132.3 3.5 %convolution_bitcast_fusion.7 = f32[4,2,2,3,128]{4,0,3,2,1:T(4,128)S(1)} fusion(f32[2,2,3,128,128]{4,3,2,1,0:T(8,128)S(1)} %multiply_reduce_fusion.7, f32[3,2,2,3,128]{4,0,3,2,1:T(4,128)S(1)} %copy_multiply_fusion.2, f32[1,2,2,3,128]{4,0,3,2,1:T(1,128)S(1)} %copy.343), kind=kOutput, calls=%fused_computation.4.clone.1 | convolution fusion | flops 22812672 | bytes 835584 | tf_op jit(solution)/shard_map/while/body/eval_jaxpr/...ab,c...b->c...a/dot_general | solution.py:49
  136.2 0.8 multiply_reduce_fusion.7
  137.1 3.5 %convolution_bitcast_fusion.7 = f32[4,2,2,3,128]{4,0,3,2,1:T(4,128)S(1)} fusion(f32[2,2,3,128,128]{4,3,2,1,0:T(8,128)S(1)} %multiply_reduce_fusion.7, f32[3,2,2,3,128]{4,0,3,2,1:T(4,128)S(1)} %copy_multiply_fusion.2, f32[1,2,2,3,128]{4,0,3,2,1:T(1,128)S(1)} %copy.343), kind=kOutput, calls=%fused_computation.4.clone.1 | convolution fusion | flops 22812672 | bytes 835584 | tf_op jit(solution)/shard_map/while/body/eval_jaxpr/...ab,c...b->c...a/dot_general | solution.py:49
  141.9 3.5 %convolution_bitcast_fusion.7 = f32[4,2,2,3,128]{4,0,3,2,1:T(4,128)S(1)} fusion(f32[2,2,3,128,128]{4,3,2,1,0:T(8,128)S(1)} %multiply_reduce_fusion.7, f32[3,2,2,3,128]{4,0,3,2,1:T(4,128)S(1)} %copy_multiply_fusion.2, f32[1,2,2,3,128]{4,0,3,2,1:T(1,128)S(1)} %copy.343), kind=kOutput, calls=%fused_computation.4.clone.1 | convolution fusion | flops 22812672 | bytes 835584 | tf_op jit(solution)/shard_map/while/body/eval_jaxpr/...ab,c...b->c...a/dot_general | solution.py:49
  146.8 3.5 %convolution_bitcast_fusion.7 = f32[4,2,2,3,128]{4,0,3,2,1:T(4,128)S(1)} fusion(f32[2,2,3,128,128]{4,3,2,1,0:T(8,128)S(1)} %multiply_reduce_fusion.7, f32[3,2,2,3,128]{4,0,3,2,1:T(4,128)S(1)} %copy_multiply_fusion.2, f32[1,2,2,3,128]{4,0,3,2,1:T(1,128)S(1)} %copy.343), kind=kOutput, calls=%fused_computation.4.clone.1 | convolution fusion | flops 22812672 | bytes 835584 | tf_op jit(solution)/shard_map/while/body/eval_jaxpr/...ab,c...b->c...a/dot_general | solution.py:49
  151.6 3.5 %convolution_bitcast_fusion.7 = f32[4,2,2,3,128]{4,0,3,2,1:T(4,128)S(1)} fusion(f32[2,2,3,128,128]{4,3,2,1,0:T(8,128)S(1)} %multiply_reduce_fusion.7, f32[3,2,2,3,128]{4,0,3,2,1:T(4,128)S(1)} %copy_multiply_fusion.2, f32[1,2,2,3,128]{4,0,3,2,1:T(1,128)S(1)} %copy.343), kind=kOutput, calls=%fused_computation.4.clone.1 | convolution fusion | flops 22812672 | bytes 835584 | tf_op jit(solution)/shard_map/while/body/eval_jaxpr/...ab,c...b->c...a/dot_general | solution.py:49
  156.5 3.5 %convolution_bitcast_fusion.7 = f32[4,2,2,3,128]{4,0,3,2,1:T(4,128)S(1)} fusion(f32[2,2,3,128,128]{4,3,2,1,0:T(8,128)S(1)} %multiply_reduce_fusion.7, f32[3,2,2,3,128]{4,0,3,2,1:T(4,128)S(1)} %copy_multiply_fusion.2, f32[1,2,2,3,128]{4,0,3,2,1:T(1,128)S(1)} %copy.343), kind=kOutput, calls=%fused_computation.4.clone.1 | convolution fusion | flops 22812672 | bytes 835584 | tf_op jit(solution)/shard_map/while/body/eval_jaxpr/...ab,c...b->c...a/dot_general | solution.py:49
  161.3 3.5 %convolution_bitcast_fusion.7 = f32[4,2,2,3,128]{4,0,3,2,1:T(4,128)S(1)} fusion(f32[2,2,3,128,128]{4,3,2,1,0:T(8,128)S(1)} %multiply_reduce_fusion.7, f32[3,2,2,3,128]{4,0,3,2,1:T(4,128)S(1)} %copy_multiply_fusion.2, f32[1,2,2,3,128]{4,0,3,2,1:T(1,128)S(1)} %copy.343), kind=kOutput, calls=%fused_computation.4.clone.1 | convolution fusion | flops 22812672 | bytes 835584 | tf_op jit(solution)/shard_map/while/body/eval_jaxpr/...ab,c...b->c...a/dot_general | solution.py:49
  166.1 3.5 %convolution_bitcast_fusion.7 = f32[4,2,2,3,128]{4,0,3,2,1:T(4,128)S(1)} fusion(f32[2,2,3,128,128]{4,3,2,1,0:T(8,128)S(1)} %multiply_reduce_fusion.7, f32[3,2,2,3,128]{4,0,3,2,1:T(4,128)S(1)} %copy_multiply_fusion.2, f32[1,2,2,3,128]{4,0,3,2,1:T(1,128)S(1)} %copy.343), kind=kOutput, calls=%fused_computation.4.clone.1 | convolution fusion | flops 22812672 | bytes 835584 | tf_op jit(solution)/shard_map/while/body/eval_jaxpr/...ab,c...b->c...a/dot_general | solution.py:49
  171.0 3.5 %convolution_bitcast_fusion.7 = f32[4,2,2,3,128]{4,0,3,2,1:T(4,128)S(1)} fusion(f32[2,2,3,128,128]{4,3,2,1,0:T(8,128)S(1)} %multiply_reduce_fusion.7, f32[3,2,2,3,128]{4,0,3,2,1:T(4,128)S(1)} %copy_multiply_fusion.2, f32[1,2,2,3,128]{4,0,3,2,1:T(1,128)S(1)} %copy.343), kind=kOutput, calls=%fused_computation.4.clone.1 | convolution fusion | flops 22812672 | bytes 835584 | tf_op jit(solution)/shard_map/while/body/eval_jaxpr/...ab,c...b->c...a/dot_general | solution.py:49
  175.8 3.5 %convolution_bitcast_fusion.7 = f32[4,2,2,3,128]{4,0,3,2,1:T(4,128)S(1)} fusion(f32[2,2,3,128,128]{4,3,2,1,0:T(8,128)S(1)} %multiply_reduce_fusion.7, f32[3,2,2,3,128]{4,0,3,2,1:T(4,128)S(1)} %copy_multiply_fusion.2, f32[1,2,2,3,128]{4,0,3,2,1:T(1,128)S(1)} %copy.343), kind=kOutput, calls=%fused_computation.4.clone.1 | convolution fusion | flops 22812672 | bytes 835584 | tf_op jit(solution)/shard_map/while/body/eval_jaxpr/...ab,c...b->c...a/dot_general | solution.py:49
  180.6 3.5 %convolution_bitcast_fusion.7 = f32[4,2,2,3,128]{4,0,3,2,1:T(4,128)S(1)} fusion(f32[2,2,3,128,128]{4,3,2,1,0:T(8,128)S(1)} %multiply_reduce_fusion.7, f32[3,2,2,3,128]{4,0,3,2,1:T(4,128)S(1)} %copy_multiply_fusion.2, f32[1,2,2,3,128]{4,0,3,2,1:T(1,128)S(1)} %copy.343), kind=kOutput, calls=%fused_computation.4.clone.1 | convolution fusion | flops 22812672 | bytes 835584 | tf_op jit(solution)/shard_map/while/body/eval_jaxpr/...ab,c...b->c...a/dot_general | solution.py:49
  185.2 1.5 collective-permute-start.7
  187.3 2.5 %collective-permute-done.6 = f32[20,6,12]{1,0,2:T(8,128)S(1)} collective-permute-done((f32[20,6,12]{1,0,2:T(8,128)S(1)}, f32[20,6,12]{1,0,2:T(8,128)S(1)}, u32[]{:S(2)}, u32[]{:S(2)}) %collective-permute-start.6) | collective-permute-done | bytes 5792 | tf_op jit(solution)/shard_map/ppermute | solution.py:28
  189.8 1.6 collective-permute-done.7
  (511 shorter events, 45.6 us)
Async XLA Ops:
  0.0 15.8 %copy-start = (f32[3,2,2,3,128]{4,2,3,1,0:T(2,128)S(1)}, f32[3,2,2,3,128]{4,2,3,1,0:T(2,128)}, u32[]{:S(2)}) copy-start(f32[3,2,2,3,128]{4,2,3,1,0:T(2,128)} %param.5) | copy-start | bytes 55300
  2.3 6.8 %collective-permute-start = (f32[4,1,2,3,128]{4,2,3,1,0:T(2,128)S(1)}, f32[4,1,2,3,128]{4,2,3,1,0:T(2,128)S(1)}, u32[]{:S(2)}, u32[]{:S(2)}) collective-permute-start(f32[4,1,2,3,128]{4,2,3,1,0:T(2,128)S(1)} %get-tuple-element.287), channel_id=1, source_target_pairs={{0,2},{2,4},{4,6},{6,8},{8,10},{10,12},{12,14},{14,16},{16,18},{18... | collective-permute-start | bytes 36872 | tf_op jit(solution)/shard_map/ppermute | solution.py:28
  2.8 6.4 %collective-permute-start.1 = (f32[4,1,2,3,128]{4,2,3,1,0:T(2,128)S(1)}, f32[4,1,2,3,128]{4,2,3,1,0:T(2,128)S(1)}, u32[]{:S(2)}, u32[]{:S(2)}) collective-permute-start(f32[4,1,2,3,128]{4,2,3,1,0:T(2,128)S(1)} %get-tuple-element.288), channel_id=1, source_target_pairs={{2,0},{4,2},{6,4},{8,6},{10,8},{12,10},{14,12},{16,14},{18,16},{20... | collective-permute-start | bytes 36872 | tf_op jit(solution)/shard_map/ppermute | solution.py:29
  10.0 4.0 %collective-permute-start.2 = (f32[4,4,1,3,128]{4,2,3,1,0:T(1,128)S(1)}, f32[4,4,1,3,128]{4,2,3,1,0:T(1,128)S(1)}, u32[]{:S(2)}, u32[]{:S(2)}) collective-permute-start(f32[4,4,1,3,128]{4,2,3,1,0:T(1,128)S(1)} %get-tuple-element.285), channel_id=1, source_target_pairs={{0,1},{1,0},{2,3},{3,2},{4,5},{5,4},{6,7},{7,6},{8,9},{9,8},{10,11... | collective-permute-start | bytes 73736 | tf_op jit(solution)/shard_map/ppermute | solution.py:28
  12.0 3.8 %collective-permute-start.3 = (f32[4,4,1,3,128]{4,2,3,1,0:T(1,128)S(1)}, f32[4,4,1,3,128]{4,2,3,1,0:T(1,128)S(1)}, u32[]{:S(2)}, u32[]{:S(2)}) collective-permute-start(f32[4,4,1,3,128]{4,2,3,1,0:T(1,128)S(1)} %get-tuple-element.286), channel_id=1, source_target_pairs={{1,0},{0,1},{3,2},{2,3},{5,4},{4,5},{7,6},{6,7},{9,8},{8,9},{11,10... | collective-permute-start | bytes 73736 | tf_op jit(solution)/shard_map/ppermute | solution.py:29
  49.1 135.4 %collective-permute-start.4 = (f32[6,8,12]{1,0,2:T(8,128)S(1)}, f32[6,8,12]{1,0,2:T(8,128)S(1)}, u32[]{:S(2)}, u32[]{:S(2)}) collective-permute-start(f32[6,8,12]{1,0,2:T(8,128)S(1)} %get-tuple-element.283), channel_id=1, source_target_pairs={{0,2},{2,4},{4,6},{6,8},{8,10},{10,12},{12,14},{14,16},{16,18},{18... | collective-permute-start | bytes 6920 | tf_op jit(solution)/shard_map/ppermute | solution.py:28
  49.5 135.0 %collective-permute-start.5 = (f32[6,8,12]{1,0,2:T(8,128)S(1)}, f32[6,8,12]{1,0,2:T(8,128)S(1)}, u32[]{:S(2)}, u32[]{:S(2)}) collective-permute-start(f32[6,8,12]{1,0,2:T(8,128)S(1)} %get-tuple-element.284), channel_id=1, source_target_pairs={{2,0},{4,2},{6,4},{8,6},{10,8},{12,10},{14,12},{16,14},{18,16},{20... | collective-permute-start | bytes 6920 | tf_op jit(solution)/shard_map/ppermute | solution.py:29
  184.6 5.2 %collective-permute-start.6 = (f32[20,6,12]{1,0,2:T(8,128)S(1)}, f32[20,6,12]{1,0,2:T(8,128)S(1)}, u32[]{:S(2)}, u32[]{:S(2)}) collective-permute-start(f32[20,6,12]{1,0,2:T(8,128)S(1)} %get-tuple-element.239), channel_id=1, source_target_pairs={{0,1},{1,0},{2,3},{3,2},{4,5},{5,4},{6,7},{7,6},{8,9},{9,8},{10,11... | collective-permute-start | bytes 17288 | tf_op jit(solution)/shard_map/ppermute | solution.py:28
  185.2 6.2 %collective-permute-start.7 = (f32[20,6,12]{1,0,2:T(8,128)S(1)}, f32[20,6,12]{1,0,2:T(8,128)S(1)}, u32[]{:S(2)}, u32[]{:S(2)}) collective-permute-start(f32[20,6,12]{1,0,2:T(8,128)S(1)} %get-tuple-element.240), channel_id=1, source_target_pairs={{1,0},{0,1},{3,2},{2,3},{5,4},{4,5},{7,6},{6,7},{9,8},{8,9},{11,10... | collective-permute-start | bytes 17288 | tf_op jit(solution)/shard_map/ppermute | solution.py:29
where the time goes:
time: 198 us
  matrix products  103 us (52%)
  other arithmetic  35.6 us (18%)
  blocking collectives  24 us (12%)
  starting transfers between devices  14.2 us (7%)
  local copies, waits for them, and re-layouts  9.03 us (5%)
  waiting for transfers between devices  6.77 us (3%)
  loops' own time  5.06 us (3%)
    dot_general x27, matrix products, pair_force(): jnp.einsum('...ab,c...b->c...a', factor, stacked, precision=HIGHEST)  93.2 us
    reduce_sum x27, other arithmetic, pair_force(): square = jnp.sum(spread * spread, axis=0) + SOFT_SQUARE  22.2 us
    all_gather x1, blocking collectives, body(): whole = lax.all_gather(rows_sub, 'space', axis=0, tiled=True)  19.6 us
    ppermute x4, starting transfers between devices, extended_2(): after = lax.ppermute(first, axis, down)  10.7 us
    another operation x1, loops' own time, short_forces(): lax.fori_loop(0, 27, add_offset, jnp.zeros((3,) + packed.shape[1:], jnp.f...  5.06 us
    all_gather x1, blocking collectives, body(): rows_sub = lax.all_gather(coarse_charge, 'sub', axis=1, tiled=True)  4.35 us
  transfers between devices with their start and end apart: 8, of which 6 were waited for; matrix products, arithmetic and copies ran while one was open for 65% of the time, Pallas kernels for 0%

commit v1 on v0

v1 whole, which is shorter than its diff:
```python
import functools
import math

import jax
import jax.numpy as jnp
import numpy as np
from jax import lax
from jax.experimental import pallas as pl
from jax.experimental.pallas import tpu as pltpu
from jax.sharding import PartitionSpec as P

F32 = jnp.float32
BF16 = jnp.bfloat16
HIGHEST = lax.Precision.HIGHEST

POINTS = 4
REACH = 4
TAPS = POINTS + 3
SOFT_SQUARE = 0.0625
FINE_WIDTHS = (1.0, 2.0)
FINE_WEIGHTS = (2.0, 0.5)
COARSE_FRACTIONS = (8.0, 4.0)
COARSE_WEIGHTS = (4.0, 2.0)

DECAY = 0.114
SMOOTH = (
    0.004718840075751518,
    0.06055603768478568,
    0.019918877505712862,
    0.1440338177504446,
    0.014789349197372625,
    0.14113616660836056,
)
SCALE = math.sqrt(DECAY * math.log2(math.e))
LEAD = SMOOTH[-1] / SCALE**3
SHIFT = math.log2(LEAD) / (len(SMOOTH) - 1)
MONIC = tuple(
    coef / SCALE**3 / LEAD ** (power / (len(SMOOTH) - 1)) for power, coef in enumerate(SMOOTH)
)
HALF_CONST = 0.5 * (SHIFT - SCALE * SCALE * SOFT_SQUARE)

FEATURES = 32
SOURCES = 16
COLUMN_ROWS = FEATURES + SOURCES
PIECES = 26


def round_up(value, step):
    return -(-value // step) * step


def mul_t(left, right, precision=None):
    return lax.dot_general(
        left, right, (((1,), (1,)), ((), ())), precision=precision, preferred_element_type=F32
    )


def mul(left, right, precision=None):
    return lax.dot_general(
        left, right, (((1,), (0,)), ((), ())), precision=precision, preferred_element_type=F32
    )


def split(value, count):
    pieces = []
    for _ in range(count - 1):
        piece = value.astype(BF16).astype(F32)
        pieces.append(piece)
        value = value - piece
    pieces.append(value.astype(BF16).astype(F32))
    return pieces


class Brick:
    def __init__(self, shape, n_space, n_sub):
        self.bx, self.by, self.bz, self.atoms = shape
        self.n_space, self.n_sub = n_space, n_sub
        self.cols = self.bx * self.by
        self.lanes = self.bz * self.atoms
        self.wide = (self.bz + 2) * self.atoms
        self.px = POINTS * self.bx + 3
        self.py = round_up(POINTS * (self.by - 1) + 8, 8)
        self.pz = POINTS * self.bz
        self.zpad = round_up(self.pz, 16)
        self.group = 128 // self.zpad
        self.atom_rows = 4 * self.cols
        self.blocks = -(-self.px // self.group)
        self.msg_rows = round_up(self.atom_rows, 8) + self.py
        self.msg_lanes = max(self.lanes, self.blocks * 128)
        self.grid_row = round_up(self.atom_rows, 8)
        self.ci = 2 * self.bx + 2
        self.cj = 2 * self.by + 2
        self.ck = 2 * self.bz
        self.coarse_rows = round_up(self.ci, 8)
        self.coarse_lanes = round_up(self.cj * self.ck, 128)
        self.own_rows = round_up(self.cols, 8)
        self.outside = [
            (x, y)
            for x in range(-1, self.bx + 1)
            for y in range(-1, self.by + 1)
            if not (0 <= x < self.bx and 0 <= y < self.by)
        ]
        self.halo_rows = round_up(len(self.outside), 8)
        self.force_rows = round_up(3 * self.cols, 8)

    def col(self, x, y):
        return x * self.by + y


def spline(shifted):
    size = jnp.abs(shifted)
    outer = jnp.maximum(2.0 - size, 0.0)
    inner = jnp.maximum(1.0 - size, 0.0)
    return (outer * outer * outer) * (1.0 / 6.0) - (inner * inner * inner) * (4.0 / 6.0)


def spline_slope(shifted):
    size = jnp.abs(shifted)
    outer = jnp.maximum(2.0 - size, 0.0)
    inner = jnp.maximum(1.0 - size, 0.0)
    slope = 2.0 * (inner * inner) - 0.5 * (outer * outer)
    return jnp.where(shifted < 0.0, -slope, slope)


def shift_xy(brick, row):
    entry = lax.broadcasted_iota(jnp.int32, (8, brick.lanes), 0).astype(F32)
    return POINTS * row - (entry - 1.0)


def shift_z(brick, row):
    parts = []
    for cell in range(brick.bz):
        point = lax.broadcasted_iota(jnp.int32, (brick.zpad, brick.atoms), 0)
        entry = lax.rem(point - POINTS * cell + 1 + brick.pz, brick.pz) - 1
        entry = jnp.where(point < brick.pz, entry, 100)
        value = row[:, cell * brick.atoms : (cell + 1) * brick.atoms]
        parts.append(POINTS * value - entry.astype(F32))
    return jnp.concatenate(parts, axis=1)


def spread_kernel(brick, counts_ref, pos_ref, charge_ref, msg_ref, coarse_ref, grid_ref):
    atoms = brick.atoms
    lane = lax.broadcasted_iota(jnp.int32, (1, atoms), 1)
    for x in range(brick.bx):
        for y in range(brick.by):
            col = brick.col(x, y)
            for z in range(brick.bz):
                span = slice(z * atoms, (z + 1) * atoms)
                for comp in range(3):
                    row = comp * brick.cols + col
                    msg_ref[row : row + 1, span] = pos_ref[comp, x, y, z : z + 1, :]
                row = 3 * brick.cols + col
                charge = charge_ref[x, y, z : z + 1, :]
                msg_ref[row : row + 1, span] = jnp.where(lane < counts_ref[x, y, z], charge, 0.0)
    grid_ref[...] = jnp.zeros(grid_ref.shape, F32)
    for x in range(brick.bx):
        for y in range(brick.by):
            col = brick.col(x, y)
            rows = [
                msg_ref[k * brick.cols + col : k * brick.cols + col + 1, 0 : brick.lanes]
                for k in range(4)
            ]
            along_x = spline(shift_xy(brick, rows[0])) * rows[3]
            along_y = spline(shift_xy(brick, rows[1]))
            along_z = spline(shift_z(brick, rows[2]))
            outer = jnp.concatenate(
                [along_x[e : e + 1, :] * along_y for e in range(TAPS)], axis=0
            )
            box = mul_t(outer, along_z, HIGHEST)
            for e in range(TAPS):
                place = (POINTS * x + e, slice(POINTS * y, POINTS * y + 8), slice(0, brick.zpad))
                grid_ref[place] = grid_ref[place] + box[8 * e : 8 * e + 8, :]
    for block in range(brick.msg_lanes // 128):
        total = jnp.zeros((brick.py, 128), F32)
        for spot in range(brick.group):
            x = block * brick.group + spot
            if x < brick.px:
                plane = grid_ref[x]
                total = total + (pltpu.roll(plane, spot * brick.zpad, 1) if spot else plane)
        msg_ref[brick.grid_row :, block * 128 : (block + 1) * 128] = total
    planes = []
    for idx in range(brick.ci):
        inside = [x for x in (2 * idx - 1, 2 * idx) if 0 <= x < brick.px]
        planes.append(sum(grid_ref[x, :, 0 : brick.zpad] for x in inside))
    stacked = jnp.concatenate(planes, axis=0)
    shape = (brick.zpad, brick.coarse_lanes)
    z_idx = lax.broadcasted_iota(jnp.int32, shape, 0)
    z_lane = lax.broadcasted_iota(jnp.int32, shape, 1)
    used = z_lane < brick.cj * brick.ck
    pairs = (z_idx // 2 == z_lane % brick.ck) & used & (z_idx < brick.pz)
    folded = mul(stacked, jnp.where(pairs, 0.125, 0.0).astype(F32), HIGHEST)
    shape = (brick.py, brick.coarse_lanes)
    y_idx = lax.broadcasted_iota(jnp.int32, shape, 0)
    y_lane = lax.broadcasted_iota(jnp.int32, shape, 1)
    mask = (y_lane // brick.ck == (y_idx + 1) // 2).astype(F32)
    sums = [
        jnp.sum(folded[i * brick.py : (i + 1) * brick.py] * mask, axis=0, keepdims=True)
        for i in range(brick.ci)
    ]
    if brick.coarse_rows > brick.ci:
        sums.append(jnp.zeros((brick.coarse_rows - brick.ci, brick.coarse_lanes), F32))
    coarse_ref[...] = jnp.broadcast_to(jnp.concatenate(sums, axis=0)[None], coarse_ref.shape)


def other_rows(rows, columns):
    table = np.zeros((COLUMN_ROWS * len(columns), PIECES * rows), np.float32)
    for place, row in enumerate(columns):
        base = COLUMN_ROWS * place
        for comp in range(3):
            for slot, piece in enumerate((0, 1, 2, 0, 1, 0)):
                table[base + 6 * comp + slot, (3 * comp + piece) * rows + row] = 1.0
        for piece in range(3):
            table[base + 18 + piece, 12 * rows + row] = 1.0
            table[base + 21 + piece, (9 + piece) * rows + row] = 1.0
        for source in range(12):
            table[base + FEATURES + source, (13 + source) * rows + row] = 1.0
    return table


def own_rows(brick):
    rows = brick.own_rows
    table = np.zeros((brick.cols, 13 * rows, FEATURES), np.float32)
    for col in range(brick.cols):
        for comp in range(3):
            for slot, piece in enumerate((0, 0, 0, 1, 1, 2)):
                table[col, (3 * comp + piece) * rows + col, 6 * comp + slot] = 2.0
        for piece in range(3):
            table[col, (9 + piece) * rows + col, 18 + piece] = 1.0
            table[col, 12 * rows + col, 21 + piece] = 1.0
    return table


def stack_pieces(brick, rows, values, places, piece_ref, coord_ref=None):
    atoms = brick.atoms

    def extend(value):
        return jnp.concatenate([value[:, -atoms:], value, value[:, :atoms]], axis=1)

    index = lax.broadcasted_iota(jnp.int32, (rows, 1), 0)
    offset_x = jnp.zeros((rows, 1), F32)
    offset_y = jnp.zeros((rows, 1), F32)
    for row, (x, y) in enumerate(places):
        offset_x = jnp.where(index == row, x - 0.5 * brick.bx, offset_x)
        offset_y = jnp.where(index == row, y - 0.5 * brick.by, offset_y)
    along_z = [values[2][:, z * atoms : (z + 1) * atoms] for z in range(brick.bz)]
    along_z = [along_z[-1]] + along_z + [along_z[0]]
    along_z = [value + (z - 1 - 0.5 * brick.bz) for z, value in enumerate(along_z)]
    coords = [
        extend((values[0] + offset_x) * SCALE),
        extend((values[1] + offset_y) * SCALE),
        jnp.concatenate(along_z, axis=1) * SCALE,
    ]
    charge = extend(values[3])
    square = HALF_CONST - (
        coords[0] * coords[0] + coords[1] * coords[1] + coords[2] * coords[2]
    )
    pieces = []
    for value in coords + [square]:
        pieces += split(value, 3)
    pieces.append(jnp.ones((rows, brick.wide), F32))
    for value in [charge] + [charge * coord for coord in coords]:
        pieces += split(value, 3)
    pieces.append(jnp.zeros((rows, brick.wide), F32))
    for number, piece in enumerate(pieces):
        piece_ref[number * rows : (number + 1) * rows, :] = piece
    if coord_ref is not None:
        for comp in range(3):
            coord_ref[comp * rows : (comp + 1) * rows, :] = coords[comp]


def load_own(brick, msg_ref, piece_ref, coord_ref):
    pad = brick.own_rows - brick.cols
    values = []
    for k in range(4):
        value = msg_ref[k * brick.cols : (k + 1) * brick.cols, 0 : brick.lanes]
        if pad:
            value = jnp.concatenate([value, jnp.zeros((pad, brick.lanes), F32)], axis=0)
        values.append(value)
    places = [(x, y) for x in range(brick.bx) for y in range(brick.by)]
    stack_pieces(brick, brick.own_rows, values, places, piece_ref, coord_ref)


def load_left(brick, piece_ref, own_table_ref, left_ref):
    span = slice(brick.atoms, brick.atoms + brick.lanes)
    rows = 13 * brick.own_rows
    full = round_up(rows, 128)
    turned = piece_ref[0:full, span].T[:, 0:rows].astype(BF16)
    for col in range(brick.cols):
        left_ref[col] = mul(turned, own_table_ref[col]).astype(BF16)


def pair_factor(left, right):
    power = mul(left, right)
    inverse = lax.rsqrt(SHIFT - power)
    base = jnp.exp2(power)
    smooth = base + MONIC[4]
    for coef in MONIC[3::-1]:
        smooth = smooth * base + coef
    factor = inverse * (inverse * inverse) - smooth
    high = factor.astype(BF16)
    low = (factor - high.astype(F32)).astype(BF16)
    return high, low


def sources(other_ref, place, span):
    base = COLUMN_ROWS * place
    return other_ref[base + FEATURES : base + COLUMN_ROWS, span]


def features(other_ref, place, span):
    base = COLUMN_ROWS * place
    return other_ref[base : base + FEATURES, span]


def moments(total, quantity):
    base = 3 * quantity
    return total[base : base + 1] + total[base + 1 : base + 2] + total[base + 2 : base + 3]


def inner_kernel(
    brick,
    msg_ref,
    own_table_ref,
    other_table_ref,
    force_ref,
    piece_ref,
    coord_ref,
    left_ref,
    other_ref,
    total_ref,
):
    atoms = brick.atoms
    load_own(brick, msg_ref, piece_ref, coord_ref)
    load_left(brick, piece_ref, own_table_ref, left_ref)
    other_ref[...] = mul(other_table_ref[...], piece_ref[...].astype(BF16)).astype(BF16)
    total_ref[...] = jnp.zeros(total_ref.shape, F32)
    force_ref[...] = jnp.zeros(force_ref.shape, F32)

    def block(col, other, z, span, first_back):
        own_span = slice((z + 1) * atoms, (z + 2) * atoms)
        left = left_ref[col, z * atoms : (z + 1) * atoms, :]
        high, low = pair_factor(left, features(other_ref, other, span))
        source = sources(other_ref, other, span)
        total_ref[col, :, own_span] += mul_t(source, high) + mul_t(source, low)
        back = sources(other_ref, col, own_span)
        back_span = slice(span.start + first_back, span.stop)
        total_ref[other, :, back_span] += mul(back, high[:, first_back:]) + mul(
            back, low[:, first_back:]
        )

    cells = [(x, y) for x in range(brick.bx) for y in range(brick.by)]
    for first, (x, y) in enumerate(cells):
        for second in range(first + 1, len(cells)):
            if max(abs(x - cells[second][0]), abs(y - cells[second][1])) > 1:
                continue
            for z in range(brick.bz):
                block(first, second, z, slice(z * atoms, (z + 3) * atoms), 0)
    for col in range(brick.cols):
        for z in range(brick.bz):
            block(col, col, z, slice((z + 1) * atoms, (z + 3) * atoms), atoms)

    for col in range(brick.cols):
        total = total_ref[col]
        charge = msg_ref[3 * brick.cols + col : 3 * brick.cols + col + 1, 0 : brick.lanes]
        weight = moments(total, 0)
        for comp in range(3):
            row = comp * brick.own_rows + col
            wide = coord_ref[row : row + 1, :] * weight - moments(total, 1 + comp)
            parts = [wide[:, (z + 1) * atoms : (z + 2) * atoms] for z in range(brick.bz)]
            parts[-1] = parts[-1] + wide[:, :atoms]
            parts[0] = parts[0] + wide[:, -atoms:]
            row = comp * brick.cols + col
            force_ref[row : row + 1, :] = (
                jnp.concatenate(parts, axis=1) * charge * (SCALE * SCALE)
            )


def halo_kernel(brick, sender, n_msgs, *refs):
    atoms = brick.atoms
    msg_ref = refs[0]
    other_msgs = refs[1 : 1 + n_msgs]
    own_table_ref, other_table_ref, part_ref, force_ref = refs[1 + n_msgs : 5 + n_msgs]
    piece_ref, coord_ref, left_ref, row_ref, halo_ref, other_ref = refs[5 + n_msgs :]
    load_own(brick, msg_ref, piece_ref, coord_ref)
    load_left(brick, piece_ref, own_table_ref, left_ref)
    rows = brick.halo_rows
    row_ref[...] = jnp.zeros(row_ref.shape, F32)
    for place, (x, y) in enumerate(brick.outside):
        near = other_msgs[sender[(x // brick.bx, y // brick.by)]]
        col = brick.col(x % brick.bx, y % brick.by)
        for k in range(4):
            row_ref[k * rows + place : k * rows + place + 1, :] = near[
                k * brick.cols + col : k * brick.cols + col + 1, 0 : brick.lanes
            ]
    values = [row_ref[k * rows : (k + 1) * rows, :] for k in range(4)]
    stack_pieces(brick, rows, values, brick.outside, halo_ref)
    other_ref[...] = mul(other_table_ref[...], halo_ref[...].astype(BF16)).astype(BF16)
    force_ref[...] = part_ref[...]
    for x in range(brick.bx):
        for y in range(brick.by):
            col = brick.col(x, y)
            near = [
                place
                for place, (ox, oy) in enumerate(brick.outside)
                if max(abs(ox - x), abs(oy - y)) <= 1
            ]
            for z in range(brick.bz):
                span = slice(z * atoms, (z + 3) * atoms)
                own_span = slice(z * atoms, (z + 1) * atoms)
                left = left_ref[col, own_span, :]
                total = jnp.zeros((SOURCES, atoms), F32)
                for place in near:
                    high, low = pair_factor(left, features(other_ref, place, span))
                    source = sources(other_ref, place, span)
                    total = total + (mul_t(source, high) + mul_t(source, low))
                charge = msg_ref[3 * brick.cols + col : 3 * brick.cols + col + 1, own_span]
                weight = moments(total, 0)
                for comp in range(3):
                    row = comp * brick.own_rows + col
                    coord = coord_ref[row : row + 1, (z + 1) * atoms : (z + 2) * atoms]
                    value = (coord * weight - moments(total, 1 + comp)) * charge
                    row = comp * brick.cols + col
                    force_ref[row : row + 1, own_span] += value * (SCALE * SCALE)


def fine_tables(brick):
    ext_x = brick.px + 2 * REACH
    rows_y = brick.py + POINTS * brick.by
    along_z = np.zeros((128, 128 * len(FINE_WIDTHS)), np.float32)
    along_xy = np.zeros((brick.px * brick.py, len(FINE_WIDTHS) * ext_x * rows_y), np.float32)

    def tap(dist, width):
        return np.where(np.abs(dist) <= REACH, np.exp(-(dist * dist) / (2.0 * width * width)), 0.0)

    for number, (width, weight) in enumerate(zip(FINE_WIDTHS, FINE_WEIGHTS)):
        for step in range(-REACH, REACH + 1):
            for z in range(brick.pz):
                along_z[(z + step) % brick.pz, 128 * number + z] += weight * tap(
                    np.float64(step), width
                )
        out_x = np.arange(brick.px) - 1.0
        in_x = np.arange(ext_x) - 1.0 - REACH
        out_y = np.arange(brick.py) - 1.0
        in_y = np.arange(rows_y) - 1.0 - POINTS * brick.by
        mat_x = tap(out_x[:, None] - in_x[None, :], width)
        mat_y = tap(out_y[:, None] - in_y[None, :], width)
        mat_y[POINTS * brick.by + 3 :] = 0.0
        size = ext_x * rows_y
        along_xy[:, number * size : (number + 1) * size] = np.kron(mat_x, mat_y)
    return along_xy, along_z


def coarse_table(brick):
    table = np.zeros((len(COARSE_WEIGHTS) * brick.coarse_lanes, 128), np.float32)
    length = brick.ck
    for number, (fraction, weight) in enumerate(zip(COARSE_FRACTIONS, COARSE_WEIGHTS)):
        width = length / fraction
        for row in range(brick.cj * brick.ck):
            for z in range(brick.pz):
                dist = (row - z // 2) % length
                dist = min(dist, length - dist)
                table[number * brick.coarse_lanes + row, z] = weight * math.exp(
                    -(dist * dist) / (2.0 * width * width)
                )
    return table


def gauss(row, col, length, fraction):
    dist = lax.rem(row - col + 2 * length, length)
    dist = jnp.minimum(dist, length - dist).astype(F32)
    width = length / fraction
    return jnp.exp(dist * dist * (-1.0 / (2.0 * width * width)))


def potential_kernel(brick, sender, n_msgs, *refs):
    atoms = brick.atoms
    place_ref, msg_ref = refs[0:2]
    other_msgs = refs[2 : 2 + n_msgs]
    (
        whole_ref,
        short_ref,
        xy_high_ref,
        xy_low_ref,
        z_ref,
        coarse_z_ref,
        out_ref,
        ext_ref,
        pot_ref,
    ) = refs[2 + n_msgs :]
    step_y = POINTS * brick.by
    rows_y = brick.py + step_y
    ext_x = brick.px + 2 * REACH
    planes = {}
    for dx in (-1, 0, 1):
        grids = []
        for dy in (-1, 0, 1):
            source = msg_ref if (dx, dy) == (0, 0) else other_msgs[sender[(dx, dy)]]
            grids.append(source[brick.grid_row :, 0 : brick.blocks * 128])
        full = brick.py + 2 * step_y
        tiles = [None] * (full // 8)
        for number, grid in enumerate(grids):
            for tile in range(brick.py // 8):
                spot = tile + number * step_y // 8
                value = grid[8 * tile : 8 * tile + 8]
                tiles[spot] = value if tiles[spot] is None else tiles[spot] + value
        column = jnp.concatenate(tiles[: rows_y // 8], axis=0)
        for x in range(brick.px):
            spot = x + POINTS * brick.bx * dx + REACH
            if 0 <= spot < ext_x:
                block, shift = divmod(x, brick.group)
                value = column[:, block * 128 : (block + 1) * 128]
                if shift:
                    value = pltpu.roll(value, 128 - shift * brick.zpad, 1)
                planes[spot] = planes[spot] + value if spot in planes else value
    for spot in range(ext_x):
        ext_ref[spot * rows_y : (spot + 1) * rows_y, :] = planes[spot]
    along = mul(ext_ref[...], z_ref[...], HIGHEST)
    along = jnp.concatenate([along[:, :128], along[:, 128:]], axis=0)
    high = along.astype(BF16)
    low = (along - high.astype(F32)).astype(BF16)
    potential = mul(xy_high_ref[...], high) + (
        mul(xy_high_ref[...], low) + mul(xy_low_ref[...], high)
    )

    total_x = 2 * brick.bx * brick.n_space
    total_y = 2 * brick.by * brick.n_sub
    first_x = place_ref[0] * (2 * brick.bx)
    first_y = place_ref[1] * (2 * brick.by)
    out_rows = round_up(brick.px, 8)
    shape = (out_rows, brick.n_space * brick.coarse_rows)
    point = lax.broadcasted_iota(jnp.int32, shape, 0)
    lane = lax.broadcasted_iota(jnp.int32, shape, 1)
    row_x = first_x + (point + 1) // 2 - 1
    col_x = lane // brick.coarse_rows * (2 * brick.bx) + lane % brick.coarse_rows - 1
    live = lane % brick.coarse_rows < brick.ci
    mats_x = jnp.concatenate(
        [
            jnp.where(live, gauss(row_x, col_x, total_x, fraction), 0.0)
            for fraction in COARSE_FRACTIONS
        ],
        axis=0,
    )
    shape = (brick.py, brick.coarse_lanes)
    point = lax.broadcasted_iota(jnp.int32, shape, 0)
    lane = lax.broadcasted_iota(jnp.int32, shape, 1)
    row_y = first_y + (point + 1) // 2 - 1
    live = lane < brick.cj * brick.ck
    lefts = [[None] * brick.px for _ in COARSE_FRACTIONS]
    for sub in range(brick.n_sub):
        part = whole_ref[:, sub].reshape(
            brick.n_space * brick.coarse_rows, brick.coarse_lanes
        )
        mixed = mul(mats_x, part, HIGHEST)
        col_y = sub * (2 * brick.by) + lane // brick.ck - 1
        for number, fraction in enumerate(COARSE_FRACTIONS):
            mat_y = jnp.where(live, gauss(row_y, col_y, total_y, fraction), 0.0)
            for x in range(brick.px):
                row = number * out_rows + x
                value = mixed[row : row + 1] * mat_y
                done = lefts[number][x]
                lefts[number][x] = value if done is None else done + value
    left = jnp.concatenate([jnp.concatenate(rows, axis=0) for rows in lefts], axis=1)
    potential = potential + mul(left, coarse_z_ref[...], HIGHEST)
    for x in range(brick.px):
        pot_ref[x] = potential[x * brick.py : (x + 1) * brick.py]

    for x in range(brick.bx):
        for y in range(brick.by):
            col = brick.col(x, y)
            rows = [
                msg_ref[k * brick.cols + col : k * brick.cols + col + 1, 0 : brick.lanes]
                for k in range(4)
            ]
            shifted = [
                shift_xy(brick, rows[0]),
                shift_xy(brick, rows[1]),
                shift_z(brick, rows[2]),
            ]
            weights = [spline(value) for value in shifted]
            slopes = [spline_slope(value) for value in shifted]
            box = jnp.concatenate(
                [
                    pot_ref[POINTS * x + e, POINTS * y : POINTS * y + 8, 0 : brick.zpad]
                    for e in range(TAPS)
                ],
                axis=0,
            )
            both = mul(box, jnp.concatenate([weights[2], slopes[2]], axis=1), HIGHEST)
            along_z = both[:, : brick.lanes]
            sloped_z = both[:, brick.lanes :]
            sums = [0.0, 0.0, 0.0]
            for e in range(TAPS):
                weight = weights[0][e : e + 1]
                slope = slopes[0][e : e + 1]
                flat = along_z[8 * e : 8 * e + 8]
                steep = sloped_z[8 * e : 8 * e + 8]
                sums[0] = sums[0] + flat * slope
                sums[1] = sums[1] + flat * weight
                sums[2] = sums[2] + steep * weight
            across = (weights[1], slopes[1], weights[1])
            for comp in range(3):
                force = jnp.sum(sums[comp] * across[comp], axis=0, keepdims=True)
                row = comp * brick.cols + col
                force = short_ref[row : row + 1, :] - POINTS * (rows[3] * force)
                for z in range(brick.bz):
                    out_ref[comp, x, y, z : z + 1, :] = force[:, z * atoms : (z + 1) * atoms]


VMEM = pl.BlockSpec(memory_space=pltpu.VMEM)
SMEM = pl.BlockSpec(memory_space=pltpu.SMEM)


def call(kernel, out_shape, in_specs, scratch, flops, *args):
    single = not isinstance(out_shape, (list, tuple))
    return pl.pallas_call(
        kernel,
        out_shape=out_shape,
        in_specs=in_specs,
        out_specs=VMEM if single else [VMEM] * len(out_shape),
        scratch_shapes=scratch,
        compiler_params=pltpu.CompilerParams(vmem_limit_bytes=40 * 1024 * 1024),
        cost_estimate=pl.CostEstimate(flops=flops, bytes_accessed=10**5, transcendentals=0),
    )(*args)


def neighbours(brick, msg):
    found = {}
    sender = {}
    msgs = []
    for dx in (-1, 0, 1):
        for dy in (-1, 0, 1):
            if (dx, dy) == (0, 0):
                continue
            key = (dx % brick.n_space, dy % brick.n_sub)
            if key not in found:
                found[key] = len(msgs)
                pairs = []
                for i in range(brick.n_space):
                    for j in range(brick.n_sub):
                        source = (i + dx) % brick.n_space * brick.n_sub + (j + dy) % brick.n_sub
                        pairs.append((source, i * brick.n_sub + j))
                msgs.append(lax.ppermute(msg, ("space", "sub"), pairs))
            sender[(dx, dy)] = found[key]
    return sender, msgs


def body(n_space, n_sub, positions, charges, counts):
    brick = Brick(charges.shape, n_space, n_sub)
    n_dev = n_space * n_sub
    own_table = jnp.asarray(own_rows(brick), BF16)
    inner_table = jnp.asarray(other_rows(brick.own_rows, range(brick.cols)), BF16)
    outer_table = jnp.asarray(other_rows(brick.halo_rows, range(len(brick.outside))), BF16)
    along_xy, along_z = fine_tables(brick)
    xy_high = along_xy.astype(BF16)
    xy_low = (along_xy - xy_high.astype(np.float32)).astype(BF16)
    coarse_z = coarse_table(brick)
    place = jnp.stack([lax.axis_index("space"), lax.axis_index("sub")]).astype(jnp.int32)

    msg, coarse = call(
        functools.partial(spread_kernel, brick),
        [
            jax.ShapeDtypeStruct((brick.msg_rows, brick.msg_lanes), F32),
            jax.ShapeDtypeStruct((n_dev, brick.coarse_rows, brick.coarse_lanes), F32),
        ],
        [SMEM, VMEM, VMEM],
        [pltpu.VMEM((brick.px, brick.py, 128), F32)],
        10**7,
        counts,
        positions,
        charges,
    )
    sender, msgs = neighbours(brick, msg)
    whole = lax.all_to_all(coarse, ("space", "sub"), 0, 0, tiled=True)
    whole = whole.reshape(n_space, n_sub, brick.coarse_rows, brick.coarse_lanes)

    own_scratch = [
        pltpu.VMEM((PIECES * brick.own_rows, brick.wide), F32),
        pltpu.VMEM((3 * brick.own_rows, brick.wide), F32),
        pltpu.VMEM((brick.cols, brick.lanes, FEATURES), BF16),
    ]
    force_shape = jax.ShapeDtypeStruct((brick.force_rows, brick.lanes), F32)
    part = call(
        functools.partial(inner_kernel, brick),
        force_shape,
        [VMEM] * 3,
        own_scratch
        + [
            pltpu.VMEM((COLUMN_ROWS * brick.cols, brick.wide), BF16),
            pltpu.VMEM((brick.cols, SOURCES, brick.wide), F32),
        ],
        10**10,
        msg,
        own_table,
        inner_table,
    )
    n_out = len(brick.outside)
    short = call(
        functools.partial(halo_kernel, brick, sender, len(msgs)),
        force_shape,
        [VMEM] * (4 + len(msgs)),
        own_scratch
        + [
            pltpu.VMEM((4 * brick.halo_rows, brick.lanes), F32),
            pltpu.VMEM((PIECES * brick.halo_rows, brick.wide), F32),
            pltpu.VMEM((COLUMN_ROWS * n_out, brick.wide), BF16),
        ],
        10**10,
        msg,
        *msgs,
        own_table,
        outer_table,
        part,
    )
    ext_x = brick.px + 2 * REACH
    rows_y = brick.py + POINTS * brick.by
    return call(
        functools.partial(potential_kernel, brick, sender, len(msgs)),
        jax.ShapeDtypeStruct(positions.shape, F32),
        [SMEM] + [VMEM] * (7 + len(msgs)),
        [
            pltpu.VMEM((ext_x * rows_y, 128), F32),
            pltpu.VMEM((brick.px, brick.py, 128), F32),
        ],
        10**8,
        place,
        msg,
        *msgs,
        whole,
        short,
        xy_high,
        xy_low,
        jnp.asarray(along_z),
        jnp.asarray(coarse_z),
    )


def solution(mesh):
    in_specs = (
        P(None, "space", "sub", None, None),
        P("space", "sub", None, None),
        P("space", "sub", None),
    )
    out_specs = P(None, "space", "sub", None, None)
    run = functools.partial(body, mesh.shape["space"], mesh.shape["sub"])
    return jax.shard_map(run, mesh=mesh, in_specs=in_specs, out_specs=out_specs, check_vma=False)
```

time: 198 us -> 39.6 us (0.20)
  matrix products: 103 us -> 0 us
  other arithmetic: 35.6 us -> 0.08 us
  blocking collectives: 24 us -> 0 us
  Pallas kernels: 0 us -> 23.1 us
  local copies, waits for them, and re-layouts: 9.03 us -> 2.08 us
  waiting for transfers between devices: 6.77 us -> 0.02 us
  loops' own time: 5.06 us -> 0 us
    dot_general x48 -> x0, matrix products: 103 us -> none  [the longest x27 93.2 us: pair_force(): jnp.einsum('...ab,c...b->c...a', factor, stacked, precision=HIGHEST)]
    all_gather x2 -> x0, blocking collectives: 24 us -> none  [the longest x1 19.6 us: body(): whole = lax.all_gather(rows_sub, 'space', axis=0, tiled=True)]
    pallas_call x0 -> x4, Pallas kernels: none -> 23.1 us  [call(): pl.pallas_call(kernel, out_shape=out_shape, in_specs=in_specs, out_specs=...]
    reduce_sum x28 -> x0, other arithmetic: 22.3 us -> none  [the longest x27 22.2 us: pair_force(): square = jnp.sum(spread * spread, axis=0) + SOFT_SQUARE]
    ppermute x8 -> x5, waiting for transfers between devices: 6.77 us -> 0.01 us  [neighbours(): msgs.append(lax.ppermute(msg, ('space', 'sub'), pairs))]
    ppermute x8 -> x5, starting transfers between devices: 14.2 us -> 8.4 us  [neighbours(): msgs.append(lax.ppermute(msg, ('space', 'sub'), pairs))]
    all_to_all x0 -> x1, starting transfers between devices: none -> 5.48 us  [body(): whole = lax.all_to_all(coarse, ('space', 'sub'), 0, 0, tiled=True)]
    another operation x1 -> x0, loops' own time: 5.06 us -> none  [short_forces(): lax.fori_loop(0, 27, add_offset, jnp.zeros((3,) + packed.shape[1:], jnp.f...]
  transfers between devices with their start and end apart: 8 -> 6, of which waited for: 6 -> 0; matrix products, arithmetic and copies ran while one was open for 65% -> 0% of each run, Pallas kernels for 0% -> 45%
where the time goes in v1:
time: 39.6 us; the launch traced here: 39.3 us
  Pallas kernels  23.1 us (58%)
  starting transfers between devices  13.9 us (35%)
  local copies, waits for them, and re-layouts  2.08 us (5%)
    pallas_call x4, Pallas kernels, call(): pl.pallas_call(kernel, out_shape=out_shape, in_specs=in_specs, out_specs=...  23.1 us
    ppermute x5, starting transfers between devices, neighbours(): msgs.append(lax.ppermute(msg, ('space', 'sub'), pairs))  8.4 us
    all_to_all x1, starting transfers between devices, body(): whole = lax.all_to_all(coarse, ('space', 'sub'), 0, 0, tiled=True)  5.48 us
    unnamed x18, local copies, waits for them, and re-layouts  1.47 us
  transfers between devices with their start and end apart: 6, of which 0 were waited for; matrix products, arithmetic and copies ran while one was open for 0% of the time, Pallas kernels for 45%

profile of v1, /device:TPU:0, one launch (start us, length us, event | category | flops | bytes accessed | tf_op | source)
XLA Modules:
  0.0 39.3 jit_solution(10910994631226476952)
XLA Ops:
  0.0 0.7 %copy.12.charge_ref = f32[2,2,3,128]{3,2,1,0:T(4,128)S(1)} copy(f32[2,2,3,128]{3,1,2,0:T(2,128)} %param.11) | data formatting | bytes 12288 | tf_op args[1]
  0.7 0.0 copy-start.4
  0.7 0.7 %copy.11.pos_ref = f32[3,2,2,3,128]{4,3,2,1,0:T(4,128)S(1)} copy(f32[3,2,2,3,128]{4,2,3,1,0:T(2,128)} %param.10) | data formatting | bytes 36864 | tf_op args[0]
  1.4 0.0 copy-done.4
  1.4 2.0 %shard_map.100 = (f32[32,384]{1,0:T(8,128)S(1)}, f32[32,8,128]{2,1,0:T(8,128)}) custom-call(s32[2,2,3]{2,1,0:T(2,128)S(1)} %copy-done.4, f32[3,2,2,3,128]{4,3,2,1,0:T(4,128)S(1)} %copy.11.pos_ref, f32[2,2,3,128]{3,2,1,0:T(4,128)S(1)} %copy.12.charge_ref), custom_call_target="tpu_custom_call" | custom-call | flops 10000000 | bytes 100000 | tf_op jit(solution)/shard_map/pallas_call | solution.py:615
  3.5 5.4 %collective-permute-start.4 = (f32[32,384]{1,0:T(8,128)S(1)}, f32[32,384]{1,0:T(8,128)S(1)}, u32[]{:S(2)}, u32[]{:S(2)}) collective-permute-start(f32[32,384]{1,0:T(8,128)S(1)} %get-tuple-element.7.msg_ref.refs_0_.refs_1_), channel_id=1, source_target_pairs={{2,0},{3,1},{4,2},{5,3},{6,4},{7,5},{8,6},{9,7},{10,8},{11,9},{12,... | collective-permute-start | bytes 147464 | tf_op jit(solution)/shard_map/ppermute | solution.py:642
  8.9 1.6 %collective-permute-start.3 = (f32[32,384]{1,0:T(8,128)S(1)}, f32[32,384]{1,0:T(8,128)S(1)}, u32[]{:S(2)}, u32[]{:S(2)}) collective-permute-start(f32[32,384]{1,0:T(8,128)S(1)} %get-tuple-element.7.msg_ref.refs_0_.refs_1_), channel_id=1, source_target_pairs={{3,0},{2,1},{5,2},{4,3},{7,4},{6,5},{9,6},{8,7},{11,8},{10,9},{13,... | collective-permute-start | bytes 147464 | tf_op jit(solution)/shard_map/ppermute | solution.py:642
  10.5 0.5 %collective-permute-start.2 = (f32[32,384]{1,0:T(8,128)S(1)}, f32[32,384]{1,0:T(8,128)S(1)}, u32[]{:S(2)}, u32[]{:S(2)}) collective-permute-start(f32[32,384]{1,0:T(8,128)S(1)} %get-tuple-element.7.msg_ref.refs_0_.refs_1_), channel_id=1, source_target_pairs={{1,0},{0,1},{3,2},{2,3},{5,4},{4,5},{7,6},{6,7},{9,8},{8,9},{11,10... | collective-permute-start | bytes 147464 | tf_op jit(solution)/shard_map/ppermute | solution.py:642
  11.0 0.0 collective-permute-start.1
  11.0 0.8 %collective-permute-start = (f32[32,384]{1,0:T(8,128)S(1)}, f32[32,384]{1,0:T(8,128)S(1)}, u32[]{:S(2)}, u32[]{:S(2)}) collective-permute-start(f32[32,384]{1,0:T(8,128)S(1)} %get-tuple-element.7.msg_ref.refs_0_.refs_1_), channel_id=1, source_target_pairs={{31,0},{30,1},{1,2},{0,3},{3,4},{2,5},{5,6},{4,7},{7,8},{6,9},{9,1... | collective-permute-start | bytes 147464 | tf_op jit(solution)/shard_map/ppermute | solution.py:642
  11.9 0.0 copy-start.6
  11.9 0.0 copy-start.7
  11.9 5.5 %all-to-all-start = ((f32[32,8,128]{2,1,0:T(8,128)}), f32[32,8,128]{2,1,0:T(8,128)S(1)}, u32[]{:S(2)}, u32[]{:S(2)}) async-start(f32[32,8,128]{2,1,0:T(8,128)} %get-tuple-element.8), calls=%async_computation | async-start | bytes 262144 | tf_op jit(solution)/shard_map/all_to_all | solution.py:673
  17.4 0.0 copy-done.6
  17.4 0.0 copy-done.7
  17.4 0.0 copy-start.5
  17.4 7.9 %shard_map.101.refs_8_ = f32[16,384]{1,0:T(8,128)S(1)} custom-call(f32[32,384]{1,0:T(8,128)S(1)} %get-tuple-element.7.msg_ref.refs_0_.refs_1_, bf16[4,104,32]{2,1,0:T(8,128)(2,1)S(1)} %copy-done.6, bf16[192,208]{1,0:T(8,128)(2,1)S(1)} %copy-done.7), custom_call_target="tpu_custom_call" | custom-call | flops 10000000000 | bytes 100000 | tf_op jit(solution)/shard_map/pallas_call | solution.py:615
  25.3 0.1 pad_add_fusion.refs_0_
  25.4 0.0 copy-start
  25.4 0.0 copy-start.1
  25.4 0.0 copy-start.2
  25.4 0.0 copy-start.3
  25.4 0.0 collective-permute-done.4.refs_5_.refs_6_
  25.4 0.0 collective-permute-done.3.refs_4_.refs_5_
  25.4 0.0 collective-permute-done.2.refs_3_.refs_4_
  25.4 0.0 collective-permute-done.1.refs_2_.refs_3_
  25.4 0.0 collective-permute-done.refs_1_.refs_2_
  25.4 0.0 copy-done.5
  25.5 9.8 %shard_map.102.refs_8_ = f32[16,384]{1,0:T(8,128)S(1)} custom-call(f32[32,384]{1,0:T(8,128)S(1)} %get-tuple-element.7.msg_ref.refs_0_.refs_1_, f32[32,384]{1,0:T(8,128)S(1)} %collective-permute-done.refs_1_.refs_2_, f32[32,384]{1,0:T(8,128)S(1)} %collective-permute-done.1.refs_2_.refs_3_, f32[32,384]{1,0:T(8,128)S(1)} %collective-permute-done.2.refs_3_.refs_4_, ...), custom_call_target="tpu_custom_call" | custom-call | flops 10000000000 | bytes 100000 | tf_op jit(solution)/shard_map/pallas_call | solution.py:615
  35.3 0.0 all-to-all-done
  35.3 0.0 copy-done
  35.3 0.0 copy-done.1
  35.3 0.0 copy-done.2
  35.3 0.0 copy-done.3
  35.3 3.4 %shard_map.103 = f32[3,2,2,3,128]{4,3,2,1,0:T(4,128)S(1)} custom-call(s32[2]{0:T(128)S(1)} %pad_add_fusion.refs_0_, f32[32,384]{1,0:T(8,128)S(1)} %get-tuple-element.7.msg_ref.refs_0_.refs_1_, f32[32,384]{1,0:T(8,128)S(1)} %collective-permute-done.refs_1_.refs_2_, f32[32,384]{1,0:T(8,128)S(1)} %collective-permute-done.1.refs_2_.refs_3_, ...), custom_call_target="tpu_custom_call" | custom-call | flops 100000000 | bytes 100000 | tf_op jit(solution)/shard_map/pallas_call | solution.py:615
  38.7 0.6 %copy.13 = f32[3,2,2,3,128]{4,2,3,1,0:T(2,128)} copy(f32[3,2,2,3,128]{4,3,2,1,0:T(4,128)S(1)} %shard_map.103) | data formatting | bytes 36864 | tf_op jit(solution)/shard_map/pallas_call | solution.py:615
Async XLA Ops:
  0.7 0.7 %copy-start.4 = (s32[2,2,3]{2,1,0:T(2,128)S(1)}, s32[2,2,3]{2,1,0:T(2,128)}, u32[]{:S(2)}) copy-start(s32[2,2,3]{2,1,0:T(2,128)} %counts_ref.1) | copy-start | bytes 148
  3.5 21.9 %collective-permute-start.4 = (f32[32,384]{1,0:T(8,128)S(1)}, f32[32,384]{1,0:T(8,128)S(1)}, u32[]{:S(2)}, u32[]{:S(2)}) collective-permute-start(f32[32,384]{1,0:T(8,128)S(1)} %get-tuple-element.7.msg_ref.refs_0_.refs_1_), channel_id=1, source_target_pairs={{2,0},{3,1},{4,2},{5,3},{6,4},{7,5},{8,6},{9,7},{10,8},{11,9},{12,... | collective-permute-start | bytes 147464 | tf_op jit(solution)/shard_map/ppermute | solution.py:642
  8.9 16.5 %collective-permute-start.3 = (f32[32,384]{1,0:T(8,128)S(1)}, f32[32,384]{1,0:T(8,128)S(1)}, u32[]{:S(2)}, u32[]{:S(2)}) collective-permute-start(f32[32,384]{1,0:T(8,128)S(1)} %get-tuple-element.7.msg_ref.refs_0_.refs_1_), channel_id=1, source_target_pairs={{3,0},{2,1},{5,2},{4,3},{7,4},{6,5},{9,6},{8,7},{11,8},{10,9},{13,... | collective-permute-start | bytes 147464 | tf_op jit(solution)/shard_map/ppermute | solution.py:642
  10.5 14.9 %collective-permute-start.2 = (f32[32,384]{1,0:T(8,128)S(1)}, f32[32,384]{1,0:T(8,128)S(1)}, u32[]{:S(2)}, u32[]{:S(2)}) collective-permute-start(f32[32,384]{1,0:T(8,128)S(1)} %get-tuple-element.7.msg_ref.refs_0_.refs_1_), channel_id=1, source_target_pairs={{1,0},{0,1},{3,2},{2,3},{5,4},{4,5},{7,6},{6,7},{9,8},{8,9},{11,10... | collective-permute-start | bytes 147464 | tf_op jit(solution)/shard_map/ppermute | solution.py:642
  11.0 14.4 %collective-permute-start.1 = (f32[32,384]{1,0:T(8,128)S(1)}, f32[32,384]{1,0:T(8,128)S(1)}, u32[]{:S(2)}, u32[]{:S(2)}) collective-permute-start(f32[32,384]{1,0:T(8,128)S(1)} %get-tuple-element.7.msg_ref.refs_0_.refs_1_), channel_id=1, source_target_pairs={{30,0},{31,1},{0,2},{1,3},{2,4},{3,5},{4,6},{5,7},{6,8},{7,9},{8,1... | collective-permute-start | bytes 147464 | tf_op jit(solution)/shard_map/ppermute | solution.py:642
  11.0 14.4 %collective-permute-start = (f32[32,384]{1,0:T(8,128)S(1)}, f32[32,384]{1,0:T(8,128)S(1)}, u32[]{:S(2)}, u32[]{:S(2)}) collective-permute-start(f32[32,384]{1,0:T(8,128)S(1)} %get-tuple-element.7.msg_ref.refs_0_.refs_1_), channel_id=1, source_target_pairs={{31,0},{30,1},{1,2},{0,3},{3,4},{2,5},{5,6},{4,7},{7,8},{6,9},{9,1... | collective-permute-start | bytes 147464 | tf_op jit(solution)/shard_map/ppermute | solution.py:642
  11.9 5.5 %copy-start.6 = (bf16[4,104,32]{2,1,0:T(8,128)(2,1)S(1)}, bf16[4,104,32]{2,1,0:T(8,128)(2,1)}, u32[]{:S(2)}) copy-start(bf16[4,104,32]{2,1,0:T(8,128)(2,1)} %constant.22.clone.own_table_ref.refs_6_) | copy-start | bytes 79876
  11.9 5.5 %copy-start.7 = (bf16[192,208]{1,0:T(8,128)(2,1)S(1)}, bf16[192,208]{1,0:T(8,128)(2,1)}, u32[]{:S(2)}) copy-start(bf16[192,208]{1,0:T(8,128)(2,1)} %constant.23.clone.other_table_ref) | copy-start | bytes 239620
  11.9 23.4 %all-to-all-start = ((f32[32,8,128]{2,1,0:T(8,128)}), f32[32,8,128]{2,1,0:T(8,128)S(1)}, u32[]{:S(2)}, u32[]{:S(2)}) async-start(f32[32,8,128]{2,1,0:T(8,128)} %get-tuple-element.8), calls=%async_computation | async-start | bytes 262144 | tf_op jit(solution)/shard_map/all_to_all | solution.py:673
  17.4 8.1 %copy-start.5 = (bf16[576,416]{1,0:T(8,128)(2,1)S(1)}, bf16[576,416]{1,0:T(8,128)(2,1)}, u32[]{:S(2)}) copy-start(bf16[576,416]{1,0:T(8,128)(2,1)} %constant.24.clone.refs_7_) | copy-start | bytes 1437700
  25.4 9.9 %copy-start = (bf16[176,912]{1,0:T(8,128)(2,1)S(1)}, bf16[176,912]{1,0:T(8,128)(2,1)}, u32[]{:S(2)}) copy-start(bf16[176,912]{1,0:T(8,128)(2,1)} %constant.28.clone.refs_10_) | copy-start | bytes 963076
  25.4 9.9 %copy-start.1 = (bf16[176,912]{1,0:T(8,128)(2,1)S(1)}, bf16[176,912]{1,0:T(8,128)(2,1)}, u32[]{:S(2)}) copy-start(bf16[176,912]{1,0:T(8,128)(2,1)} %constant.27.clone.refs_9_) | copy-start | bytes 963076
  25.4 9.9 %copy-start.2 = (f32[256,128]{1,0:T(8,128)S(1)}, f32[256,128]{1,0:T(8,128)}, u32[]{:S(2)}) copy-start(f32[256,128]{1,0:T(8,128)} %constant.26.clone.refs_12_) | copy-start | bytes 393220
  25.4 9.9 %copy-start.3 = (f32[128,256]{1,0:T(8,128)S(1)}, f32[128,256]{1,0:T(8,128)}, u32[]{:S(2)}) copy-start(f32[128,256]{1,0:T(8,128)} %constant.25.clone.refs_11_) | copy-start | bytes 393220

commit v2 on v1

--- a/solution.py
+++ b/solution.py
@@ -41,8 +41,6 @@
 
 FEATURES = 32
 SOURCES = 16
-COLUMN_ROWS = FEATURES + SOURCES
-PIECES = 26
 
 
 def round_up(value, step):
@@ -94,13 +92,10 @@
         self.coarse_rows = round_up(self.ci, 8)
         self.coarse_lanes = round_up(self.cj * self.ck, 128)
         self.own_rows = round_up(self.cols, 8)
-        self.outside = [
-            (x, y)
-            for x in range(-1, self.bx + 1)
-            for y in range(-1, self.by + 1)
-            if not (0 <= x < self.bx and 0 <= y < self.by)
+        self.columns = [
+            (x, y) for x in range(-1, self.bx + 1) for y in range(-1, self.by + 1)
         ]
-        self.halo_rows = round_up(len(self.outside), 8)
+        self.ext_rows = round_up(len(self.columns), 8)
         self.force_rows = round_up(3 * self.cols, 8)
 
     def col(self, x, y):
@@ -202,91 +197,42 @@
     coarse_ref[...] = jnp.broadcast_to(jnp.concatenate(sums, axis=0)[None], coarse_ref.shape)
 
 
-def other_rows(rows, columns):
-    table = np.zeros((COLUMN_ROWS * len(columns), PIECES * rows), np.float32)
-    for place, row in enumerate(columns):
-        base = COLUMN_ROWS * place
-        for comp in range(3):
-            for slot, piece in enumerate((0, 1, 2, 0, 1, 0)):
-                table[base + 6 * comp + slot, (3 * comp + piece) * rows + row] = 1.0
-        for piece in range(3):
-            table[base + 18 + piece, 12 * rows + row] = 1.0
-            table[base + 21 + piece, (9 + piece) * rows + row] = 1.0
-        for source in range(12):
-            table[base + FEATURES + source, (13 + source) * rows + row] = 1.0
-    return table
-
-
-def own_rows(brick):
-    rows = brick.own_rows
-    table = np.zeros((brick.cols, 13 * rows, FEATURES), np.float32)
-    for col in range(brick.cols):
-        for comp in range(3):
-            for slot, piece in enumerate((0, 0, 0, 1, 1, 2)):
-                table[col, (3 * comp + piece) * rows + col, 6 * comp + slot] = 2.0
-        for piece in range(3):
-            table[col, (9 + piece) * rows + col, 18 + piece] = 1.0
-            table[col, 12 * rows + col, 21 + piece] = 1.0
-    return table
-
-
-def stack_pieces(brick, rows, values, places, piece_ref, coord_ref=None):
-    atoms = brick.atoms
-
-    def extend(value):
-        return jnp.concatenate([value[:, -atoms:], value, value[:, :atoms]], axis=1)
-
-    index = lax.broadcasted_iota(jnp.int32, (rows, 1), 0)
-    offset_x = jnp.zeros((rows, 1), F32)
-    offset_y = jnp.zeros((rows, 1), F32)
-    for row, (x, y) in enumerate(places):
-        offset_x = jnp.where(index == row, x - 0.5 * brick.bx, offset_x)
-        offset_y = jnp.where(index == row, y - 0.5 * brick.by, offset_y)
-    along_z = [values[2][:, z * atoms : (z + 1) * atoms] for z in range(brick.bz)]
-    along_z = [along_z[-1]] + along_z + [along_z[0]]
-    along_z = [value + (z - 1 - 0.5 * brick.bz) for z, value in enumerate(along_z)]
-    coords = [
-        extend((values[0] + offset_x) * SCALE),
-        extend((values[1] + offset_y) * SCALE),
-        jnp.concatenate(along_z, axis=1) * SCALE,
+def store_pieces(piece_ref, rows, arrays):
+    for number, value in enumerate(arrays):
+        for block in range(piece_ref.shape[0]):
+            piece_ref[block, number * rows : (number + 1) * rows, :] = value[
+                :, block * 128 : (block + 1) * 128
+            ]
+
+
+def load_pieces(piece_ref, rows, row, count):
+    parts = [
+        piece_ref[block, pl.ds(row, count, stride=rows), :] for block in range(piece_ref.shape[0])
     ]
-    charge = extend(values[3])
-    square = HALF_CONST - (
-        coords[0] * coords[0] + coords[1] * coords[1] + coords[2] * coords[2]
-    )
-    pieces = []
-    for value in coords + [square]:
-        pieces += split(value, 3)
-    pieces.append(jnp.ones((rows, brick.wide), F32))
+    return jnp.concatenate(parts, axis=1)
+
+
+def feature_arrays(coords, square, order, square_first):
+    rows = coords[0].shape
+    arrays = []
+    for value in coords:
+        pieces = split(value, 3)
+        arrays += [pieces[piece] for piece in order]
+    squares = split(square, 3)
+    ones = [jnp.ones(rows, F32)] * 3
+    arrays += squares + ones if square_first else ones + squares
+    return arrays + [jnp.zeros(rows, F32)] * (FEATURES - len(arrays))
+
+
+def source_arrays(coords, charge):
+    arrays = []
     for value in [charge] + [charge * coord for coord in coords]:
-        pieces += split(value, 3)
-    pieces.append(jnp.zeros((rows, brick.wide), F32))
-    for number, piece in enumerate(pieces):
-        piece_ref[number * rows : (number + 1) * rows, :] = piece
-    if coord_ref is not None:
-        for comp in range(3):
-            coord_ref[comp * rows : (comp + 1) * rows, :] = coords[comp]
-
-
-def load_own(brick, msg_ref, piece_ref, coord_ref):
-    pad = brick.own_rows - brick.cols
-    values = []
-    for k in range(4):
-        value = msg_ref[k * brick.cols : (k + 1) * brick.cols, 0 : brick.lanes]
-        if pad:
-            value = jnp.concatenate([value, jnp.zeros((pad, brick.lanes), F32)], axis=0)
-        values.append(value)
-    places = [(x, y) for x in range(brick.bx) for y in range(brick.by)]
-    stack_pieces(brick, brick.own_rows, values, places, piece_ref, coord_ref)
-
-
-def load_left(brick, piece_ref, own_table_ref, left_ref):
-    span = slice(brick.atoms, brick.atoms + brick.lanes)
-    rows = 13 * brick.own_rows
-    full = round_up(rows, 128)
-    turned = piece_ref[0:full, span].T[:, 0:rows].astype(BF16)
-    for col in range(brick.cols):
-        left_ref[col] = mul(turned, own_table_ref[col]).astype(BF16)
+        arrays += split(value, 3)
+    return arrays + [jnp.zeros(charge.shape, F32)] * (SOURCES - len(arrays))
+
+
+def minus_square(coords):
+    return HALF_CONST - (coords[0] * coords[0] + coords[1] * coords[1] + coords[2] * coords[2])
 
 
 def pair_factor(left, right):
@@ -302,125 +248,149 @@
     return high, low
 
 
-def sources(other_ref, place, span):
-    base = COLUMN_ROWS * place
-    return other_ref[base + FEATURES : base + COLUMN_ROWS, span]
-
-
-def features(other_ref, place, span):
-    base = COLUMN_ROWS * place
-    return other_ref[base : base + FEATURES, span]
-
-
 def moments(total, quantity):
     base = 3 * quantity
     return total[base : base + 1] + total[base + 1 : base + 2] + total[base + 2 : base + 3]
 
 
-def inner_kernel(
-    brick,
-    msg_ref,
-    own_table_ref,
-    other_table_ref,
-    force_ref,
-    piece_ref,
-    coord_ref,
-    left_ref,
-    other_ref,
-    total_ref,
-):
-    atoms = brick.atoms
-    load_own(brick, msg_ref, piece_ref, coord_ref)
-    load_left(brick, piece_ref, own_table_ref, left_ref)
-    other_ref[...] = mul(other_table_ref[...], piece_ref[...].astype(BF16)).astype(BF16)
-    total_ref[...] = jnp.zeros(total_ref.shape, F32)
-    force_ref[...] = jnp.zeros(force_ref.shape, F32)
-
-    def block(col, other, z, span, first_back):
-        own_span = slice((z + 1) * atoms, (z + 2) * atoms)
-        left = left_ref[col, z * atoms : (z + 1) * atoms, :]
-        high, low = pair_factor(left, features(other_ref, other, span))
-        source = sources(other_ref, other, span)
-        total_ref[col, :, own_span] += mul_t(source, high) + mul_t(source, low)
-        back = sources(other_ref, col, own_span)
-        back_span = slice(span.start + first_back, span.stop)
-        total_ref[other, :, back_span] += mul(back, high[:, first_back:]) + mul(
-            back, low[:, first_back:]
-        )
-
-    cells = [(x, y) for x in range(brick.bx) for y in range(brick.by)]
-    for first, (x, y) in enumerate(cells):
-        for second in range(first + 1, len(cells)):
-            if max(abs(x - cells[second][0]), abs(y - cells[second][1])) > 1:
-                continue
-            for z in range(brick.bz):
-                block(first, second, z, slice(z * atoms, (z + 3) * atoms), 0)
-    for col in range(brick.cols):
-        for z in range(brick.bz):
-            block(col, col, z, slice((z + 1) * atoms, (z + 3) * atoms), atoms)
-
-    for col in range(brick.cols):
-        total = total_ref[col]
-        charge = msg_ref[3 * brick.cols + col : 3 * brick.cols + col + 1, 0 : brick.lanes]
-        weight = moments(total, 0)
-        for comp in range(3):
-            row = comp * brick.own_rows + col
-            wide = coord_ref[row : row + 1, :] * weight - moments(total, 1 + comp)
-            parts = [wide[:, (z + 1) * atoms : (z + 2) * atoms] for z in range(brick.bz)]
-            parts[-1] = parts[-1] + wide[:, :atoms]
-            parts[0] = parts[0] + wide[:, -atoms:]
-            row = comp * brick.cols + col
-            force_ref[row : row + 1, :] = (
-                jnp.concatenate(parts, axis=1) * charge * (SCALE * SCALE)
-            )
-
-
-def halo_kernel(brick, sender, n_msgs, *refs):
-    atoms = brick.atoms
+def pairs_kernel(brick, sender, n_msgs, *refs):
+    atoms, lanes = brick.atoms, brick.lanes
     msg_ref = refs[0]
     other_msgs = refs[1 : 1 + n_msgs]
-    own_table_ref, other_table_ref, part_ref, force_ref = refs[1 + n_msgs : 5 + n_msgs]
-    piece_ref, coord_ref, left_ref, row_ref, halo_ref, other_ref = refs[5 + n_msgs :]
-    load_own(brick, msg_ref, piece_ref, coord_ref)
-    load_left(brick, piece_ref, own_table_ref, left_ref)
-    rows = brick.halo_rows
-    row_ref[...] = jnp.zeros(row_ref.shape, F32)
-    for place, (x, y) in enumerate(brick.outside):
-        near = other_msgs[sender[(x // brick.bx, y // brick.by)]]
+    force_ref = refs[1 + n_msgs]
+    (
+        row_ref,
+        other_piece_ref,
+        source_piece_ref,
+        own_piece_ref,
+        own_source_ref,
+        left_ref,
+        source_ref,
+        right_ref,
+        back_ref,
+        back_sum_ref,
+    ) = refs[2 + n_msgs :]
+    half = 0.5 * brick.bz
+
+    rows = brick.ext_rows
+    if rows > len(brick.columns):
+        row_ref[...] = jnp.zeros(row_ref.shape, F32)
+    for place, (x, y) in enumerate(brick.columns):
+        shift = (x // brick.bx, y // brick.by)
+        near = msg_ref if shift == (0, 0) else other_msgs[sender[shift]]
         col = brick.col(x % brick.bx, y % brick.by)
         for k in range(4):
             row_ref[k * rows + place : k * rows + place + 1, :] = near[
-                k * brick.cols + col : k * brick.cols + col + 1, 0 : brick.lanes
+                k * brick.cols + col : k * brick.cols + col + 1, 0:lanes
             ]
-    values = [row_ref[k * rows : (k + 1) * rows, :] for k in range(4)]
-    stack_pieces(brick, rows, values, brick.outside, halo_ref)
-    other_ref[...] = mul(other_table_ref[...], halo_ref[...].astype(BF16)).astype(BF16)
-    force_ref[...] = part_ref[...]
+    index = lax.broadcasted_iota(jnp.int32, (rows, 1), 0)
+    ext_y = brick.by + 2
+    offset_x = (index // ext_y - 1).astype(F32) - 0.5 * brick.bx
+    offset_y = (index % ext_y - 1).astype(F32) - 0.5 * brick.by
+    lane_z = (lax.broadcasted_iota(jnp.int32, (1, lanes), 1) // atoms).astype(F32)
+    coords = [
+        (row_ref[0:rows, :] + offset_x) * SCALE,
+        (row_ref[rows : 2 * rows, :] + offset_y) * SCALE,
+        (row_ref[2 * rows : 3 * rows, :] + (lane_z - half)) * SCALE,
+    ]
+    charge = row_ref[3 * rows : 4 * rows, :]
+    store_pieces(
+        other_piece_ref,
+        rows,
+        feature_arrays(coords, minus_square(coords), (0, 1, 2, 0, 1, 0), False),
+    )
+    store_pieces(source_piece_ref, rows, source_arrays(coords, charge))
+    for place in range(len(brick.columns)):
+        feature = load_pieces(other_piece_ref, rows, place, FEATURES)
+        left_ref[place] = feature.T.astype(BF16)
+        source = load_pieces(source_piece_ref, rows, place, SOURCES).astype(BF16)
+        for z in range(brick.bz):
+            part = source[:, z * atoms : (z + 1) * atoms]
+            source_ref[place, z] = jnp.concatenate([part, part], axis=1)
+
+    rows = brick.own_rows
+    own = []
+    for k in range(4):
+        value = msg_ref[k * brick.cols : (k + 1) * brick.cols, 0:lanes]
+        if rows > brick.cols:
+            value = jnp.concatenate([value, jnp.zeros((rows - brick.cols, lanes), F32)], axis=0)
+        own.append(value)
+    index = lax.broadcasted_iota(jnp.int32, (rows, 1), 0)
+    own_x = (own[0] + ((index // brick.by).astype(F32) - 0.5 * brick.bx)) * SCALE
+    own_y = (own[1] + ((index % brick.by).astype(F32) - 0.5 * brick.by)) * SCALE
+    own_z = []
+    for other_z in range(brick.bz):
+        step = other_z - lane_z
+        step = jnp.where(step > half, step - brick.bz, step)
+        step = jnp.where(step < -half, step + brick.bz, step)
+        own_z.append((own[2] + (other_z - step - half)) * SCALE)
+        coords = [own_x, own_y, own_z[-1]]
+        arrays = feature_arrays(coords, minus_square(coords), (0, 0, 0, 1, 1, 2), True)
+        arrays = [2.0 * value for value in arrays[:18]] + arrays[18:]
+        store_pieces(own_piece_ref, rows, arrays)
+        store_pieces(own_source_ref, rows, source_arrays(coords, own[3]))
+        for col in range(brick.cols):
+            part = load_pieces(own_piece_ref, rows, col, FEATURES)
+            right_ref[col, other_z] = part.astype(BF16)
+            part = load_pieces(own_source_ref, rows, col, SOURCES).astype(BF16)
+            back_ref[col, other_z] = jnp.concatenate([part, part], axis=1)
+
+    back_sum_ref[...] = jnp.zeros(back_sum_ref.shape, F32)
     for x in range(brick.bx):
         for y in range(brick.by):
             col = brick.col(x, y)
-            near = [
-                place
-                for place, (ox, oy) in enumerate(brick.outside)
-                if max(abs(ox - x), abs(oy - y)) <= 1
-            ]
+            here = brick.columns.index((x, y))
+            forces = [0.0, 0.0, 0.0]
             for z in range(brick.bz):
-                span = slice(z * atoms, (z + 3) * atoms)
-                own_span = slice(z * atoms, (z + 1) * atoms)
-                left = left_ref[col, own_span, :]
-                total = jnp.zeros((SOURCES, atoms), F32)
-                for place in near:
-                    high, low = pair_factor(left, features(other_ref, place, span))
-                    source = sources(other_ref, place, span)
-                    total = total + (mul_t(source, high) + mul_t(source, low))
-                charge = msg_ref[3 * brick.cols + col : 3 * brick.cols + col + 1, own_span]
+                total = jnp.zeros((SOURCES, lanes), F32)
+                right = right_ref[col, z]
+                back = back_ref[col, z]
+                for place, (ox, oy) in enumerate(brick.columns):
+                    if max(abs(ox - x), abs(oy - y)) > 1:
+                        continue
+                    inside = 0 <= ox < brick.bx and 0 <= oy < brick.by
+                    if inside and place < here:
+                        continue
+                    left = left_ref[place, z * atoms : (z + 1) * atoms, :]
+                    if place != here:
+                        high, low = pair_factor(left, right)
+                        total = total + mul(
+                            source_ref[place, z], jnp.concatenate([high, low], axis=0)
+                        )
+                        if inside:
+                            back_sum_ref[brick.col(ox, oy), z] += mul_t(
+                                back, jnp.concatenate([high, low], axis=1)
+                            )
+                        continue
+                    after = (z + 1) % brick.bz
+                    spans = [slice(cell * atoms, (cell + 1) * atoms) for cell in (z, after)]
+                    both = jnp.concatenate([right[:, span] for span in spans], axis=1)
+                    high, low = pair_factor(left, both)
+                    part = mul(source_ref[place, z], jnp.concatenate([high, low], axis=0))
+                    parts = [jnp.zeros((SOURCES, atoms), F32)] * brick.bz
+                    parts[z] = part[:, :atoms]
+                    parts[after] = part[:, atoms:]
+                    total = total + jnp.concatenate(parts, axis=1)
+                    back_sum_ref[col, z] += mul_t(
+                        jnp.concatenate([back[:, spans[1]]] * 2, axis=1),
+                        jnp.concatenate([high[:, atoms:], low[:, atoms:]], axis=1),
+                    )
                 weight = moments(total, 0)
-                for comp in range(3):
-                    row = comp * brick.own_rows + col
-                    coord = coord_ref[row : row + 1, (z + 1) * atoms : (z + 2) * atoms]
-                    value = (coord * weight - moments(total, 1 + comp)) * charge
-                    row = comp * brick.cols + col
-                    force_ref[row : row + 1, own_span] += value * (SCALE * SCALE)
+                for comp, coord in enumerate((own_x, own_y, own_z[z])):
+                    value = coord[col : col + 1] * weight - moments(total, 1 + comp)
+                    forces[comp] = forces[comp] + value
+            for comp in range(3):
+                row = comp * brick.cols + col
+                force_ref[row : row + 1, :] = forces[comp]
+    for col in range(brick.cols):
+        total = jnp.concatenate([back_sum_ref[col, z] for z in range(brick.bz)], axis=1)
+        weight = moments(total, 0)
+        home = (own[2] + (lane_z - half)) * SCALE
+        for comp, coord in enumerate((own_x, own_y, home)):
+            row = comp * brick.cols + col
+            value = coord[col : col + 1] * weight - moments(total, 1 + comp)
+            value = value + force_ref[row : row + 1, :]
+            force_ref[row : row + 1, :] = value * (own[3][col : col + 1] * (SCALE * SCALE))
 
 
 def fine_tables(brick):
@@ -647,9 +617,6 @@
 def body(n_space, n_sub, positions, charges, counts):
     brick = Brick(charges.shape, n_space, n_sub)
     n_dev = n_space * n_sub
-    own_table = jnp.asarray(own_rows(brick), BF16)
-    inner_table = jnp.asarray(other_rows(brick.own_rows, range(brick.cols)), BF16)
-    outer_table = jnp.asarray(other_rows(brick.halo_rows, range(len(brick.outside))), BF16)
     along_xy, along_z = fine_tables(brick)
     xy_high = along_xy.astype(BF16)
     xy_low = (along_xy - xy_high.astype(np.float32)).astype(BF16)
@@ -673,43 +640,26 @@
     whole = lax.all_to_all(coarse, ("space", "sub"), 0, 0, tiled=True)
     whole = whole.reshape(n_space, n_sub, brick.coarse_rows, brick.coarse_lanes)
 
-    own_scratch = [
-        pltpu.VMEM((PIECES * brick.own_rows, brick.wide), F32),
-        pltpu.VMEM((3 * brick.own_rows, brick.wide), F32),
-        pltpu.VMEM((brick.cols, brick.lanes, FEATURES), BF16),
-    ]
-    force_shape = jax.ShapeDtypeStruct((brick.force_rows, brick.lanes), F32)
-    part = call(
-        functools.partial(inner_kernel, brick),
-        force_shape,
-        [VMEM] * 3,
-        own_scratch
-        + [
-            pltpu.VMEM((COLUMN_ROWS * brick.cols, brick.wide), BF16),
-            pltpu.VMEM((brick.cols, SOURCES, brick.wide), F32),
-        ],
-        10**10,
-        msg,
-        own_table,
-        inner_table,
-    )
-    n_out = len(brick.outside)
+    n_col = len(brick.columns)
     short = call(
-        functools.partial(halo_kernel, brick, sender, len(msgs)),
-        force_shape,
-        [VMEM] * (4 + len(msgs)),
-        own_scratch
-        + [
-            pltpu.VMEM((4 * brick.halo_rows, brick.lanes), F32),
-            pltpu.VMEM((PIECES * brick.halo_rows, brick.wide), F32),
-            pltpu.VMEM((COLUMN_ROWS * n_out, brick.wide), BF16),
+        functools.partial(pairs_kernel, brick, sender, len(msgs)),
+        jax.ShapeDtypeStruct((brick.force_rows, brick.lanes), F32),
+        [VMEM] * (1 + len(msgs)),
+        [
+            pltpu.VMEM((4 * brick.ext_rows, brick.lanes), F32),
+            pltpu.VMEM((brick.lanes // 128, FEATURES * brick.ext_rows, 128), F32),
+            pltpu.VMEM((brick.lanes // 128, SOURCES * brick.ext_rows, 128), F32),
+            pltpu.VMEM((brick.lanes // 128, FEATURES * brick.own_rows, 128), F32),
+            pltpu.VMEM((brick.lanes // 128, SOURCES * brick.own_rows, 128), F32),
+            pltpu.VMEM((n_col, brick.lanes, FEATURES), BF16),
+            pltpu.VMEM((n_col, brick.bz, SOURCES, 2 * brick.atoms), BF16),
+            pltpu.VMEM((brick.cols, brick.bz, FEATURES, brick.lanes), BF16),
+            pltpu.VMEM((brick.cols, brick.bz, SOURCES, 2 * brick.lanes), BF16),
+            pltpu.VMEM((brick.cols, brick.bz, SOURCES, brick.atoms), F32),
         ],
         10**10,
         msg,
         *msgs,
-        own_table,
-        outer_table,
-        part,
     )
     ext_x = brick.px + 2 * REACH
     rows_y = brick.py + POINTS * brick.by

time: 39.6 us -> 41.2 us (1.040)
  waiting for transfers between devices: 0.02 us -> 1.24 us
  Pallas kernels: 23.1 us -> 23.6 us
    ppermute x5, waiting for transfers between devices: 0.01 us -> 1.24 us  [neighbours(): msgs.append(lax.ppermute(msg, ('space', 'sub'), pairs))]
    pallas_call x4 -> x3, Pallas kernels: 23.1 us -> 23.6 us  [call(): pl.pallas_call(kernel, out_shape=out_shape, in_specs=in_specs, out_specs=...]
    unnamed x18 -> x12, local copies, waits for them, and re-layouts: 1.47 us -> 1.45 us
  transfers between devices with their start and end apart: 6 -> 6, of which waited for: 0 -> 1; matrix products, arithmetic and copies ran while one was open for 0% -> 0% of each run, Pallas kernels for 45% -> 44%
where the time goes in v2:
time: 41.2 us; the launch traced here: 41 us
  Pallas kernels  23.6 us (57%)
  starting transfers between devices  13.9 us (34%)
  local copies, waits for them, and re-layouts  2.07 us (5%)
  waiting for transfers between devices  1.24 us (3%)
    pallas_call x3, Pallas kernels, call(): pl.pallas_call(kernel, out_shape=out_shape, in_specs=in_specs, out_specs=...  23.6 us
    ppermute x5, starting transfers between devices, neighbours(): msgs.append(lax.ppermute(msg, ('space', 'sub'), pairs))  8.4 us
    all_to_all x1, starting transfers between devices, body(): whole = lax.all_to_all(coarse, ('space', 'sub'), 0, 0, tiled=True)  5.48 us
    unnamed x12, local copies, waits for them, and re-layouts  1.45 us
    ppermute x5, waiting for transfers between devices, neighbours(): msgs.append(lax.ppermute(msg, ('space', 'sub'), pairs))  1.24 us
  transfers between devices with their start and end apart: 6, of which 1 were waited for; matrix products, arithmetic and copies ran while one was open for 0% of the time, Pallas kernels for 44%

profile of v2, /device:TPU:0, one launch (start us, length us, event | category | flops | bytes accessed | tf_op | source)
XLA Modules:
  0.0 41.0 jit_solution(11517463412181876461)
XLA Ops:
  0.0 0.7 %copy.9.charge_ref = f32[2,2,3,128]{3,2,1,0:T(4,128)S(1)} copy(f32[2,2,3,128]{3,1,2,0:T(2,128)} %param.8) | data formatting | bytes 12288 | tf_op args[1]
  0.7 0.0 copy-start.4
  0.7 0.7 %copy.8.pos_ref = f32[3,2,2,3,128]{4,3,2,1,0:T(4,128)S(1)} copy(f32[3,2,2,3,128]{4,2,3,1,0:T(2,128)} %param.7) | data formatting | bytes 36864 | tf_op args[0]
  1.4 0.0 copy-done.4
  1.4 2.0 %shard_map.73 = (f32[32,384]{1,0:T(8,128)S(1)}, f32[32,8,128]{2,1,0:T(8,128)}) custom-call(s32[2,2,3]{2,1,0:T(2,128)S(1)} %copy-done.4, f32[3,2,2,3,128]{4,3,2,1,0:T(4,128)S(1)} %copy.8.pos_ref, f32[2,2,3,128]{3,2,1,0:T(4,128)S(1)} %copy.9.charge_ref), custom_call_target="tpu_custom_call" | custom-call | flops 10000000 | bytes 100000 | tf_op jit(solution)/shard_map/pallas_call | solution.py:585
  3.5 5.4 %collective-permute-start.4 = (f32[32,384]{1,0:T(8,128)S(1)}, f32[32,384]{1,0:T(8,128)S(1)}, u32[]{:S(2)}, u32[]{:S(2)}) collective-permute-start(f32[32,384]{1,0:T(8,128)S(1)} %get-tuple-element.7.refs_0_.refs_1_), channel_id=1, source_target_pairs={{2,0},{3,1},{4,2},{5,3},{6,4},{7,5},{8,6},{9,7},{10,8},{11,9},{12,... | collective-permute-start | bytes 147464 | tf_op jit(solution)/shard_map/ppermute | solution.py:612
  8.9 1.6 %collective-permute-start.3 = (f32[32,384]{1,0:T(8,128)S(1)}, f32[32,384]{1,0:T(8,128)S(1)}, u32[]{:S(2)}, u32[]{:S(2)}) collective-permute-start(f32[32,384]{1,0:T(8,128)S(1)} %get-tuple-element.7.refs_0_.refs_1_), channel_id=1, source_target_pairs={{3,0},{2,1},{5,2},{4,3},{7,4},{6,5},{9,6},{8,7},{11,8},{10,9},{13,... | collective-permute-start | bytes 147464 | tf_op jit(solution)/shard_map/ppermute | solution.py:612
  10.5 0.5 %collective-permute-start.2 = (f32[32,384]{1,0:T(8,128)S(1)}, f32[32,384]{1,0:T(8,128)S(1)}, u32[]{:S(2)}, u32[]{:S(2)}) collective-permute-start(f32[32,384]{1,0:T(8,128)S(1)} %get-tuple-element.7.refs_0_.refs_1_), channel_id=1, source_target_pairs={{1,0},{0,1},{3,2},{2,3},{5,4},{4,5},{7,6},{6,7},{9,8},{8,9},{11,10... | collective-permute-start | bytes 147464 | tf_op jit(solution)/shard_map/ppermute | solution.py:612
  11.0 0.0 collective-permute-start.1
  11.0 0.8 %collective-permute-start = (f32[32,384]{1,0:T(8,128)S(1)}, f32[32,384]{1,0:T(8,128)S(1)}, u32[]{:S(2)}, u32[]{:S(2)}) collective-permute-start(f32[32,384]{1,0:T(8,128)S(1)} %get-tuple-element.7.refs_0_.refs_1_), channel_id=1, source_target_pairs={{31,0},{30,1},{1,2},{0,3},{3,4},{2,5},{5,6},{4,7},{7,8},{6,9},{9,1... | collective-permute-start | bytes 147464 | tf_op jit(solution)/shard_map/ppermute | solution.py:612
  11.9 5.5 %all-to-all-start = ((f32[32,8,128]{2,1,0:T(8,128)}), f32[32,8,128]{2,1,0:T(8,128)S(1)}, u32[]{:S(2)}, u32[]{:S(2)}) async-start(f32[32,8,128]{2,1,0:T(8,128)} %get-tuple-element.8), calls=%async_computation | async-start | bytes 262144 | tf_op jit(solution)/shard_map/all_to_all | solution.py:640
  17.3 0.1 pad_add_fusion.refs_0_
  17.4 0.0 copy-start
  17.4 0.0 copy-start.1
  17.4 0.0 copy-start.2
  17.4 0.0 copy-start.3
  17.4 0.0 collective-permute-done.4.refs_5_.refs_6_
  17.4 0.0 collective-permute-done.3.refs_4_.refs_5_
  17.5 0.0 collective-permute-done.2.refs_3_.refs_4_
  17.5 0.0 collective-permute-done.1.refs_2_.refs_3_
  17.5 1.2 %collective-permute-done.refs_1_.refs_2_ = f32[32,384]{1,0:T(8,128)S(1)} collective-permute-done((f32[32,384]{1,0:T(8,128)S(1)}, f32[32,384]{1,0:T(8,128)S(1)}, u32[]{:S(2)}, u32[]{:S(2)}) %collective-permute-start) | collective-permute-done | bytes 49184 | tf_op jit(solution)/shard_map/ppermute | solution.py:612
  18.7 18.2 %shard_map.74.refs_8_ = f32[16,384]{1,0:T(8,128)S(1)} custom-call(f32[32,384]{1,0:T(8,128)S(1)} %get-tuple-element.7.refs_0_.refs_1_, f32[32,384]{1,0:T(8,128)S(1)} %collective-permute-done.refs_1_.refs_2_, f32[32,384]{1,0:T(8,128)S(1)} %collective-permute-done.1.refs_2_.refs_3_, f32[32,384]{1,0:T(8,128)S(1)} %collective-permute-done.2.refs_3_.refs_4_, ...), custom_call_target="tpu_custom_call" | custom-call | flops 10000000000 | bytes 100000 | tf_op jit(solution)/shard_map/pallas_call | solution.py:585
  36.9 0.0 all-to-all-done
  36.9 0.0 copy-done
  36.9 0.0 copy-done.1
  37.0 0.0 copy-done.2
  37.0 0.0 copy-done.3
  37.0 3.4 %shard_map.75 = f32[3,2,2,3,128]{4,3,2,1,0:T(4,128)S(1)} custom-call(s32[2]{0:T(128)S(1)} %pad_add_fusion.refs_0_, f32[32,384]{1,0:T(8,128)S(1)} %get-tuple-element.7.refs_0_.refs_1_, f32[32,384]{1,0:T(8,128)S(1)} %collective-permute-done.refs_1_.refs_2_, f32[32,384]{1,0:T(8,128)S(1)} %collective-permute-done.1.refs_2_.refs_3_, ...), custom_call_target="tpu_custom_call" | custom-call | flops 100000000 | bytes 100000 | tf_op jit(solution)/shard_map/pallas_call | solution.py:585
  40.4 0.6 %copy.10 = f32[3,2,2,3,128]{4,2,3,1,0:T(2,128)} copy(f32[3,2,2,3,128]{4,3,2,1,0:T(4,128)S(1)} %shard_map.75) | data formatting | bytes 36864 | tf_op jit(solution)/shard_map/pallas_call | solution.py:585
Async XLA Ops:
  0.7 0.7 %copy-start.4 = (s32[2,2,3]{2,1,0:T(2,128)S(1)}, s32[2,2,3]{2,1,0:T(2,128)}, u32[]{:S(2)}) copy-start(s32[2,2,3]{2,1,0:T(2,128)} %counts_ref.1) | copy-start | bytes 148
  3.5 14.0 %collective-permute-start.4 = (f32[32,384]{1,0:T(8,128)S(1)}, f32[32,384]{1,0:T(8,128)S(1)}, u32[]{:S(2)}, u32[]{:S(2)}) collective-permute-start(f32[32,384]{1,0:T(8,128)S(1)} %get-tuple-element.7.refs_0_.refs_1_), channel_id=1, source_target_pairs={{2,0},{3,1},{4,2},{5,3},{6,4},{7,5},{8,6},{9,7},{10,8},{11,9},{12,... | collective-permute-start | bytes 147464 | tf_op jit(solution)/shard_map/ppermute | solution.py:612
  8.9 8.6 %collective-permute-start.3 = (f32[32,384]{1,0:T(8,128)S(1)}, f32[32,384]{1,0:T(8,128)S(1)}, u32[]{:S(2)}, u32[]{:S(2)}) collective-permute-start(f32[32,384]{1,0:T(8,128)S(1)} %get-tuple-element.7.refs_0_.refs_1_), channel_id=1, source_target_pairs={{3,0},{2,1},{5,2},{4,3},{7,4},{6,5},{9,6},{8,7},{11,8},{10,9},{13,... | collective-permute-start | bytes 147464 | tf_op jit(solution)/shard_map/ppermute | solution.py:612
  10.5 7.0 %collective-permute-start.2 = (f32[32,384]{1,0:T(8,128)S(1)}, f32[32,384]{1,0:T(8,128)S(1)}, u32[]{:S(2)}, u32[]{:S(2)}) collective-permute-start(f32[32,384]{1,0:T(8,128)S(1)} %get-tuple-element.7.refs_0_.refs_1_), channel_id=1, source_target_pairs={{1,0},{0,1},{3,2},{2,3},{5,4},{4,5},{7,6},{6,7},{9,8},{8,9},{11,10... | collective-permute-start | bytes 147464 | tf_op jit(solution)/shard_map/ppermute | solution.py:612
  11.0 6.5 %collective-permute-start.1 = (f32[32,384]{1,0:T(8,128)S(1)}, f32[32,384]{1,0:T(8,128)S(1)}, u32[]{:S(2)}, u32[]{:S(2)}) collective-permute-start(f32[32,384]{1,0:T(8,128)S(1)} %get-tuple-element.7.refs_0_.refs_1_), channel_id=1, source_target_pairs={{30,0},{31,1},{0,2},{1,3},{2,4},{3,5},{4,6},{5,7},{6,8},{7,9},{8,1... | collective-permute-start | bytes 147464 | tf_op jit(solution)/shard_map/ppermute | solution.py:612
  11.0 7.7 %collective-permute-start = (f32[32,384]{1,0:T(8,128)S(1)}, f32[32,384]{1,0:T(8,128)S(1)}, u32[]{:S(2)}, u32[]{:S(2)}) collective-permute-start(f32[32,384]{1,0:T(8,128)S(1)} %get-tuple-element.7.refs_0_.refs_1_), channel_id=1, source_target_pairs={{31,0},{30,1},{1,2},{0,3},{3,4},{2,5},{5,6},{4,7},{7,8},{6,9},{9,1... | collective-permute-start | bytes 147464 | tf_op jit(solution)/shard_map/ppermute | solution.py:612
  11.9 25.1 %all-to-all-start = ((f32[32,8,128]{2,1,0:T(8,128)}), f32[32,8,128]{2,1,0:T(8,128)S(1)}, u32[]{:S(2)}, u32[]{:S(2)}) async-start(f32[32,8,128]{2,1,0:T(8,128)} %get-tuple-element.8), calls=%async_computation | async-start | bytes 262144 | tf_op jit(solution)/shard_map/all_to_all | solution.py:640
  17.4 19.5 %copy-start = (bf16[176,912]{1,0:T(8,128)(2,1)S(1)}, bf16[176,912]{1,0:T(8,128)(2,1)}, u32[]{:S(2)}) copy-start(bf16[176,912]{1,0:T(8,128)(2,1)} %constant.19.clone.refs_10_) | copy-start | bytes 963076
  17.4 19.5 %copy-start.1 = (bf16[176,912]{1,0:T(8,128)(2,1)S(1)}, bf16[176,912]{1,0:T(8,128)(2,1)}, u32[]{:S(2)}) copy-start(bf16[176,912]{1,0:T(8,128)(2,1)} %constant.18.clone.refs_9_) | copy-start | bytes 963076
  17.4 19.5 %copy-start.2 = (f32[256,128]{1,0:T(8,128)S(1)}, f32[256,128]{1,0:T(8,128)}, u32[]{:S(2)}) copy-start(f32[256,128]{1,0:T(8,128)} %constant.17.clone.refs_12_) | copy-start | bytes 393220
  17.4 19.5 %copy-start.3 = (f32[128,256]{1,0:T(8,128)S(1)}, f32[128,256]{1,0:T(8,128)}, u32[]{:S(2)}) copy-start(f32[128,256]{1,0:T(8,128)} %constant.16.clone.refs_11_) | copy-start | bytes 393220

commit v3 on v2

--- a/solution.py
+++ b/solution.py
@@ -96,6 +96,7 @@
             (x, y) for x in range(-1, self.bx + 1) for y in range(-1, self.by + 1)
         ]
         self.ext_rows = round_up(len(self.columns), 8)
+        self.kept = 2 * self.atoms * (1 + self.bz * (self.cols - 1))
         self.force_rows = round_up(3 * self.cols, 8)
 
     def col(self, x, y):
@@ -268,7 +269,8 @@
         source_ref,
         right_ref,
         back_ref,
-        back_sum_ref,
+        total_ref,
+        kept_ref,
     ) = refs[2 + n_msgs :]
     half = 0.5 * brick.bz
 
@@ -318,13 +320,13 @@
     index = lax.broadcasted_iota(jnp.int32, (rows, 1), 0)
     own_x = (own[0] + ((index // brick.by).astype(F32) - 0.5 * brick.bx)) * SCALE
     own_y = (own[1] + ((index % brick.by).astype(F32) - 0.5 * brick.by)) * SCALE
-    own_z = []
+    own_z_coords = []
     for other_z in range(brick.bz):
         step = other_z - lane_z
         step = jnp.where(step > half, step - brick.bz, step)
         step = jnp.where(step < -half, step + brick.bz, step)
-        own_z.append((own[2] + (other_z - step - half)) * SCALE)
-        coords = [own_x, own_y, own_z[-1]]
+        own_z_coords.append((own[2] + (other_z - step - half)) * SCALE)
+        coords = [own_x, own_y, own_z_coords[-1]]
         arrays = feature_arrays(coords, minus_square(coords), (0, 0, 0, 1, 1, 2), True)
         arrays = [2.0 * value for value in arrays[:18]] + arrays[18:]
         store_pieces(own_piece_ref, rows, arrays)
@@ -333,63 +335,66 @@
             part = load_pieces(own_piece_ref, rows, col, FEATURES)
             right_ref[col, other_z] = part.astype(BF16)
             part = load_pieces(own_source_ref, rows, col, SOURCES).astype(BF16)
-            back_ref[col, other_z] = jnp.concatenate([part, part], axis=1)
-
-    back_sum_ref[...] = jnp.zeros(back_sum_ref.shape, F32)
-    for x in range(brick.bx):
-        for y in range(brick.by):
-            col = brick.col(x, y)
-            here = brick.columns.index((x, y))
-            forces = [0.0, 0.0, 0.0]
             for z in range(brick.bz):
-                total = jnp.zeros((SOURCES, lanes), F32)
-                right = right_ref[col, z]
-                back = back_ref[col, z]
-                for place, (ox, oy) in enumerate(brick.columns):
-                    if max(abs(ox - x), abs(oy - y)) > 1:
-                        continue
-                    inside = 0 <= ox < brick.bx and 0 <= oy < brick.by
-                    if inside and place < here:
-                        continue
-                    left = left_ref[place, z * atoms : (z + 1) * atoms, :]
-                    if place != here:
-                        high, low = pair_factor(left, right)
-                        total = total + mul(
-                            source_ref[place, z], jnp.concatenate([high, low], axis=0)
-                        )
-                        if inside:
-                            back_sum_ref[brick.col(ox, oy), z] += mul_t(
-                                back, jnp.concatenate([high, low], axis=1)
-                            )
-                        continue
-                    after = (z + 1) % brick.bz
-                    spans = [slice(cell * atoms, (cell + 1) * atoms) for cell in (z, after)]
-                    both = jnp.concatenate([right[:, span] for span in spans], axis=1)
-                    high, low = pair_factor(left, both)
-                    part = mul(source_ref[place, z], jnp.concatenate([high, low], axis=0))
-                    parts = [jnp.zeros((SOURCES, atoms), F32)] * brick.bz
-                    parts[z] = part[:, :atoms]
-                    parts[after] = part[:, atoms:]
-                    total = total + jnp.concatenate(parts, axis=1)
-                    back_sum_ref[col, z] += mul_t(
-                        jnp.concatenate([back[:, spans[1]]] * 2, axis=1),
-                        jnp.concatenate([high[:, atoms:], low[:, atoms:]], axis=1),
-                    )
-                weight = moments(total, 0)
-                for comp, coord in enumerate((own_x, own_y, own_z[z])):
-                    value = coord[col : col + 1] * weight - moments(total, 1 + comp)
-                    forces[comp] = forces[comp] + value
-            for comp in range(3):
-                row = comp * brick.cols + col
-                force_ref[row : row + 1, :] = forces[comp]
+                cell = part[:, z * atoms : (z + 1) * atoms]
+                back_ref[col, other_z, z] = jnp.concatenate([cell, cell], axis=1)
+
+    total_ref[...] = jnp.zeros(total_ref.shape, F32)
+    cells = [(x, y) for x in range(brick.bx) for y in range(brick.by)]
+    mirrors = {(col, z): [] for col in range(brick.cols) for z in range(brick.bz)}
+
+    def block(place, z, col, own_z, mirrored=None):
+        span = slice(own_z * atoms, (own_z + 1) * atoms)
+        left = left_ref[place, z * atoms : (z + 1) * atoms, :]
+        high, low = pair_factor(left, right_ref[col, z, :, span])
+        total_ref[col, z, :, span] += mul(
+            source_ref[place, z], jnp.concatenate([high, low], axis=0)
+        )
+        if mirrored is not None:
+            spot = 2 * atoms * len(mirrors[(mirrored, z)])
+            mirrors[(mirrored, z)].append((col, own_z))
+            kept_ref[mirrored, z, :, spot : spot + atoms] = high
+            kept_ref[mirrored, z, :, spot + atoms : spot + 2 * atoms] = low
+
+    def visit(place, x, y):
+        inside = (x, y) in cells
+        for z in range(brick.bz):
+            for col, (cell_x, cell_y) in enumerate(cells):
+                if max(abs(cell_x - x), abs(cell_y - y)) > 1:
+                    continue
+                if not inside:
+                    for own_z in range(brick.bz):
+                        block(place, z, col, own_z)
+                elif col == brick.col(x, y):
+                    block(place, z, col, z)
+                    block(place, z, col, (z + 1) % brick.bz, col)
+                elif col < brick.col(x, y):
+                    for own_z in range(brick.bz):
+                        block(place, z, col, own_z, brick.col(x, y))
+
+    order = sorted(enumerate(brick.columns), key=lambda item: item[1] not in cells)
+    for place, (x, y) in order:
+        visit(place, x, y)
+    back_sums = {}
+    for (col, z), list_of in mirrors.items():
+        back = jnp.concatenate([back_ref[c, z, own_z] for c, own_z in list_of], axis=1)
+        back_sums[(col, z)] = mul_t(kept_ref[col, z, :, 0 : back.shape[1]], back).T
+
     for col in range(brick.cols):
-        total = jnp.concatenate([back_sum_ref[col, z] for z in range(brick.bz)], axis=1)
+        forces = [0.0, 0.0, 0.0]
+        for z in range(brick.bz):
+            total = total_ref[col, z]
+            weight = moments(total, 0)
+            for comp, coord in enumerate((own_x, own_y, own_z_coords[z])):
+                value = coord[col : col + 1] * weight - moments(total, 1 + comp)
+                forces[comp] = forces[comp] + value
+        total = jnp.concatenate([back_sums[(col, z)] for z in range(brick.bz)], axis=1)
         weight = moments(total, 0)
         home = (own[2] + (lane_z - half)) * SCALE
         for comp, coord in enumerate((own_x, own_y, home)):
             row = comp * brick.cols + col
             value = coord[col : col + 1] * weight - moments(total, 1 + comp)
-            value = value + force_ref[row : row + 1, :]
+            value = value + forces[comp]
             force_ref[row : row + 1, :] = value * (own[3][col : col + 1] * (SCALE * SCALE))
 
 
@@ -654,8 +659,9 @@
             pltpu.VMEM((n_col, brick.lanes, FEATURES), BF16),
             pltpu.VMEM((n_col, brick.bz, SOURCES, 2 * brick.atoms), BF16),
             pltpu.VMEM((brick.cols, brick.bz, FEATURES, brick.lanes), BF16),
-            pltpu.VMEM((brick.cols, brick.bz, SOURCES, 2 * brick.lanes), BF16),
-            pltpu.VMEM((brick.cols, brick.bz, SOURCES, brick.atoms), F32),
+            pltpu.VMEM((brick.cols, brick.bz, brick.bz, SOURCES, 2 * brick.atoms), BF16),
+            pltpu.VMEM((brick.cols, brick.bz, SOURCES, brick.lanes), F32),
+            pltpu.VMEM((brick.cols, brick.bz, brick.atoms, brick.kept), BF16),
         ],
         10**10,
         msg,

time: 41.2 us -> 36.4 us (0.88)
  Pallas kernels: 23.6 us -> 18.8 us
    pallas_call x3, Pallas kernels: 23.6 us -> 18.8 us  [call(): pl.pallas_call(kernel, out_shape=out_shape, in_specs=in_specs, out_specs=...]
  transfers between devices with their start and end apart: 6 -> 6, of which waited for: 1 -> 1; matrix products, arithmetic and copies ran while one was open for 0% -> 0% of each run, Pallas kernels for 44% -> 37%
where the time goes in v3:
time: 36.4 us; the launch traced here: 36.2 us
  Pallas kernels  18.8 us (52%)
  starting transfers between devices  13.9 us (38%)
  local copies, waits for them, and re-layouts  2.07 us (6%)
  waiting for transfers between devices  1.24 us (3%)
    pallas_call x3, Pallas kernels, call(): pl.pallas_call(kernel, out_shape=out_shape, in_specs=in_specs, out_specs=...  18.8 us
    ppermute x5, starting transfers between devices, neighbours(): msgs.append(lax.ppermute(msg, ('space', 'sub'), pairs))  8.4 us
    all_to_all x1, starting transfers between devices, body(): whole = lax.all_to_all(coarse, ('space', 'sub'), 0, 0, tiled=True)  5.48 us
    unnamed x12, local copies, waits for them, and re-layouts  1.45 us
    ppermute x5, waiting for transfers between devices, neighbours(): msgs.append(lax.ppermute(msg, ('space', 'sub'), pairs))  1.24 us
  transfers between devices with their start and end apart: 6, of which 1 were waited for; matrix products, arithmetic and copies ran while one was open for 0% of the time, Pallas kernels for 37%

profile of v3, /device:TPU:0, one launch (start us, length us, event | category | flops | bytes accessed | tf_op | source)
XLA Modules:
  0.0 36.2 jit_solution(10496499149977917579)
XLA Ops:
  0.0 0.7 %copy.9.charge_ref = f32[2,2,3,128]{3,2,1,0:T(4,128)S(1)} copy(f32[2,2,3,128]{3,1,2,0:T(2,128)} %param.8) | data formatting | bytes 12288 | tf_op args[1]
  0.7 0.0 copy-start.4
  0.7 0.7 %copy.8.pos_ref = f32[3,2,2,3,128]{4,3,2,1,0:T(4,128)S(1)} copy(f32[3,2,2,3,128]{4,2,3,1,0:T(2,128)} %param.7) | data formatting | bytes 36864 | tf_op args[0]
  1.4 0.0 copy-done.4
  1.4 2.0 %shard_map.73 = (f32[32,384]{1,0:T(8,128)S(1)}, f32[32,8,128]{2,1,0:T(8,128)}) custom-call(s32[2,2,3]{2,1,0:T(2,128)S(1)} %copy-done.4, f32[3,2,2,3,128]{4,3,2,1,0:T(4,128)S(1)} %copy.8.pos_ref, f32[2,2,3,128]{3,2,1,0:T(4,128)S(1)} %copy.9.charge_ref), custom_call_target="tpu_custom_call" | custom-call | flops 10000000 | bytes 100000 | tf_op jit(solution)/shard_map/pallas_call | solution.py:590
  3.5 5.4 %collective-permute-start.4 = (f32[32,384]{1,0:T(8,128)S(1)}, f32[32,384]{1,0:T(8,128)S(1)}, u32[]{:S(2)}, u32[]{:S(2)}) collective-permute-start(f32[32,384]{1,0:T(8,128)S(1)} %get-tuple-element.7.refs_0_.refs_1_), channel_id=1, source_target_pairs={{2,0},{3,1},{4,2},{5,3},{6,4},{7,5},{8,6},{9,7},{10,8},{11,9},{12,... | collective-permute-start | bytes 147464 | tf_op jit(solution)/shard_map/ppermute | solution.py:617
  8.9 1.6 %collective-permute-start.3 = (f32[32,384]{1,0:T(8,128)S(1)}, f32[32,384]{1,0:T(8,128)S(1)}, u32[]{:S(2)}, u32[]{:S(2)}) collective-permute-start(f32[32,384]{1,0:T(8,128)S(1)} %get-tuple-element.7.refs_0_.refs_1_), channel_id=1, source_target_pairs={{3,0},{2,1},{5,2},{4,3},{7,4},{6,5},{9,6},{8,7},{11,8},{10,9},{13,... | collective-permute-start | bytes 147464 | tf_op jit(solution)/shard_map/ppermute | solution.py:617
  10.5 0.5 %collective-permute-start.2 = (f32[32,384]{1,0:T(8,128)S(1)}, f32[32,384]{1,0:T(8,128)S(1)}, u32[]{:S(2)}, u32[]{:S(2)}) collective-permute-start(f32[32,384]{1,0:T(8,128)S(1)} %get-tuple-element.7.refs_0_.refs_1_), channel_id=1, source_target_pairs={{1,0},{0,1},{3,2},{2,3},{5,4},{4,5},{7,6},{6,7},{9,8},{8,9},{11,10... | collective-permute-start | bytes 147464 | tf_op jit(solution)/shard_map/ppermute | solution.py:617
  11.0 0.0 collective-permute-start.1
  11.0 0.8 %collective-permute-start = (f32[32,384]{1,0:T(8,128)S(1)}, f32[32,384]{1,0:T(8,128)S(1)}, u32[]{:S(2)}, u32[]{:S(2)}) collective-permute-start(f32[32,384]{1,0:T(8,128)S(1)} %get-tuple-element.7.refs_0_.refs_1_), channel_id=1, source_target_pairs={{31,0},{30,1},{1,2},{0,3},{3,4},{2,5},{5,6},{4,7},{7,8},{6,9},{9,1... | collective-permute-start | bytes 147464 | tf_op jit(solution)/shard_map/ppermute | solution.py:617
  11.9 5.5 %all-to-all-start = ((f32[32,8,128]{2,1,0:T(8,128)}), f32[32,8,128]{2,1,0:T(8,128)S(1)}, u32[]{:S(2)}, u32[]{:S(2)}) async-start(f32[32,8,128]{2,1,0:T(8,128)} %get-tuple-element.8), calls=%async_computation | async-start | bytes 262144 | tf_op jit(solution)/shard_map/all_to_all | solution.py:645
  17.3 0.1 pad_add_fusion.refs_0_
  17.4 0.0 copy-start
  17.4 0.0 copy-start.1
  17.4 0.0 copy-start.2
  17.4 0.0 copy-start.3
  17.4 0.0 collective-permute-done.4.refs_5_.refs_6_
  17.4 0.0 collective-permute-done.3.refs_4_.refs_5_
  17.5 0.0 collective-permute-done.2.refs_3_.refs_4_
  17.5 0.0 collective-permute-done.1.refs_2_.refs_3_
  17.5 1.2 %collective-permute-done.refs_1_.refs_2_ = f32[32,384]{1,0:T(8,128)S(1)} collective-permute-done((f32[32,384]{1,0:T(8,128)S(1)}, f32[32,384]{1,0:T(8,128)S(1)}, u32[]{:S(2)}, u32[]{:S(2)}) %collective-permute-start) | collective-permute-done | bytes 49184 | tf_op jit(solution)/shard_map/ppermute | solution.py:617
  18.7 13.4 %shard_map.74.refs_8_ = f32[16,384]{1,0:T(8,128)S(1)} custom-call(f32[32,384]{1,0:T(8,128)S(1)} %get-tuple-element.7.refs_0_.refs_1_, f32[32,384]{1,0:T(8,128)S(1)} %collective-permute-done.refs_1_.refs_2_, f32[32,384]{1,0:T(8,128)S(1)} %collective-permute-done.1.refs_2_.refs_3_, f32[32,384]{1,0:T(8,128)S(1)} %collective-permute-done.2.refs_3_.refs_4_, ...), custom_call_target="tpu_custom_call" | custom-call | flops 10000000000 | bytes 100000 | tf_op jit(solution)/shard_map/pallas_call | solution.py:590
  32.1 0.0 all-to-all-done
  32.1 0.0 copy-done
  32.1 0.0 copy-done.1
  32.1 0.0 copy-done.2
  32.1 0.0 copy-done.3
  32.2 3.4 %shard_map.75 = f32[3,2,2,3,128]{4,3,2,1,0:T(4,128)S(1)} custom-call(s32[2]{0:T(128)S(1)} %pad_add_fusion.refs_0_, f32[32,384]{1,0:T(8,128)S(1)} %get-tuple-element.7.refs_0_.refs_1_, f32[32,384]{1,0:T(8,128)S(1)} %collective-permute-done.refs_1_.refs_2_, f32[32,384]{1,0:T(8,128)S(1)} %collective-permute-done.1.refs_2_.refs_3_, ...), custom_call_target="tpu_custom_call" | custom-call | flops 100000000 | bytes 100000 | tf_op jit(solution)/shard_map/pallas_call | solution.py:590
  35.6 0.6 %copy.10 = f32[3,2,2,3,128]{4,2,3,1,0:T(2,128)} copy(f32[3,2,2,3,128]{4,3,2,1,0:T(4,128)S(1)} %shard_map.75) | data formatting | bytes 36864 | tf_op jit(solution)/shard_map/pallas_call | solution.py:590
Async XLA Ops:
  0.7 0.7 %copy-start.4 = (s32[2,2,3]{2,1,0:T(2,128)S(1)}, s32[2,2,3]{2,1,0:T(2,128)}, u32[]{:S(2)}) copy-start(s32[2,2,3]{2,1,0:T(2,128)} %counts_ref.1) | copy-start | bytes 148
  3.5 14.0 %collective-permute-start.4 = (f32[32,384]{1,0:T(8,128)S(1)}, f32[32,384]{1,0:T(8,128)S(1)}, u32[]{:S(2)}, u32[]{:S(2)}) collective-permute-start(f32[32,384]{1,0:T(8,128)S(1)} %get-tuple-element.7.refs_0_.refs_1_), channel_id=1, source_target_pairs={{2,0},{3,1},{4,2},{5,3},{6,4},{7,5},{8,6},{9,7},{10,8},{11,9},{12,... | collective-permute-start | bytes 147464 | tf_op jit(solution)/shard_map/ppermute | solution.py:617
  8.9 8.6 %collective-permute-start.3 = (f32[32,384]{1,0:T(8,128)S(1)}, f32[32,384]{1,0:T(8,128)S(1)}, u32[]{:S(2)}, u32[]{:S(2)}) collective-permute-start(f32[32,384]{1,0:T(8,128)S(1)} %get-tuple-element.7.refs_0_.refs_1_), channel_id=1, source_target_pairs={{3,0},{2,1},{5,2},{4,3},{7,4},{6,5},{9,6},{8,7},{11,8},{10,9},{13,... | collective-permute-start | bytes 147464 | tf_op jit(solution)/shard_map/ppermute | solution.py:617
  10.5 7.0 %collective-permute-start.2 = (f32[32,384]{1,0:T(8,128)S(1)}, f32[32,384]{1,0:T(8,128)S(1)}, u32[]{:S(2)}, u32[]{:S(2)}) collective-permute-start(f32[32,384]{1,0:T(8,128)S(1)} %get-tuple-element.7.refs_0_.refs_1_), channel_id=1, source_target_pairs={{1,0},{0,1},{3,2},{2,3},{5,4},{4,5},{7,6},{6,7},{9,8},{8,9},{11,10... | collective-permute-start | bytes 147464 | tf_op jit(solution)/shard_map/ppermute | solution.py:617
  11.0 6.5 %collective-permute-start.1 = (f32[32,384]{1,0:T(8,128)S(1)}, f32[32,384]{1,0:T(8,128)S(1)}, u32[]{:S(2)}, u32[]{:S(2)}) collective-permute-start(f32[32,384]{1,0:T(8,128)S(1)} %get-tuple-element.7.refs_0_.refs_1_), channel_id=1, source_target_pairs={{30,0},{31,1},{0,2},{1,3},{2,4},{3,5},{4,6},{5,7},{6,8},{7,9},{8,1... | collective-permute-start | bytes 147464 | tf_op jit(solution)/shard_map/ppermute | solution.py:617
  11.0 7.7 %collective-permute-start = (f32[32,384]{1,0:T(8,128)S(1)}, f32[32,384]{1,0:T(8,128)S(1)}, u32[]{:S(2)}, u32[]{:S(2)}) collective-permute-start(f32[32,384]{1,0:T(8,128)S(1)} %get-tuple-element.7.refs_0_.refs_1_), channel_id=1, source_target_pairs={{31,0},{30,1},{1,2},{0,3},{3,4},{2,5},{5,6},{4,7},{7,8},{6,9},{9,1... | collective-permute-start | bytes 147464 | tf_op jit(solution)/shard_map/ppermute | solution.py:617
  11.9 20.3 %all-to-all-start = ((f32[32,8,128]{2,1,0:T(8,128)}), f32[32,8,128]{2,1,0:T(8,128)S(1)}, u32[]{:S(2)}, u32[]{:S(2)}) async-start(f32[32,8,128]{2,1,0:T(8,128)} %get-tuple-element.8), calls=%async_computation | async-start | bytes 262144 | tf_op jit(solution)/shard_map/all_to_all | solution.py:645
  17.4 14.7 %copy-start = (bf16[176,912]{1,0:T(8,128)(2,1)S(1)}, bf16[176,912]{1,0:T(8,128)(2,1)}, u32[]{:S(2)}) copy-start(bf16[176,912]{1,0:T(8,128)(2,1)} %constant.19.clone.refs_10_) | copy-start | bytes 963076
  17.4 14.7 %copy-start.1 = (bf16[176,912]{1,0:T(8,128)(2,1)S(1)}, bf16[176,912]{1,0:T(8,128)(2,1)}, u32[]{:S(2)}) copy-start(bf16[176,912]{1,0:T(8,128)(2,1)} %constant.18.clone.refs_9_) | copy-start | bytes 963076
  17.4 14.7 %copy-start.2 = (f32[256,128]{1,0:T(8,128)S(1)}, f32[256,128]{1,0:T(8,128)}, u32[]{:S(2)}) copy-start(f32[256,128]{1,0:T(8,128)} %constant.17.clone.refs_12_) | copy-start | bytes 393220
  17.4 14.7 %copy-start.3 = (f32[128,256]{1,0:T(8,128)S(1)}, f32[128,256]{1,0:T(8,128)}, u32[]{:S(2)}) copy-start(f32[128,256]{1,0:T(8,128)} %constant.16.clone.refs_11_) | copy-start | bytes 393220

commit v4 on v3

--- a/solution.py
+++ b/solution.py
@@ -22,21 +22,14 @@
 COARSE_FRACTIONS = (8.0, 4.0)
 COARSE_WEIGHTS = (4.0, 2.0)
 
-DECAY = 0.114
-SMOOTH = (
-    0.004718840075751518,
-    0.06055603768478568,
-    0.019918877505712862,
-    0.1440338177504446,
-    0.014789349197372625,
-    0.14113616660836056,
-)
+DECAY = 0.11446730730706552
+LEAD = 0.13637726630426547
+SMOOTH = (1.0312317180277653, 0.44426879021665455, 0.1544174241571791, -0.004580112368867706)
 SCALE = math.sqrt(DECAY * math.log2(math.e))
-LEAD = SMOOTH[-1] / SCALE**3
-SHIFT = math.log2(LEAD) / (len(SMOOTH) - 1)
-MONIC = tuple(
-    coef / SCALE**3 / LEAD ** (power / (len(SMOOTH) - 1)) for power, coef in enumerate(SMOOTH)
-)
+STRETCH = (LEAD / SCALE**3) ** 0.2
+SHIFT = math.log2(STRETCH)
+QUARTIC = (SMOOTH[0] * STRETCH**2, SMOOTH[1] * STRETCH**4, SMOOTH[2] * STRETCH)
+LEVEL = SMOOTH[3] / SCALE**3
 HALF_CONST = 0.5 * (SHIFT - SCALE * SCALE * SOFT_SQUARE)
 
 FEATURES = 32
@@ -134,7 +127,19 @@
     return jnp.concatenate(parts, axis=1)
 
 
-def spread_kernel(brick, counts_ref, pos_ref, charge_ref, msg_ref, coarse_ref, grid_ref):
+def spread_kernel(brick, *refs):
+    inputs, (msg_ref, coarse_ref), held = refs[0:3], refs[3:5], refs[5:8]
+    grid_ref, arrived = refs[8:]
+    counts_ref, pos_ref, charge_ref = held
+    copies = [
+        pltpu.make_async_copy(source, target, arrived.at[number])
+        for number, (source, target) in enumerate(zip(inputs, held))
+    ]
+    for copy in copies:
+        copy.start()
+    grid_ref[...] = jnp.zeros(grid_ref.shape, F32)
+    for copy in copies:
+        copy.wait()
     atoms = brick.atoms
     lane = lax.broadcasted_iota(jnp.int32, (1, atoms), 1)
     for x in range(brick.bx):
@@ -144,11 +149,10 @@
                 span = slice(z * atoms, (z + 1) * atoms)
                 for comp in range(3):
                     row = comp * brick.cols + col
-                    msg_ref[row : row + 1, span] = pos_ref[comp, x, y, z : z + 1, :]
+                    msg_ref[row : row + 1, span] = pos_ref[comp, x, z, y : y + 1, :]
                 row = 3 * brick.cols + col
-                charge = charge_ref[x, y, z : z + 1, :]
+                charge = charge_ref[x, z, y : y + 1, :]
                 msg_ref[row : row + 1, span] = jnp.where(lane < counts_ref[x, y, z], charge, 0.0)
-    grid_ref[...] = jnp.zeros(grid_ref.shape, F32)
     for x in range(brick.bx):
         for y in range(brick.by):
             col = brick.col(x, y)
@@ -240,9 +244,8 @@
     power = mul(left, right)
     inverse = lax.rsqrt(SHIFT - power)
     base = jnp.exp2(power)
-    smooth = base + MONIC[4]
-    for coef in MONIC[3::-1]:
-        smooth = smooth * base + coef
+    square = base * base
+    smooth = ((square + QUARTIC[0]) * square + QUARTIC[1]) * (base + QUARTIC[2])
     factor = inverse * (inverse * inverse) - smooth
     high = factor.astype(BF16)
     low = (factor - high.astype(F32)).astype(BF16)
@@ -302,12 +305,15 @@
         feature_arrays(coords, minus_square(coords), (0, 1, 2, 0, 1, 0), False),
     )
     store_pieces(source_piece_ref, rows, source_arrays(coords, charge))
+    level_sums = {}
     for place in range(len(brick.columns)):
         feature = load_pieces(other_piece_ref, rows, place, FEATURES)
         left_ref[place] = feature.T.astype(BF16)
-        source = load_pieces(source_piece_ref, rows, place, SOURCES).astype(BF16)
+        source = load_pieces(source_piece_ref, rows, place, SOURCES)
         for z in range(brick.bz):
             part = source[:, z * atoms : (z + 1) * atoms]
+            level_sums[(place, z)] = -LEVEL * jnp.sum(part, axis=1, keepdims=True)
+            part = part.astype(BF16)
             source_ref[place, z] = jnp.concatenate([part, part], axis=1)
 
     rows = brick.own_rows
@@ -339,46 +345,47 @@
                 cell = part[:, z * atoms : (z + 1) * atoms]
                 back_ref[col, other_z, z] = jnp.concatenate([cell, cell], axis=1)
 
-    total_ref[...] = jnp.zeros(total_ref.shape, F32)
     cells = [(x, y) for x in range(brick.bx) for y in range(brick.by)]
+    tiles = []
+    for place, (x, y) in sorted(enumerate(brick.columns), key=lambda item: item[1] not in cells):
+        home = cells.index((x, y)) if (x, y) in cells else None
+        for z in range(brick.bz):
+            for col, (cell_x, cell_y) in enumerate(cells):
+                if max(abs(cell_x - x), abs(cell_y - y)) > 1 or (home is not None and col > home):
+                    continue
+                if col == home:
+                    tiles.append((place, z, col, z, None))
+                    tiles.append((place, z, col, (z + 1) % brick.bz, home))
+                else:
+                    tiles += [(place, z, col, own_z, home) for own_z in range(brick.bz)]
+
+    for col in range(brick.cols):
+        for z in range(brick.bz):
+            for own_z in range(brick.bz):
+                level = sum(
+                    level_sums[(tile[0], z)] for tile in tiles if tile[1:4] == (z, col, own_z)
+                )
+                span = slice(own_z * atoms, (own_z + 1) * atoms)
+                total_ref[col, z, :, span] = jnp.broadcast_to(level, (SOURCES, atoms))
+
     mirrors = {(col, z): [] for col in range(brick.cols) for z in range(brick.bz)}
-
-    def block(place, z, col, own_z, mirrored=None):
+    for place, z, col, own_z, home in tiles:
         span = slice(own_z * atoms, (own_z + 1) * atoms)
         left = left_ref[place, z * atoms : (z + 1) * atoms, :]
         high, low = pair_factor(left, right_ref[col, z, :, span])
         total_ref[col, z, :, span] += mul(
             source_ref[place, z], jnp.concatenate([high, low], axis=0)
         )
-        if mirrored is not None:
-            spot = 2 * atoms * len(mirrors[(mirrored, z)])
-            mirrors[(mirrored, z)].append((col, own_z))
-            kept_ref[mirrored, z, :, spot : spot + atoms] = high
-            kept_ref[mirrored, z, :, spot + atoms : spot + 2 * atoms] = low
-
-    def visit(place, x, y):
-        inside = (x, y) in cells
-        for z in range(brick.bz):
-            for col, (cell_x, cell_y) in enumerate(cells):
-                if max(abs(cell_x - x), abs(cell_y - y)) > 1:
-                    continue
-                if not inside:
-                    for own_z in range(brick.bz):
-                        block(place, z, col, own_z)
-                elif col == brick.col(x, y):
-                    block(place, z, col, z)
-                    block(place, z, col, (z + 1) % brick.bz, col)
-                elif col < brick.col(x, y):
-                    for own_z in range(brick.bz):
-                        block(place, z, col, own_z, brick.col(x, y))
-
-    order = sorted(enumerate(brick.columns), key=lambda item: item[1] not in cells)
-    for place, (x, y) in order:
-        visit(place, x, y)
+        if home is not None:
+            spot = 2 * atoms * len(mirrors[(home, z)])
+            mirrors[(home, z)].append((col, own_z))
+            kept_ref[home, z, :, spot : spot + atoms] = high
+            kept_ref[home, z, :, spot + atoms : spot + 2 * atoms] = low
     back_sums = {}
-    for (col, z), list_of in mirrors.items():
-        back = jnp.concatenate([back_ref[c, z, own_z] for c, own_z in list_of], axis=1)
-        back_sums[(col, z)] = mul_t(kept_ref[col, z, :, 0 : back.shape[1]], back).T
+    for (col, z), found in mirrors.items():
+        back = jnp.concatenate([back_ref[c, z, own_z] for c, own_z in found], axis=1)
+        level = (-0.5 * LEVEL) * jnp.sum(back.astype(F32), axis=1, keepdims=True)
+        back_sums[(col, z)] = mul_t(kept_ref[col, z, :, 0 : back.shape[1]], back).T + level
 
     for col in range(brick.cols):
         forces = [0.0, 0.0, 0.0]
@@ -578,20 +585,22 @@
                 row = comp * brick.cols + col
                 force = short_ref[row : row + 1, :] - POINTS * (rows[3] * force)
                 for z in range(brick.bz):
-                    out_ref[comp, x, y, z : z + 1, :] = force[:, z * atoms : (z + 1) * atoms]
+                    out_ref[comp, x, z, y : y + 1, :] = force[:, z * atoms : (z + 1) * atoms]
 
 
 VMEM = pl.BlockSpec(memory_space=pltpu.VMEM)
 SMEM = pl.BlockSpec(memory_space=pltpu.SMEM)
-
-
-def call(kernel, out_shape, in_specs, scratch, flops, *args):
+ANY = pl.BlockSpec(memory_space=pl.ANY)
+WHOLE = pl.BlockSpec()
+
+
+def call(kernel, out_shape, in_specs, scratch, flops, *args, out_spec=VMEM):
     single = not isinstance(out_shape, (list, tuple))
     return pl.pallas_call(
         kernel,
         out_shape=out_shape,
         in_specs=in_specs,
-        out_specs=VMEM if single else [VMEM] * len(out_shape),
+        out_specs=out_spec if single else [out_spec] * len(out_shape),
         scratch_shapes=scratch,
         compiler_params=pltpu.CompilerParams(vmem_limit_bytes=40 * 1024 * 1024),
         cost_estimate=pl.CostEstimate(flops=flops, bytes_accessed=10**5, transcendentals=0),
@@ -628,18 +637,24 @@
     coarse_z = coarse_table(brick)
     place = jnp.stack([lax.axis_index("space"), lax.axis_index("sub")]).astype(jnp.int32)
 
+    turned = (positions.transpose(0, 1, 3, 2, 4), charges.transpose(0, 2, 1, 3))
     msg, coarse = call(
         functools.partial(spread_kernel, brick),
         [
             jax.ShapeDtypeStruct((brick.msg_rows, brick.msg_lanes), F32),
             jax.ShapeDtypeStruct((n_dev, brick.coarse_rows, brick.coarse_lanes), F32),
         ],
-        [SMEM, VMEM, VMEM],
-        [pltpu.VMEM((brick.px, brick.py, 128), F32)],
+        [ANY, ANY, ANY],
+        [
+            pltpu.SMEM(counts.shape, jnp.int32),
+            pltpu.VMEM(turned[0].shape, F32),
+            pltpu.VMEM(turned[1].shape, F32),
+            pltpu.VMEM((brick.px, brick.py, 128), F32),
+            pltpu.SemaphoreType.DMA((3,)),
+        ],
         10**7,
         counts,
-        positions,
-        charges,
+        *turned,
     )
     sender, msgs = neighbours(brick, msg)
     whole = lax.all_to_all(coarse, ("space", "sub"), 0, 0, tiled=True)
@@ -669,9 +684,10 @@
     )
     ext_x = brick.px + 2 * REACH
     rows_y = brick.py + POINTS * brick.by
-    return call(
+    comps, size_x, size_y, size_z, atoms = positions.shape
+    forces = call(
         functools.partial(potential_kernel, brick, sender, len(msgs)),
-        jax.ShapeDtypeStruct(positions.shape, F32),
+        jax.ShapeDtypeStruct((comps, size_x, size_z, size_y, atoms), F32),
         [SMEM] + [VMEM] * (7 + len(msgs)),
         [
             pltpu.VMEM((ext_x * rows_y, 128), F32),
@@ -687,7 +703,9 @@
         xy_low,
         jnp.asarray(along_z),
         jnp.asarray(coarse_z),
-    )
+        out_spec=WHOLE,
+    )
+    return forces.transpose(0, 1, 3, 2, 4)
 
 
 def solution(mesh):

time: 36.4 us -> 35 us (0.962)
  Pallas kernels: 18.8 us -> 17.2 us
    pallas_call x3, Pallas kernels: 18.8 us -> 17.2 us  [call(): pl.pallas_call(kernel, out_shape=out_shape, in_specs=in_specs, out_specs=...]
    unnamed x12 -> x14, local copies, waits for them, and re-layouts: 1.45 us -> 2.11 us
    pallas_call x1 -> x0, local copies, waits for them, and re-layouts: 0.62 us -> none  [call(): pl.pallas_call(kernel, out_shape=out_shape, in_specs=in_specs, out_specs=...]
  transfers between devices with their start and end apart: 6 -> 6, of which waited for: 1 -> 1; matrix products, arithmetic and copies ran while one was open for 0% -> 0% of each run, Pallas kernels for 37% -> 32%
where the time goes in v4:
time: 35 us; the launch traced here: 34.7 us
  Pallas kernels  17.2 us (49%)
  starting transfers between devices  13.9 us (40%)
  local copies, waits for them, and re-layouts  2.11 us (6%)
  waiting for transfers between devices  1.24 us (4%)
    pallas_call x3, Pallas kernels, call(): pl.pallas_call(kernel, out_shape=out_shape, in_specs=in_specs, out_specs=...  17.2 us
    ppermute x5, starting transfers between devices, neighbours(): msgs.append(lax.ppermute(msg, ('space', 'sub'), pairs))  8.46 us
    all_to_all x1, starting transfers between devices, body(): whole = lax.all_to_all(coarse, ('space', 'sub'), 0, 0, tiled=True)  5.48 us
    unnamed x14, local copies, waits for them, and re-layouts  2.11 us
    ppermute x5, waiting for transfers between devices, neighbours(): msgs.append(lax.ppermute(msg, ('space', 'sub'), pairs))  1.24 us
  transfers between devices with their start and end apart: 6, of which 1 were waited for; matrix products, arithmetic and copies ran while one was open for 0% of the time, Pallas kernels for 32%

profile of v4, /device:TPU:0, one launch (start us, length us, event | category | flops | bytes accessed | tf_op | source)
XLA Modules:
  0.0 34.7 jit_solution(355606389738188235)
XLA Ops:
  0.0 0.0 copy-start.6
  0.0 0.7 %copy-done.6 = s32[2,2,3]{2,1,0:T(2,128)S(1)} copy-done((s32[2,2,3]{2,1,0:T(2,128)S(1)}, s32[2,2,3]{2,1,0:T(2,128)}, u32[]{:S(2)}) %copy-start.6) | copy-done | bytes 72
  0.7 0.0 copy-start.4
  0.7 0.7 %copy-done.4 = f32[3,2,2,3,128]{4,2,3,1,0:T(2,128)S(1)} copy-done((f32[3,2,2,3,128]{4,2,3,1,0:T(2,128)S(1)}, f32[3,2,2,3,128]{4,2,3,1,0:T(2,128)}, u32[]{:S(2)}) %copy-start.4) | copy-done | bytes 18456
  1.4 0.0 copy-start.5
  1.4 0.7 %copy-done.5 = f32[2,2,3,128]{3,1,2,0:T(2,128)S(1)} copy-done((f32[2,2,3,128]{3,1,2,0:T(2,128)S(1)}, f32[2,2,3,128]{3,1,2,0:T(2,128)}, u32[]{:S(2)}) %copy-start.5) | copy-done | bytes 6168
  2.1 2.0 %shard_map.73 = (f32[32,384]{1,0:T(8,128)S(1)}, f32[32,8,128]{2,1,0:T(8,128)}) custom-call(s32[2,2,3]{2,1,0:T(2,128)S(1)} %copy-done.6, f32[3,2,3,2,128]{4,3,2,1,0:T(2,128)S(1)} %bitcast.7, f32[2,3,2,128]{3,2,1,0:T(2,128)S(1)} %bitcast.8), custom_call_target="tpu_custom_call" | custom-call | flops 10000000 | bytes 100000 | tf_op jit(solution)/shard_map/pallas_call | solution.py:599
  4.1 5.5 %collective-permute-start.4 = (f32[32,384]{1,0:T(8,128)S(1)}, f32[32,384]{1,0:T(8,128)S(1)}, u32[]{:S(2)}, u32[]{:S(2)}) collective-permute-start(f32[32,384]{1,0:T(8,128)S(1)} %get-tuple-element.7.refs_0_.refs_1_), channel_id=1, source_target_pairs={{2,0},{3,1},{4,2},{5,3},{6,4},{7,5},{8,6},{9,7},{10,8},{11,9},{12,... | collective-permute-start | bytes 147464 | tf_op jit(solution)/shard_map/ppermute | solution.py:626
  9.6 1.6 %collective-permute-start.3 = (f32[32,384]{1,0:T(8,128)S(1)}, f32[32,384]{1,0:T(8,128)S(1)}, u32[]{:S(2)}, u32[]{:S(2)}) collective-permute-start(f32[32,384]{1,0:T(8,128)S(1)} %get-tuple-element.7.refs_0_.refs_1_), channel_id=1, source_target_pairs={{3,0},{2,1},{5,2},{4,3},{7,4},{6,5},{9,6},{8,7},{11,8},{10,9},{13,... | collective-permute-start | bytes 147464 | tf_op jit(solution)/shard_map/ppermute | solution.py:626
  11.2 0.5 %collective-permute-start.2 = (f32[32,384]{1,0:T(8,128)S(1)}, f32[32,384]{1,0:T(8,128)S(1)}, u32[]{:S(2)}, u32[]{:S(2)}) collective-permute-start(f32[32,384]{1,0:T(8,128)S(1)} %get-tuple-element.7.refs_0_.refs_1_), channel_id=1, source_target_pairs={{1,0},{0,1},{3,2},{2,3},{5,4},{4,5},{7,6},{6,7},{9,8},{8,9},{11,10... | collective-permute-start | bytes 147464 | tf_op jit(solution)/shard_map/ppermute | solution.py:626
  11.7 0.0 collective-permute-start.1
  11.7 0.8 %collective-permute-start = (f32[32,384]{1,0:T(8,128)S(1)}, f32[32,384]{1,0:T(8,128)S(1)}, u32[]{:S(2)}, u32[]{:S(2)}) collective-permute-start(f32[32,384]{1,0:T(8,128)S(1)} %get-tuple-element.7.refs_0_.refs_1_), channel_id=1, source_target_pairs={{31,0},{30,1},{1,2},{0,3},{3,4},{2,5},{5,6},{4,7},{7,8},{6,9},{9,1... | collective-permute-start | bytes 147464 | tf_op jit(solution)/shard_map/ppermute | solution.py:626
  12.6 5.5 %all-to-all-start = ((f32[32,8,128]{2,1,0:T(8,128)}), f32[32,8,128]{2,1,0:T(8,128)S(1)}, u32[]{:S(2)}, u32[]{:S(2)}) async-start(f32[32,8,128]{2,1,0:T(8,128)} %get-tuple-element.8), calls=%async_computation | async-start | bytes 262144 | tf_op jit(solution)/shard_map/all_to_all | solution.py:660
  18.1 0.1 pad_add_fusion.refs_0_
  18.2 0.0 copy-start
  18.2 0.0 copy-start.1
  18.2 0.0 copy-start.2
  18.2 0.0 copy-start.3
  18.2 0.0 collective-permute-done.4.refs_5_.refs_6_
  18.2 0.0 collective-permute-done.3.refs_4_.refs_5_
  18.2 0.0 collective-permute-done.2.refs_3_.refs_4_
  18.2 0.0 collective-permute-done.1.refs_2_.refs_3_
  18.2 1.2 %collective-permute-done.refs_1_.refs_2_ = f32[32,384]{1,0:T(8,128)S(1)} collective-permute-done((f32[32,384]{1,0:T(8,128)S(1)}, f32[32,384]{1,0:T(8,128)S(1)}, u32[]{:S(2)}, u32[]{:S(2)}) %collective-permute-start) | collective-permute-done | bytes 49184 | tf_op jit(solution)/shard_map/ppermute | solution.py:626
  19.4 11.2 %shard_map.74.refs_8_ = f32[16,384]{1,0:T(8,128)S(1)} custom-call(f32[32,384]{1,0:T(8,128)S(1)} %get-tuple-element.7.refs_0_.refs_1_, f32[32,384]{1,0:T(8,128)S(1)} %collective-permute-done.refs_1_.refs_2_, f32[32,384]{1,0:T(8,128)S(1)} %collective-permute-done.1.refs_2_.refs_3_, f32[32,384]{1,0:T(8,128)S(1)} %collective-permute-done.2.refs_3_.refs_4_, ...), custom_call_target="tpu_custom_call" | custom-call | flops 10000000000 | bytes 100000 | tf_op jit(solution)/shard_map/pallas_call | solution.py:599
  30.6 0.0 all-to-all-done
  30.7 0.0 copy-done
  30.7 0.0 copy-done.1
  30.7 0.0 copy-done.2
  30.7 0.0 copy-done.3
  30.7 4.0 %shard_map.75 = f32[3,2,3,2,128]{4,3,2,1,0:T(2,128)} custom-call(s32[2]{0:T(128)S(1)} %pad_add_fusion.refs_0_, f32[32,384]{1,0:T(8,128)S(1)} %get-tuple-element.7.refs_0_.refs_1_, f32[32,384]{1,0:T(8,128)S(1)} %collective-permute-done.refs_1_.refs_2_, f32[32,384]{1,0:T(8,128)S(1)} %collective-permute-done.1.refs_2_.refs_3_, ...), custom_call_target="tpu_custom_call" | custom-call | flops 100000000 | bytes 100000 | tf_op jit(solution)/shard_map/pallas_call | solution.py:599
Async XLA Ops:
  0.0 0.7 %copy-start.6 = (s32[2,2,3]{2,1,0:T(2,128)S(1)}, s32[2,2,3]{2,1,0:T(2,128)}, u32[]{:S(2)}) copy-start(s32[2,2,3]{2,1,0:T(2,128)} %refs_0_.1) | copy-start | bytes 148
  0.7 0.7 %copy-start.4 = (f32[3,2,2,3,128]{4,2,3,1,0:T(2,128)S(1)}, f32[3,2,2,3,128]{4,2,3,1,0:T(2,128)}, u32[]{:S(2)}) copy-start(f32[3,2,2,3,128]{4,2,3,1,0:T(2,128)} %param.7) | copy-start | bytes 55300
  1.4 0.7 %copy-start.5 = (f32[2,2,3,128]{3,1,2,0:T(2,128)S(1)}, f32[2,2,3,128]{3,1,2,0:T(2,128)}, u32[]{:S(2)}) copy-start(f32[2,2,3,128]{3,1,2,0:T(2,128)} %param.8) | copy-start | bytes 18436
  4.1 14.0 %collective-permute-start.4 = (f32[32,384]{1,0:T(8,128)S(1)}, f32[32,384]{1,0:T(8,128)S(1)}, u32[]{:S(2)}, u32[]{:S(2)}) collective-permute-start(f32[32,384]{1,0:T(8,128)S(1)} %get-tuple-element.7.refs_0_.refs_1_), channel_id=1, source_target_pairs={{2,0},{3,1},{4,2},{5,3},{6,4},{7,5},{8,6},{9,7},{10,8},{11,9},{12,... | collective-permute-start | bytes 147464 | tf_op jit(solution)/shard_map/ppermute | solution.py:626
  9.6 8.6 %collective-permute-start.3 = (f32[32,384]{1,0:T(8,128)S(1)}, f32[32,384]{1,0:T(8,128)S(1)}, u32[]{:S(2)}, u32[]{:S(2)}) collective-permute-start(f32[32,384]{1,0:T(8,128)S(1)} %get-tuple-element.7.refs_0_.refs_1_), channel_id=1, source_target_pairs={{3,0},{2,1},{5,2},{4,3},{7,4},{6,5},{9,6},{8,7},{11,8},{10,9},{13,... | collective-permute-start | bytes 147464 | tf_op jit(solution)/shard_map/ppermute | solution.py:626
  11.2 7.0 %collective-permute-start.2 = (f32[32,384]{1,0:T(8,128)S(1)}, f32[32,384]{1,0:T(8,128)S(1)}, u32[]{:S(2)}, u32[]{:S(2)}) collective-permute-start(f32[32,384]{1,0:T(8,128)S(1)} %get-tuple-element.7.refs_0_.refs_1_), channel_id=1, source_target_pairs={{1,0},{0,1},{3,2},{2,3},{5,4},{4,5},{7,6},{6,7},{9,8},{8,9},{11,10... | collective-permute-start | bytes 147464 | tf_op jit(solution)/shard_map/ppermute | solution.py:626
  11.7 6.5 %collective-permute-start.1 = (f32[32,384]{1,0:T(8,128)S(1)}, f32[32,384]{1,0:T(8,128)S(1)}, u32[]{:S(2)}, u32[]{:S(2)}) collective-permute-start(f32[32,384]{1,0:T(8,128)S(1)} %get-tuple-element.7.refs_0_.refs_1_), channel_id=1, source_target_pairs={{30,0},{31,1},{0,2},{1,3},{2,4},{3,5},{4,6},{5,7},{6,8},{7,9},{8,1... | collective-permute-start | bytes 147464 | tf_op jit(solution)/shard_map/ppermute | solution.py:626
  11.7 7.7 %collective-permute-start = (f32[32,384]{1,0:T(8,128)S(1)}, f32[32,384]{1,0:T(8,128)S(1)}, u32[]{:S(2)}, u32[]{:S(2)}) collective-permute-start(f32[32,384]{1,0:T(8,128)S(1)} %get-tuple-element.7.refs_0_.refs_1_), channel_id=1, source_target_pairs={{31,0},{30,1},{1,2},{0,3},{3,4},{2,5},{5,6},{4,7},{7,8},{6,9},{9,1... | collective-permute-start | bytes 147464 | tf_op jit(solution)/shard_map/ppermute | solution.py:626
  12.6 18.1 %all-to-all-start = ((f32[32,8,128]{2,1,0:T(8,128)}), f32[32,8,128]{2,1,0:T(8,128)S(1)}, u32[]{:S(2)}, u32[]{:S(2)}) async-start(f32[32,8,128]{2,1,0:T(8,128)} %get-tuple-element.8), calls=%async_computation | async-start | bytes 262144 | tf_op jit(solution)/shard_map/all_to_all | solution.py:660
  18.2 12.5 %copy-start = (bf16[176,912]{1,0:T(8,128)(2,1)S(1)}, bf16[176,912]{1,0:T(8,128)(2,1)}, u32[]{:S(2)}) copy-start(bf16[176,912]{1,0:T(8,128)(2,1)} %constant.19.clone.refs_10_) | copy-start | bytes 963076
  18.2 12.5 %copy-start.1 = (bf16[176,912]{1,0:T(8,128)(2,1)S(1)}, bf16[176,912]{1,0:T(8,128)(2,1)}, u32[]{:S(2)}) copy-start(bf16[176,912]{1,0:T(8,128)(2,1)} %constant.18.clone.refs_9_) | copy-start | bytes 963076
  18.2 12.5 %copy-start.2 = (f32[256,128]{1,0:T(8,128)S(1)}, f32[256,128]{1,0:T(8,128)}, u32[]{:S(2)}) copy-start(f32[256,128]{1,0:T(8,128)} %constant.17.clone.refs_12_) | copy-start | bytes 393220
  18.2 12.5 %copy-start.3 = (f32[128,256]{1,0:T(8,128)S(1)}, f32[128,256]{1,0:T(8,128)}, u32[]{:S(2)}) copy-start(f32[128,256]{1,0:T(8,128)} %constant.16.clone.refs_11_) | copy-start | bytes 393220

commit v5 on v4

--- a/solution.py
+++ b/solution.py
@@ -259,9 +259,9 @@
 
 def pairs_kernel(brick, sender, n_msgs, *refs):
     atoms, lanes = brick.atoms, brick.lanes
-    msg_ref = refs[0]
-    other_msgs = refs[1 : 1 + n_msgs]
-    force_ref = refs[1 + n_msgs]
+    place_ref, msg_ref = refs[0:2]
+    other_msgs = refs[2 : 2 + n_msgs]
+    force_ref = refs[2 + n_msgs]
     (
         row_ref,
         other_piece_ref,
@@ -274,7 +274,8 @@
         back_ref,
         total_ref,
         kept_ref,
-    ) = refs[2 + n_msgs :]
+    ) = refs[3 + n_msgs :]
+    even = place_ref[0] % 2 == 0
     half = 0.5 * brick.bz
 
     rows = brick.ext_rows
@@ -282,12 +283,14 @@
         row_ref[...] = jnp.zeros(row_ref.shape, F32)
     for place, (x, y) in enumerate(brick.columns):
         shift = (x // brick.bx, y // brick.by)
-        near = msg_ref if shift == (0, 0) else other_msgs[sender[shift]]
         col = brick.col(x % brick.bx, y % brick.by)
         for k in range(4):
-            row_ref[k * rows + place : k * rows + place + 1, :] = near[
-                k * brick.cols + col : k * brick.cols + col + 1, 0:lanes
-            ]
+            near = slice(k * brick.cols + col, k * brick.cols + col + 1)
+            if shift == (0, 0):
+                value = msg_ref[near, 0:lanes]
+            else:
+                value = near_rows(other_msgs, sender[shift], even, near, slice(0, lanes))
+            row_ref[k * rows + place : k * rows + place + 1, :] = value
     index = lax.broadcasted_iota(jnp.int32, (rows, 1), 0)
     ext_y = brick.by + 2
     offset_x = (index // ext_y - 1).astype(F32) - 0.5 * brick.bx
@@ -469,6 +472,7 @@
         ext_ref,
         pot_ref,
     ) = refs[2 + n_msgs :]
+    even = place_ref[0] % 2 == 0
     step_y = POINTS * brick.by
     rows_y = brick.py + step_y
     ext_x = brick.px + 2 * REACH
@@ -476,8 +480,12 @@
     for dx in (-1, 0, 1):
         grids = []
         for dy in (-1, 0, 1):
-            source = msg_ref if (dx, dy) == (0, 0) else other_msgs[sender[(dx, dy)]]
-            grids.append(source[brick.grid_row :, 0 : brick.blocks * 128])
+            near = slice(brick.grid_row, brick.msg_rows)
+            span = slice(0, brick.blocks * 128)
+            if (dx, dy) == (0, 0):
+                grids.append(msg_ref[near, span])
+            else:
+                grids.append(near_rows(other_msgs, sender[(dx, dy)], even, near, span))
         full = brick.py + 2 * step_y
         tiles = [None] * (full // 8)
         for number, grid in enumerate(grids):
@@ -594,7 +602,7 @@
 WHOLE = pl.BlockSpec()
 
 
-def call(kernel, out_shape, in_specs, scratch, flops, *args, out_spec=VMEM):
+def call(kernel, out_shape, in_specs, scratch, flops, *args, out_spec=VMEM, grant=40):
     single = not isinstance(out_shape, (list, tuple))
     return pl.pallas_call(
         kernel,
@@ -602,30 +610,47 @@
         in_specs=in_specs,
         out_specs=out_spec if single else [out_spec] * len(out_shape),
         scratch_shapes=scratch,
-        compiler_params=pltpu.CompilerParams(vmem_limit_bytes=40 * 1024 * 1024),
+        compiler_params=pltpu.CompilerParams(vmem_limit_bytes=grant * 1024 * 1024),
         cost_estimate=pl.CostEstimate(flops=flops, bytes_accessed=10**5, transcendentals=0),
     )(*args)
 
 
 def neighbours(brick, msg):
+    size, wide = brick.n_space, brick.n_sub
+    pairings = {
+        0: lambda i: i,
+        1: lambda i: i ^ 1,
+        2: lambda i: (((i + 1) % size ^ 1) - 1) % size,
+    }
     found = {}
     sender = {}
     msgs = []
-    for dx in (-1, 0, 1):
-        for dy in (-1, 0, 1):
+    for dx in (0, -1, 1):
+        for dy in (0, -1, 1):
             if (dx, dy) == (0, 0):
                 continue
-            key = (dx % brick.n_space, dy % brick.n_sub)
-            if key not in found:
-                found[key] = len(msgs)
-                pairs = []
-                for i in range(brick.n_space):
-                    for j in range(brick.n_sub):
-                        source = (i + dx) % brick.n_space * brick.n_sub + (j + dy) % brick.n_sub
-                        pairs.append((source, i * brick.n_sub + j))
-                msgs.append(lax.ppermute(msg, ("space", "sub"), pairs))
-            sender[(dx, dy)] = found[key]
+            numbers = []
+            for parity in (0, 1):
+                pairing = 0 if dx == 0 else 1 if (dx == 1) == (parity == 0) else 2
+                key = (pairing, dy % wide)
+                if key not in found:
+                    found[key] = len(msgs)
+                    pairs = [
+                        (pairings[pairing](i) * wide + (j + dy) % wide, i * wide + j)
+                        for i in range(size)
+                        for j in range(wide)
+                    ]
+                    msgs.append(lax.ppermute(msg, ("space", "sub"), pairs))
+                numbers.append(found[key])
+            sender[(dx, dy)] = tuple(numbers)
     return sender, msgs
+
+
+def near_rows(msgs, numbers, even, rows, span):
+    first = msgs[numbers[0]][rows, span]
+    if numbers[0] == numbers[1]:
+        return first
+    return jnp.where(even, first, msgs[numbers[1]][rows, span])
 
 
 def body(n_space, n_sub, positions, charges, counts):
@@ -655,6 +680,7 @@
         10**7,
         counts,
         *turned,
+        grant=64,
     )
     sender, msgs = neighbours(brick, msg)
     whole = lax.all_to_all(coarse, ("space", "sub"), 0, 0, tiled=True)
@@ -664,7 +690,7 @@
     short = call(
         functools.partial(pairs_kernel, brick, sender, len(msgs)),
         jax.ShapeDtypeStruct((brick.force_rows, brick.lanes), F32),
-        [VMEM] * (1 + len(msgs)),
+        [SMEM] + [VMEM] * (1 + len(msgs)),
         [
             pltpu.VMEM((4 * brick.ext_rows, brick.lanes), F32),
             pltpu.VMEM((brick.lanes // 128, FEATURES * brick.ext_rows, 128), F32),
@@ -679,6 +705,7 @@
             pltpu.VMEM((brick.cols, brick.bz, brick.atoms, brick.kept), BF16),
         ],
         10**10,
+        place,
         msg,
         *msgs,
     )

time: 35 us -> 32 us (0.914)
  local copies, waits for them, and re-layouts: 2.11 us -> 0.02 us
  waiting for transfers between devices: 1.24 us -> 0.25 us
  Pallas kernels: 17.2 us -> 18 us
  starting transfers between devices: 13.9 us -> 13.3 us
    unnamed x14 -> x10, local copies, waits for them, and re-layouts: 2.11 us -> 0.02 us
    all_to_all x1, starting transfers between devices: 5.48 us -> 3.88 us  [body(): whole = lax.all_to_all(coarse, ('space', 'sub'), 0, 0, tiled=True)]
    ppermute x5, waiting for transfers between devices: 1.24 us -> 0.25 us  [neighbours(): msgs.append(lax.ppermute(msg, ('space', 'sub'), pairs))]
    ppermute x5, starting transfers between devices: 8.46 us -> 9.39 us  [neighbours(): msgs.append(lax.ppermute(msg, ('space', 'sub'), pairs))]
    pallas_call x3, Pallas kernels: 17.2 us -> 18 us  [call(): pl.pallas_call(kernel, out_shape=out_shape, in_specs=in_specs, out_specs=...]
  transfers between devices with their start and end apart: 6 -> 6, of which waited for: 1 -> 1; matrix products, arithmetic and copies ran while one was open for 0% -> 0% of each run, Pallas kernels for 32% -> 37%
where the time goes in v5:
time: 32 us; the launch traced here: 31.7 us
  Pallas kernels  18 us (56%)
  starting transfers between devices  13.3 us (42%)
    pallas_call x3, Pallas kernels, call(): pl.pallas_call(kernel, out_shape=out_shape, in_specs=in_specs, out_specs=...  18 us
    ppermute x5, starting transfers between devices, neighbours(): msgs.append(lax.ppermute(msg, ('space', 'sub'), pairs))  9.39 us
    all_to_all x1, starting transfers between devices, body(): whole = lax.all_to_all(coarse, ('space', 'sub'), 0, 0, tiled=True)  3.88 us
  transfers between devices with their start and end apart: 6, of which 1 were waited for; matrix products, arithmetic and copies ran while one was open for 0% of the time, Pallas kernels for 37%

profile of v5, /device:TPU:0, one launch (start us, length us, event | category | flops | bytes accessed | tf_op | source)
XLA Modules:
  0.0 31.7 jit_solution(14020602319862755543)
XLA Ops:
  0.0 2.2 %shard_map.73 = (f32[32,384]{1,0:T(8,128)}, f32[32,8,128]{2,1,0:T(8,128)}) custom-call(s32[2,2,3]{2,1,0:T(2,128)} %refs_0_.1, f32[3,2,3,2,128]{4,3,2,1,0:T(2,128)} %bitcast.7, f32[2,3,2,128]{3,2,1,0:T(2,128)} %bitcast.8), custom_call_target="tpu_custom_call" | custom-call | flops 10000000 | bytes 100000 | tf_op jit(solution)/shard_map/pallas_call | solution.py:607
  2.2 2.5 %collective-permute-start.4 = (f32[32,384]{1,0:T(8,128)}, f32[32,384]{1,0:T(8,128)S(1)}, u32[]{:S(2)}, u32[]{:S(2)}) collective-permute-start(f32[32,384]{1,0:T(8,128)} %get-tuple-element.7.refs_1_), channel_id=1, source_target_pairs={{3,0},{2,1},{1,2},{0,3},{7,4},{6,5},{5,6},{4,7},{11,8},{10,9},{9,1... | collective-permute-start | bytes 147464 | tf_op jit(solution)/shard_map/ppermute | solution.py:643
  4.7 4.8 %collective-permute-start.3 = (f32[32,384]{1,0:T(8,128)}, f32[32,384]{1,0:T(8,128)S(1)}, u32[]{:S(2)}, u32[]{:S(2)}) collective-permute-start(f32[32,384]{1,0:T(8,128)} %get-tuple-element.7.refs_1_), channel_id=1, source_target_pairs={{31,0},{30,1},{5,2},{4,3},{3,4},{2,5},{9,6},{8,7},{7,8},{6,9},{13,... | collective-permute-start | bytes 147464 | tf_op jit(solution)/shard_map/ppermute | solution.py:643
  9.4 0.0 collective-permute-start.2
  9.4 0.6 %collective-permute-start.1 = (f32[32,384]{1,0:T(8,128)}, f32[32,384]{1,0:T(8,128)S(1)}, u32[]{:S(2)}, u32[]{:S(2)}) collective-permute-start(f32[32,384]{1,0:T(8,128)} %get-tuple-element.7.refs_1_), channel_id=1, source_target_pairs={{30,0},{31,1},{4,2},{5,3},{2,4},{3,5},{8,6},{9,7},{6,8},{7,9},{12,... | collective-permute-start | bytes 147464 | tf_op jit(solution)/shard_map/ppermute | solution.py:643
  10.1 1.5 %collective-permute-start = (f32[32,384]{1,0:T(8,128)}, f32[32,384]{1,0:T(8,128)S(1)}, u32[]{:S(2)}, u32[]{:S(2)}) collective-permute-start(f32[32,384]{1,0:T(8,128)} %get-tuple-element.7.refs_1_), channel_id=1, source_target_pairs={{1,0},{0,1},{3,2},{2,3},{5,4},{4,5},{7,6},{6,7},{9,8},{8,9},{11,10... | collective-permute-start | bytes 147464 | tf_op jit(solution)/shard_map/ppermute | solution.py:643
  11.6 0.0 copy-start.4
  11.6 3.9 %all-to-all-start = ((f32[32,8,128]{2,1,0:T(8,128)}), f32[32,8,128]{2,1,0:T(8,128)S(1)}, u32[]{:S(2)}, u32[]{:S(2)}) async-start(f32[32,8,128]{2,1,0:T(8,128)} %get-tuple-element.8), calls=%async_computation | async-start | bytes 262144 | tf_op jit(solution)/shard_map/all_to_all | solution.py:686
  15.5 0.1 pad_add_fusion.refs_0_
  15.6 0.0 copy-start
  15.6 0.0 copy-start.1
  15.6 0.0 copy-start.2
  15.6 0.0 copy-start.3
  15.6 0.0 collective-permute-done.4.refs_6_
  15.6 0.0 collective-permute-done.3.refs_5_
  15.6 0.0 collective-permute-done.2.refs_4_
  15.6 0.2 collective-permute-done.1.refs_3_
  15.8 0.0 collective-permute-done.refs_2_
  15.8 0.0 copy-done.4
  15.8 11.8 %shard_map.74.refs_8_ = f32[16,384]{1,0:T(8,128)S(1)} custom-call(s32[2]{0:T(128)S(1)} %pad_add_fusion.refs_0_, f32[32,384]{1,0:T(8,128)S(1)} %copy-done.4, f32[32,384]{1,0:T(8,128)S(1)} %collective-permute-done.refs_2_, f32[32,384]{1,0:T(8,128)S(1)} %collective-permute-done.1.refs_3_, f32[32,384]{1,0:T(8,128)S(1)} %collective-permute-done.2.refs_4_, ...), custom_call_target="tpu_custom_call" | custom-call | flops 10000000000 | bytes 100000 | tf_op jit(solution)/shard_map/pallas_call | solution.py:607
  27.6 0.0 all-to-all-done
  27.7 0.0 copy-done
  27.7 0.0 copy-done.1
  27.7 0.0 copy-done.2
  27.7 0.0 copy-done.3
  27.7 4.0 %shard_map.75 = f32[3,2,3,2,128]{4,3,2,1,0:T(2,128)} custom-call(s32[2]{0:T(128)S(1)} %pad_add_fusion.refs_0_, f32[32,384]{1,0:T(8,128)S(1)} %copy-done.4, f32[32,384]{1,0:T(8,128)S(1)} %collective-permute-done.refs_2_, f32[32,384]{1,0:T(8,128)S(1)} %collective-permute-done.1.refs_3_, f32[32,384]{1,0:T(8,128)S(1)} %collective-permute-done.2.refs_4_, ...), custom_call_target="tpu_custom_call" | custom-call | flops 100000000 | bytes 100000 | tf_op jit(solution)/shard_map/pallas_call | solution.py:607
Async XLA Ops:
  2.2 13.4 %collective-permute-start.4 = (f32[32,384]{1,0:T(8,128)}, f32[32,384]{1,0:T(8,128)S(1)}, u32[]{:S(2)}, u32[]{:S(2)}) collective-permute-start(f32[32,384]{1,0:T(8,128)} %get-tuple-element.7.refs_1_), channel_id=1, source_target_pairs={{3,0},{2,1},{1,2},{0,3},{7,4},{6,5},{5,6},{4,7},{11,8},{10,9},{9,1... | collective-permute-start | bytes 147464 | tf_op jit(solution)/shard_map/ppermute | solution.py:643
  4.7 10.9 %collective-permute-start.3 = (f32[32,384]{1,0:T(8,128)}, f32[32,384]{1,0:T(8,128)S(1)}, u32[]{:S(2)}, u32[]{:S(2)}) collective-permute-start(f32[32,384]{1,0:T(8,128)} %get-tuple-element.7.refs_1_), channel_id=1, source_target_pairs={{31,0},{30,1},{5,2},{4,3},{3,4},{2,5},{9,6},{8,7},{7,8},{6,9},{13,... | collective-permute-start | bytes 147464 | tf_op jit(solution)/shard_map/ppermute | solution.py:643
  9.4 6.2 %collective-permute-start.2 = (f32[32,384]{1,0:T(8,128)}, f32[32,384]{1,0:T(8,128)S(1)}, u32[]{:S(2)}, u32[]{:S(2)}) collective-permute-start(f32[32,384]{1,0:T(8,128)} %get-tuple-element.7.refs_1_), channel_id=1, source_target_pairs={{2,0},{3,1},{0,2},{1,3},{6,4},{7,5},{4,6},{5,7},{10,8},{11,9},{8,1... | collective-permute-start | bytes 147464 | tf_op jit(solution)/shard_map/ppermute | solution.py:643
  9.4 6.4 %collective-permute-start.1 = (f32[32,384]{1,0:T(8,128)}, f32[32,384]{1,0:T(8,128)S(1)}, u32[]{:S(2)}, u32[]{:S(2)}) collective-permute-start(f32[32,384]{1,0:T(8,128)} %get-tuple-element.7.refs_1_), channel_id=1, source_target_pairs={{30,0},{31,1},{4,2},{5,3},{2,4},{3,5},{8,6},{9,7},{6,8},{7,9},{12,... | collective-permute-start | bytes 147464 | tf_op jit(solution)/shard_map/ppermute | solution.py:643
  10.1 5.8 %collective-permute-start = (f32[32,384]{1,0:T(8,128)}, f32[32,384]{1,0:T(8,128)S(1)}, u32[]{:S(2)}, u32[]{:S(2)}) collective-permute-start(f32[32,384]{1,0:T(8,128)} %get-tuple-element.7.refs_1_), channel_id=1, source_target_pairs={{1,0},{0,1},{3,2},{2,3},{5,4},{4,5},{7,6},{6,7},{9,8},{8,9},{11,10... | collective-permute-start | bytes 147464 | tf_op jit(solution)/shard_map/ppermute | solution.py:643
  11.6 4.3 %copy-start.4 = (f32[32,384]{1,0:T(8,128)S(1)}, f32[32,384]{1,0:T(8,128)}, u32[]{:S(2)}) copy-start(f32[32,384]{1,0:T(8,128)} %get-tuple-element.7.refs_1_) | copy-start | bytes 147460
  11.6 16.1 %all-to-all-start = ((f32[32,8,128]{2,1,0:T(8,128)}), f32[32,8,128]{2,1,0:T(8,128)S(1)}, u32[]{:S(2)}, u32[]{:S(2)}) async-start(f32[32,8,128]{2,1,0:T(8,128)} %get-tuple-element.8), calls=%async_computation | async-start | bytes 262144 | tf_op jit(solution)/shard_map/all_to_all | solution.py:686
  15.6 12.1 %copy-start = (bf16[176,912]{1,0:T(8,128)(2,1)S(1)}, bf16[176,912]{1,0:T(8,128)(2,1)}, u32[]{:S(2)}) copy-start(bf16[176,912]{1,0:T(8,128)(2,1)} %constant.19.clone.refs_10_) | copy-start | bytes 963076
  15.6 12.1 %copy-start.1 = (bf16[176,912]{1,0:T(8,128)(2,1)S(1)}, bf16[176,912]{1,0:T(8,128)(2,1)}, u32[]{:S(2)}) copy-start(bf16[176,912]{1,0:T(8,128)(2,1)} %constant.18.clone.refs_9_) | copy-start | bytes 963076
  15.6 12.1 %copy-start.2 = (f32[256,128]{1,0:T(8,128)S(1)}, f32[256,128]{1,0:T(8,128)}, u32[]{:S(2)}) copy-start(f32[256,128]{1,0:T(8,128)} %constant.17.clone.refs_12_) | copy-start | bytes 393220
  15.6 12.1 %copy-start.3 = (f32[128,256]{1,0:T(8,128)S(1)}, f32[128,256]{1,0:T(8,128)}, u32[]{:S(2)}) copy-start(f32[128,256]{1,0:T(8,128)} %constant.16.clone.refs_11_) | copy-start | bytes 393220

commit v6 on v5

--- a/solution.py
+++ b/solution.py
@@ -166,7 +166,13 @@
             outer = jnp.concatenate(
                 [along_x[e : e + 1, :] * along_y for e in range(TAPS)], axis=0
             )
-            box = mul_t(outer, along_z, HIGHEST)
+            count = outer.shape[0]
+            outer = jnp.concatenate(split(outer, 2), axis=0).astype(BF16)
+            table = jnp.concatenate(split(along_z, 2), axis=0).astype(BF16)
+            box = mul_t(outer, table)
+            box = (
+                box[:count, : brick.zpad] + box[:count, brick.zpad :] + box[count:, : brick.zpad]
+            )
             for e in range(TAPS):
                 place = (POINTS * x + e, slice(POINTS * y, POINTS * y + 8), slice(0, brick.zpad))
                 grid_ref[place] = grid_ref[place] + box[8 * e : 8 * e + 8, :]
@@ -411,28 +417,29 @@
 def fine_tables(brick):
     ext_x = brick.px + 2 * REACH
     rows_y = brick.py + POINTS * brick.by
-    along_z = np.zeros((128, 128 * len(FINE_WIDTHS)), np.float32)
-    along_xy = np.zeros((brick.px * brick.py, len(FINE_WIDTHS) * ext_x * rows_y), np.float32)
+    out_lanes = brick.blocks * 128
+    in_lanes = round_up(max(ext_x * brick.zpad, out_lanes), 128)
+    count = len(FINE_WIDTHS)
+    along_xz = np.zeros((in_lanes, count * out_lanes), np.float32)
+    along_y = np.zeros((brick.py, count * rows_y), np.float32)
 
     def tap(dist, width):
         return np.where(np.abs(dist) <= REACH, np.exp(-(dist * dist) / (2.0 * width * width)), 0.0)
 
     for number, (width, weight) in enumerate(zip(FINE_WIDTHS, FINE_WEIGHTS)):
+        mat_z = np.zeros((brick.zpad, brick.zpad))
         for step in range(-REACH, REACH + 1):
             for z in range(brick.pz):
-                along_z[(z + step) % brick.pz, 128 * number + z] += weight * tap(
-                    np.float64(step), width
-                )
-        out_x = np.arange(brick.px) - 1.0
-        in_x = np.arange(ext_x) - 1.0 - REACH
-        out_y = np.arange(brick.py) - 1.0
+                mat_z[(z + step) % brick.pz, z] += weight * tap(np.float64(step), width)
+        mat_x = tap(np.arange(ext_x)[:, None] - np.arange(brick.px)[None, :] - REACH, width)
+        dense = np.kron(mat_x, mat_z)
+        along_xz[: dense.shape[0], number * out_lanes : number * out_lanes + dense.shape[1]] = dense
+        out_y = np.arange(POINTS * brick.by + 3) - 1.0
         in_y = np.arange(rows_y) - 1.0 - POINTS * brick.by
-        mat_x = tap(out_x[:, None] - in_x[None, :], width)
-        mat_y = tap(out_y[:, None] - in_y[None, :], width)
-        mat_y[POINTS * brick.by + 3 :] = 0.0
-        size = ext_x * rows_y
-        along_xy[:, number * size : (number + 1) * size] = np.kron(mat_x, mat_y)
-    return along_xy, along_z
+        along_y[: len(out_y), number * rows_y : (number + 1) * rows_y] = tap(
+            out_y[:, None] - in_y[None, :], width
+        )
+    return along_xz, along_y
 
 
 def coarse_table(brick):
@@ -464,53 +471,49 @@
     (
         whole_ref,
         short_ref,
-        xy_high_ref,
-        xy_low_ref,
-        z_ref,
+        xz_high_ref,
+        xz_low_ref,
+        y_ref,
         coarse_z_ref,
         out_ref,
-        ext_ref,
         pot_ref,
     ) = refs[2 + n_msgs :]
     even = place_ref[0] % 2 == 0
     step_y = POINTS * brick.by
     rows_y = brick.py + step_y
-    ext_x = brick.px + 2 * REACH
-    planes = {}
+    in_lanes = xz_high_ref.shape[0]
+    out_lanes = brick.blocks * 128
+    grid = None
     for dx in (-1, 0, 1):
         grids = []
         for dy in (-1, 0, 1):
             near = slice(brick.grid_row, brick.msg_rows)
-            span = slice(0, brick.blocks * 128)
+            span = slice(0, out_lanes)
             if (dx, dy) == (0, 0):
                 grids.append(msg_ref[near, span])
             else:
                 grids.append(near_rows(other_msgs, sender[(dx, dy)], even, near, span))
-        full = brick.py + 2 * step_y
-        tiles = [None] * (full // 8)
-        for number, grid in enumerate(grids):
+        tiles = [None] * ((brick.py + 2 * step_y) // 8)
+        for number, part in enumerate(grids):
             for tile in range(brick.py // 8):
                 spot = tile + number * step_y // 8
-                value = grid[8 * tile : 8 * tile + 8]
+                value = part[8 * tile : 8 * tile + 8]
                 tiles[spot] = value if tiles[spot] is None else tiles[spot] + value
         column = jnp.concatenate(tiles[: rows_y // 8], axis=0)
-        for x in range(brick.px):
-            spot = x + POINTS * brick.bx * dx + REACH
-            if 0 <= spot < ext_x:
-                block, shift = divmod(x, brick.group)
-                value = column[:, block * 128 : (block + 1) * 128]
-                if shift:
-                    value = pltpu.roll(value, 128 - shift * brick.zpad, 1)
-                planes[spot] = planes[spot] + value if spot in planes else value
-    for spot in range(ext_x):
-        ext_ref[spot * rows_y : (spot + 1) * rows_y, :] = planes[spot]
-    along = mul(ext_ref[...], z_ref[...], HIGHEST)
-    along = jnp.concatenate([along[:, :128], along[:, 128:]], axis=0)
-    high = along.astype(BF16)
-    low = (along - high.astype(F32)).astype(BF16)
-    potential = mul(xy_high_ref[...], high) + (
-        mul(xy_high_ref[...], low) + mul(xy_low_ref[...], high)
-    )
+        if in_lanes > out_lanes:
+            column = jnp.concatenate(
+                [column, jnp.zeros((rows_y, in_lanes - out_lanes), F32)], axis=1
+            )
+        shift = (REACH + POINTS * brick.bx * dx) * brick.zpad
+        column = pltpu.roll(column, shift % in_lanes, 1)
+        grid = column if grid is None else grid + column
+    pieces = jnp.concatenate(split(grid, 2), axis=0).astype(BF16)
+    mixed = mul(pieces, xz_high_ref[...]) + mul(pieces, xz_low_ref[...])
+    mixed = mixed[:rows_y] + mixed[rows_y:]
+    mixed = jnp.concatenate(
+        [mixed[:, n * out_lanes : (n + 1) * out_lanes] for n in range(len(FINE_WIDTHS))], axis=0
+    )
+    fine = mul(y_ref[...], mixed, HIGHEST)
 
     total_x = 2 * brick.bx * brick.n_space
     total_y = 2 * brick.by * brick.n_sub
@@ -550,9 +553,18 @@
                 done = lefts[number][x]
                 lefts[number][x] = value if done is None else done + value
     left = jnp.concatenate([jnp.concatenate(rows, axis=0) for rows in lefts], axis=1)
-    potential = potential + mul(left, coarse_z_ref[...], HIGHEST)
+    coarse = mul(left, coarse_z_ref[...], HIGHEST)
+    lane = lax.broadcasted_iota(jnp.int32, (brick.py, 128), 1)
     for x in range(brick.px):
-        pot_ref[x] = potential[x * brick.py : (x + 1) * brick.py]
+        block, shift = divmod(x, brick.group)
+        value = fine[:, block * 128 : (block + 1) * 128]
+        if shift:
+            value = pltpu.roll(value, 128 - shift * brick.zpad, 1)
+        value = value + coarse[x * brick.py : (x + 1) * brick.py]
+        high, low = split(jnp.where(lane < brick.zpad, value, 0.0), 2)
+        pot_ref[x] = (
+            high + pltpu.roll(high, brick.zpad, 1) + pltpu.roll(low, 2 * brick.zpad, 1)
+        )
 
     for x in range(brick.bx):
         for y in range(brick.by):
@@ -570,12 +582,14 @@
             slopes = [spline_slope(value) for value in shifted]
             box = jnp.concatenate(
                 [
-                    pot_ref[POINTS * x + e, POINTS * y : POINTS * y + 8, 0 : brick.zpad]
+                    pot_ref[POINTS * x + e, POINTS * y : POINTS * y + 8, 0 : 3 * brick.zpad]
                     for e in range(TAPS)
                 ],
                 axis=0,
             )
-            both = mul(box, jnp.concatenate([weights[2], slopes[2]], axis=1), HIGHEST)
+            high, low = split(jnp.concatenate([weights[2], slopes[2]], axis=1), 2)
+            tables = jnp.concatenate([high, low, high], axis=0).astype(BF16)
+            both = mul(box.astype(BF16), tables)
             along_z = both[:, : brick.lanes]
             sloped_z = both[:, brick.lanes :]
             sums = [0.0, 0.0, 0.0]
@@ -656,9 +670,9 @@
 def body(n_space, n_sub, positions, charges, counts):
     brick = Brick(charges.shape, n_space, n_sub)
     n_dev = n_space * n_sub
-    along_xy, along_z = fine_tables(brick)
-    xy_high = along_xy.astype(BF16)
-    xy_low = (along_xy - xy_high.astype(np.float32)).astype(BF16)
+    along_xz, along_y = fine_tables(brick)
+    xz_high = along_xz.astype(BF16)
+    xz_low = (along_xz - xz_high.astype(np.float32)).astype(BF16)
     coarse_z = coarse_table(brick)
     place = jnp.stack([lax.axis_index("space"), lax.axis_index("sub")]).astype(jnp.int32)
 
@@ -709,15 +723,12 @@
         msg,
         *msgs,
     )
-    ext_x = brick.px + 2 * REACH
-    rows_y = brick.py + POINTS * brick.by
     comps, size_x, size_y, size_z, atoms = positions.shape
     forces = call(
         functools.partial(potential_kernel, brick, sender, len(msgs)),
         jax.ShapeDtypeStruct((comps, size_x, size_z, size_y, atoms), F32),
         [SMEM] + [VMEM] * (7 + len(msgs)),
         [
-            pltpu.VMEM((ext_x * rows_y, 128), F32),
             pltpu.VMEM((brick.px, brick.py, 128), F32),
         ],
         10**8,
@@ -726,9 +737,9 @@
         *msgs,
         whole,
         short,
-        xy_high,
-        xy_low,
-        jnp.asarray(along_z),
+        xz_high,
+        xz_low,
+        jnp.asarray(along_y),
         jnp.asarray(coarse_z),
         out_spec=WHOLE,
     )

time: 32 us -> 30.2 us (0.944)
  Pallas kernels: 18 us -> 16.2 us
    pallas_call x3, Pallas kernels: 18 us -> 16.2 us  [call(): pl.pallas_call(kernel, out_shape=out_shape, in_specs=in_specs, out_specs=...]
  transfers between devices with their start and end apart: 6 -> 6, of which waited for: 1 -> 1; matrix products, arithmetic and copies ran while one was open for 0% -> 0% of each run, Pallas kernels for 37% -> 39%
where the time goes in v6:
time: 30.2 us; the launch traced here: 29.9 us
  Pallas kernels  16.2 us (54%)
  starting transfers between devices  13.3 us (44%)
    pallas_call x3, Pallas kernels, call(): pl.pallas_call(kernel, out_shape=out_shape, in_specs=in_specs, out_specs=...  16.2 us
    ppermute x5, starting transfers between devices, neighbours(): msgs.append(lax.ppermute(msg, ('space', 'sub'), pairs))  9.39 us
    all_to_all x1, starting transfers between devices, body(): whole = lax.all_to_all(coarse, ('space', 'sub'), 0, 0, tiled=True)  3.88 us
  transfers between devices with their start and end apart: 6, of which 1 were waited for; matrix products, arithmetic and copies ran while one was open for 0% of the time, Pallas kernels for 39%

profile of v6, /device:TPU:0, one launch (start us, length us, event | category | flops | bytes accessed | tf_op | source)
XLA Modules:
  0.0 29.9 jit_solution(1647657668387411307)
XLA Ops:
  0.0 2.0 %shard_map.73 = (f32[32,384]{1,0:T(8,128)}, f32[32,8,128]{2,1,0:T(8,128)}) custom-call(s32[2,2,3]{2,1,0:T(2,128)} %refs_0_.1, f32[3,2,3,2,128]{4,3,2,1,0:T(2,128)} %bitcast.7, f32[2,3,2,128]{3,2,1,0:T(2,128)} %bitcast.8), custom_call_target="tpu_custom_call" | custom-call | flops 10000000 | bytes 100000 | tf_op jit(solution)/shard_map/pallas_call | solution.py:621
  2.0 2.5 %collective-permute-start.4 = (f32[32,384]{1,0:T(8,128)}, f32[32,384]{1,0:T(8,128)S(1)}, u32[]{:S(2)}, u32[]{:S(2)}) collective-permute-start(f32[32,384]{1,0:T(8,128)} %get-tuple-element.7.refs_1_), channel_id=1, source_target_pairs={{3,0},{2,1},{1,2},{0,3},{7,4},{6,5},{5,6},{4,7},{11,8},{10,9},{9,1... | collective-permute-start | bytes 147464 | tf_op jit(solution)/shard_map/ppermute | solution.py:657
  4.5 4.8 %collective-permute-start.3 = (f32[32,384]{1,0:T(8,128)}, f32[32,384]{1,0:T(8,128)S(1)}, u32[]{:S(2)}, u32[]{:S(2)}) collective-permute-start(f32[32,384]{1,0:T(8,128)} %get-tuple-element.7.refs_1_), channel_id=1, source_target_pairs={{31,0},{30,1},{5,2},{4,3},{3,4},{2,5},{9,6},{8,7},{7,8},{6,9},{13,... | collective-permute-start | bytes 147464 | tf_op jit(solution)/shard_map/ppermute | solution.py:657
  9.3 0.0 collective-permute-start.2
  9.3 0.6 %collective-permute-start.1 = (f32[32,384]{1,0:T(8,128)}, f32[32,384]{1,0:T(8,128)S(1)}, u32[]{:S(2)}, u32[]{:S(2)}) collective-permute-start(f32[32,384]{1,0:T(8,128)} %get-tuple-element.7.refs_1_), channel_id=1, source_target_pairs={{30,0},{31,1},{4,2},{5,3},{2,4},{3,5},{8,6},{9,7},{6,8},{7,9},{12,... | collective-permute-start | bytes 147464 | tf_op jit(solution)/shard_map/ppermute | solution.py:657
  9.9 1.5 %collective-permute-start = (f32[32,384]{1,0:T(8,128)}, f32[32,384]{1,0:T(8,128)S(1)}, u32[]{:S(2)}, u32[]{:S(2)}) collective-permute-start(f32[32,384]{1,0:T(8,128)} %get-tuple-element.7.refs_1_), channel_id=1, source_target_pairs={{1,0},{0,1},{3,2},{2,3},{5,4},{4,5},{7,6},{6,7},{9,8},{8,9},{11,10... | collective-permute-start | bytes 147464 | tf_op jit(solution)/shard_map/ppermute | solution.py:657
  11.4 0.0 copy-start.3
  11.4 3.9 %all-to-all-start = ((f32[32,8,128]{2,1,0:T(8,128)}), f32[32,8,128]{2,1,0:T(8,128)S(1)}, u32[]{:S(2)}, u32[]{:S(2)}) async-start(f32[32,8,128]{2,1,0:T(8,128)} %get-tuple-element.8), calls=%async_computation | async-start | bytes 262144 | tf_op jit(solution)/shard_map/all_to_all | solution.py:700
  15.3 0.1 pad_add_fusion.refs_0_
  15.4 0.0 copy-start
  15.4 0.0 copy-start.1
  15.4 0.0 copy-start.2
  15.4 0.0 copy-start.4
  15.4 0.0 collective-permute-done.4.refs_6_
  15.4 0.0 collective-permute-done.3.refs_5_
  15.4 0.0 collective-permute-done.2.refs_4_
  15.4 0.2 collective-permute-done.1.refs_3_
  15.7 0.0 collective-permute-done.refs_2_
  15.7 0.0 copy-done.3
  15.7 11.8 %shard_map.74.refs_8_ = f32[16,384]{1,0:T(8,128)S(1)} custom-call(s32[2]{0:T(128)S(1)} %pad_add_fusion.refs_0_, f32[32,384]{1,0:T(8,128)S(1)} %copy-done.3, f32[32,384]{1,0:T(8,128)S(1)} %collective-permute-done.refs_2_, f32[32,384]{1,0:T(8,128)S(1)} %collective-permute-done.1.refs_3_, f32[32,384]{1,0:T(8,128)S(1)} %collective-permute-done.2.refs_4_, ...), custom_call_target="tpu_custom_call" | custom-call | flops 10000000000 | bytes 100000 | tf_op jit(solution)/shard_map/pallas_call | solution.py:621
  27.5 0.0 all-to-all-done
  27.5 0.0 copy-done
  27.5 0.0 copy-done.1
  27.5 0.0 copy-done.2
  27.5 0.0 copy-done.4
  27.5 2.4 %shard_map.75 = f32[3,2,3,2,128]{4,3,2,1,0:T(2,128)} custom-call(s32[2]{0:T(128)S(1)} %pad_add_fusion.refs_0_, f32[32,384]{1,0:T(8,128)S(1)} %copy-done.3, f32[32,384]{1,0:T(8,128)S(1)} %collective-permute-done.refs_2_, f32[32,384]{1,0:T(8,128)S(1)} %collective-permute-done.1.refs_3_, f32[32,384]{1,0:T(8,128)S(1)} %collective-permute-done.2.refs_4_, ...), custom_call_target="tpu_custom_call" | custom-call | flops 100000000 | bytes 100000 | tf_op jit(solution)/shard_map/pallas_call | solution.py:621
Async XLA Ops:
  2.0 13.4 %collective-permute-start.4 = (f32[32,384]{1,0:T(8,128)}, f32[32,384]{1,0:T(8,128)S(1)}, u32[]{:S(2)}, u32[]{:S(2)}) collective-permute-start(f32[32,384]{1,0:T(8,128)} %get-tuple-element.7.refs_1_), channel_id=1, source_target_pairs={{3,0},{2,1},{1,2},{0,3},{7,4},{6,5},{5,6},{4,7},{11,8},{10,9},{9,1... | collective-permute-start | bytes 147464 | tf_op jit(solution)/shard_map/ppermute | solution.py:657
  4.5 10.9 %collective-permute-start.3 = (f32[32,384]{1,0:T(8,128)}, f32[32,384]{1,0:T(8,128)S(1)}, u32[]{:S(2)}, u32[]{:S(2)}) collective-permute-start(f32[32,384]{1,0:T(8,128)} %get-tuple-element.7.refs_1_), channel_id=1, source_target_pairs={{31,0},{30,1},{5,2},{4,3},{3,4},{2,5},{9,6},{8,7},{7,8},{6,9},{13,... | collective-permute-start | bytes 147464 | tf_op jit(solution)/shard_map/ppermute | solution.py:657
  9.3 6.2 %collective-permute-start.2 = (f32[32,384]{1,0:T(8,128)}, f32[32,384]{1,0:T(8,128)S(1)}, u32[]{:S(2)}, u32[]{:S(2)}) collective-permute-start(f32[32,384]{1,0:T(8,128)} %get-tuple-element.7.refs_1_), channel_id=1, source_target_pairs={{2,0},{3,1},{0,2},{1,3},{6,4},{7,5},{4,6},{5,7},{10,8},{11,9},{8,1... | collective-permute-start | bytes 147464 | tf_op jit(solution)/shard_map/ppermute | solution.py:657
  9.3 6.4 %collective-permute-start.1 = (f32[32,384]{1,0:T(8,128)}, f32[32,384]{1,0:T(8,128)S(1)}, u32[]{:S(2)}, u32[]{:S(2)}) collective-permute-start(f32[32,384]{1,0:T(8,128)} %get-tuple-element.7.refs_1_), channel_id=1, source_target_pairs={{30,0},{31,1},{4,2},{5,3},{2,4},{3,5},{8,6},{9,7},{6,8},{7,9},{12,... | collective-permute-start | bytes 147464 | tf_op jit(solution)/shard_map/ppermute | solution.py:657
  9.9 5.8 %collective-permute-start = (f32[32,384]{1,0:T(8,128)}, f32[32,384]{1,0:T(8,128)S(1)}, u32[]{:S(2)}, u32[]{:S(2)}) collective-permute-start(f32[32,384]{1,0:T(8,128)} %get-tuple-element.7.refs_1_), channel_id=1, source_target_pairs={{1,0},{0,1},{3,2},{2,3},{5,4},{4,5},{7,6},{6,7},{9,8},{8,9},{11,10... | collective-permute-start | bytes 147464 | tf_op jit(solution)/shard_map/ppermute | solution.py:657
  11.4 4.3 %copy-start.3 = (f32[32,384]{1,0:T(8,128)S(1)}, f32[32,384]{1,0:T(8,128)}, u32[]{:S(2)}) copy-start(f32[32,384]{1,0:T(8,128)} %get-tuple-element.7.refs_1_) | copy-start | bytes 147460
  11.4 16.1 %all-to-all-start = ((f32[32,8,128]{2,1,0:T(8,128)}), f32[32,8,128]{2,1,0:T(8,128)S(1)}, u32[]{:S(2)}, u32[]{:S(2)}) async-start(f32[32,8,128]{2,1,0:T(8,128)} %get-tuple-element.8), calls=%async_computation | async-start | bytes 262144 | tf_op jit(solution)/shard_map/all_to_all | solution.py:700
  15.4 12.1 %copy-start = (bf16[384,512]{1,0:T(8,128)(2,1)S(1)}, bf16[384,512]{1,0:T(8,128)(2,1)}, u32[]{:S(2)}) copy-start(bf16[384,512]{1,0:T(8,128)(2,1)} %constant.19.clone.refs_10_) | copy-start | bytes 1179652
  15.4 12.1 %copy-start.1 = (bf16[384,512]{1,0:T(8,128)(2,1)S(1)}, bf16[384,512]{1,0:T(8,128)(2,1)}, u32[]{:S(2)}) copy-start(bf16[384,512]{1,0:T(8,128)(2,1)} %constant.18.clone.refs_9_) | copy-start | bytes 1179652
  15.4 12.1 %copy-start.2 = (f32[256,128]{1,0:T(8,128)S(1)}, f32[256,128]{1,0:T(8,128)}, u32[]{:S(2)}) copy-start(f32[256,128]{1,0:T(8,128)} %constant.17.clone.refs_12_) | copy-start | bytes 393220
  15.4 12.1 %copy-start.4 = (f32[16,48]{1,0:T(8,128)S(1)}, f32[16,48]{1,0:T(8,128)}, u32[]{:S(2)}) copy-start(f32[16,48]{1,0:T(8,128)} %constant.16.clone.refs_11_) | copy-start | bytes 9220

commit v7 on v6

--- a/solution.py
+++ b/solution.py
@@ -265,9 +265,9 @@
 
 def pairs_kernel(brick, sender, n_msgs, *refs):
     atoms, lanes = brick.atoms, brick.lanes
-    place_ref, msg_ref = refs[0:2]
-    other_msgs = refs[2 : 2 + n_msgs]
-    force_ref = refs[2 + n_msgs]
+    msg_ref = refs[0]
+    other_msgs = refs[1 : 1 + n_msgs]
+    force_ref = refs[1 + n_msgs]
     (
         row_ref,
         other_piece_ref,
@@ -280,8 +280,7 @@
         back_ref,
         total_ref,
         kept_ref,
-    ) = refs[3 + n_msgs :]
-    even = place_ref[0] % 2 == 0
+    ) = refs[2 + n_msgs :]
     half = 0.5 * brick.bz
 
     rows = brick.ext_rows
@@ -295,7 +294,7 @@
             if shift == (0, 0):
                 value = msg_ref[near, 0:lanes]
             else:
-                value = near_rows(other_msgs, sender[shift], even, near, slice(0, lanes))
+                value = other_msgs[sender[shift]][near, 0:lanes]
             row_ref[k * rows + place : k * rows + place + 1, :] = value
     index = lax.broadcasted_iota(jnp.int32, (rows, 1), 0)
     ext_y = brick.by + 2
@@ -478,7 +477,6 @@
         out_ref,
         pot_ref,
     ) = refs[2 + n_msgs :]
-    even = place_ref[0] % 2 == 0
     step_y = POINTS * brick.by
     rows_y = brick.py + step_y
     in_lanes = xz_high_ref.shape[0]
@@ -492,7 +490,7 @@
             if (dx, dy) == (0, 0):
                 grids.append(msg_ref[near, span])
             else:
-                grids.append(near_rows(other_msgs, sender[(dx, dy)], even, near, span))
+                grids.append(other_msgs[sender[(dx, dy)]][near, span])
         tiles = [None] * ((brick.py + 2 * step_y) // 8)
         for number, part in enumerate(grids):
             for tile in range(brick.py // 8):
@@ -631,40 +629,24 @@
 
 def neighbours(brick, msg):
     size, wide = brick.n_space, brick.n_sub
-    pairings = {
-        0: lambda i: i,
-        1: lambda i: i ^ 1,
-        2: lambda i: (((i + 1) % size ^ 1) - 1) % size,
-    }
     found = {}
     sender = {}
     msgs = []
-    for dx in (0, -1, 1):
+    for dx in (1, 0, -1):
         for dy in (0, -1, 1):
             if (dx, dy) == (0, 0):
                 continue
-            numbers = []
-            for parity in (0, 1):
-                pairing = 0 if dx == 0 else 1 if (dx == 1) == (parity == 0) else 2
-                key = (pairing, dy % wide)
-                if key not in found:
-                    found[key] = len(msgs)
-                    pairs = [
-                        (pairings[pairing](i) * wide + (j + dy) % wide, i * wide + j)
-                        for i in range(size)
-                        for j in range(wide)
-                    ]
-                    msgs.append(lax.ppermute(msg, ("space", "sub"), pairs))
-                numbers.append(found[key])
-            sender[(dx, dy)] = tuple(numbers)
+            key = (dx % size, dy % wide)
+            if key not in found:
+                found[key] = len(msgs)
+                pairs = [
+                    ((i + dx) % size * wide + (j + dy) % wide, i * wide + j)
+                    for i in range(size)
+                    for j in range(wide)
+                ]
+                msgs.append(lax.ppermute(msg, ("space", "sub"), pairs))
+            sender[(dx, dy)] = found[key]
     return sender, msgs
-
-
-def near_rows(msgs, numbers, even, rows, span):
-    first = msgs[numbers[0]][rows, span]
-    if numbers[0] == numbers[1]:
-        return first
-    return jnp.where(even, first, msgs[numbers[1]][rows, span])
 
 
 def body(n_space, n_sub, positions, charges, counts):
@@ -704,7 +686,7 @@
     short = call(
         functools.partial(pairs_kernel, brick, sender, len(msgs)),
         jax.ShapeDtypeStruct((brick.force_rows, brick.lanes), F32),
-        [SMEM] + [VMEM] * (1 + len(msgs)),
+        [VMEM] * (1 + len(msgs)),
         [
             pltpu.VMEM((4 * brick.ext_rows, brick.lanes), F32),
             pltpu.VMEM((brick.lanes // 128, FEATURES * brick.ext_rows, 128), F32),
@@ -719,7 +701,6 @@
             pltpu.VMEM((brick.cols, brick.bz, brick.atoms, brick.kept), BF16),
         ],
         10**10,
-        place,
         msg,
         *msgs,
     )

time: 30.2 us -> 27.8 us (0.921)
  starting transfers between devices: 13.3 us -> 11.7 us
  Pallas kernels: 16.2 us -> 15.6 us
    all_to_all x1, starting transfers between devices: 3.88 us -> 2.69 us  [body(): whole = lax.all_to_all(coarse, ('space', 'sub'), 0, 0, tiled=True)]
    pallas_call x3, Pallas kernels: 16.2 us -> 15.6 us  [call(): pl.pallas_call(kernel, out_shape=out_shape, in_specs=in_specs, out_specs=...]
    ppermute x5, starting transfers between devices: 9.39 us -> 9.04 us  [neighbours(): msgs.append(lax.ppermute(msg, ('space', 'sub'), pairs))]
  transfers between devices with their start and end apart: 6 -> 6, of which waited for: 1 -> 0; matrix products, arithmetic and copies ran while one was open for 0% -> 0% of each run, Pallas kernels for 39% -> 41%
where the time goes in v7:
time: 27.8 us; the launch traced here: 27.5 us
  Pallas kernels  15.6 us (56%)
  starting transfers between devices  11.7 us (42%)
    pallas_call x3, Pallas kernels, call(): pl.pallas_call(kernel, out_shape=out_shape, in_specs=in_specs, out_specs=...  15.6 us
    ppermute x5, starting transfers between devices, neighbours(): msgs.append(lax.ppermute(msg, ('space', 'sub'), pairs))  9.04 us
    all_to_all x1, starting transfers between devices, body(): whole = lax.all_to_all(coarse, ('space', 'sub'), 0, 0, tiled=True)  2.69 us
  transfers between devices with their start and end apart: 6, of which 0 were waited for; matrix products, arithmetic and copies ran while one was open for 0% of the time, Pallas kernels for 41%

profile of v7, /device:TPU:0, one launch (start us, length us, event | category | flops | bytes accessed | tf_op | source)
XLA Modules:
  0.0 27.5 jit_solution(3709907700493006169)
XLA Ops:
  0.0 2.0 %shard_map.73 = (f32[32,384]{1,0:T(8,128)}, f32[32,8,128]{2,1,0:T(8,128)}) custom-call(s32[2,2,3]{2,1,0:T(2,128)} %refs_0_.1, f32[3,2,3,2,128]{4,3,2,1,0:T(2,128)} %bitcast.7, f32[2,3,2,128]{3,2,1,0:T(2,128)} %bitcast.8), custom_call_target="tpu_custom_call" | custom-call | flops 10000000 | bytes 100000 | tf_op jit(solution)/shard_map/pallas_call | solution.py:619
  2.0 2.5 %collective-permute-start.4 = (f32[32,384]{1,0:T(8,128)}, f32[32,384]{1,0:T(8,128)S(1)}, u32[]{:S(2)}, u32[]{:S(2)}) collective-permute-start(f32[32,384]{1,0:T(8,128)} %get-tuple-element.7.refs_0_.refs_1_), channel_id=1, source_target_pairs={{31,0},{30,1},{1,2},{0,3},{3,4},{2,5},{5,6},{4,7},{7,8},{6,9},{9,1... | collective-permute-start | bytes 147464 | tf_op jit(solution)/shard_map/ppermute | solution.py:647
  4.5 1.6 %collective-permute-start.3 = (f32[32,384]{1,0:T(8,128)}, f32[32,384]{1,0:T(8,128)S(1)}, u32[]{:S(2)}, u32[]{:S(2)}) collective-permute-start(f32[32,384]{1,0:T(8,128)} %get-tuple-element.7.refs_0_.refs_1_), channel_id=1, source_target_pairs={{30,0},{31,1},{0,2},{1,3},{2,4},{3,5},{4,6},{5,7},{6,8},{7,9},{8,1... | collective-permute-start | bytes 147464 | tf_op jit(solution)/shard_map/ppermute | solution.py:647
  6.1 0.5 %collective-permute-start.2 = (f32[32,384]{1,0:T(8,128)}, f32[32,384]{1,0:T(8,128)S(1)}, u32[]{:S(2)}, u32[]{:S(2)}) collective-permute-start(f32[32,384]{1,0:T(8,128)} %get-tuple-element.7.refs_0_.refs_1_), channel_id=1, source_target_pairs={{1,0},{0,1},{3,2},{2,3},{5,4},{4,5},{7,6},{6,7},{9,8},{8,9},{11,10... | collective-permute-start | bytes 147464 | tf_op jit(solution)/shard_map/ppermute | solution.py:647
  6.6 3.5 %collective-permute-start.1 = (f32[32,384]{1,0:T(8,128)}, f32[32,384]{1,0:T(8,128)S(1)}, u32[]{:S(2)}, u32[]{:S(2)}) collective-permute-start(f32[32,384]{1,0:T(8,128)} %get-tuple-element.7.refs_0_.refs_1_), channel_id=1, source_target_pairs={{3,0},{2,1},{5,2},{4,3},{7,4},{6,5},{9,6},{8,7},{11,8},{10,9},{13,... | collective-permute-start | bytes 147464 | tf_op jit(solution)/shard_map/ppermute | solution.py:647
  10.1 1.0 %collective-permute-start = (f32[32,384]{1,0:T(8,128)}, f32[32,384]{1,0:T(8,128)S(1)}, u32[]{:S(2)}, u32[]{:S(2)}) collective-permute-start(f32[32,384]{1,0:T(8,128)} %get-tuple-element.7.refs_0_.refs_1_), channel_id=1, source_target_pairs={{2,0},{3,1},{4,2},{5,3},{6,4},{7,5},{8,6},{9,7},{10,8},{11,9},{12,... | collective-permute-start | bytes 147464 | tf_op jit(solution)/shard_map/ppermute | solution.py:647
  11.1 0.0 copy-start.3
  11.1 2.7 %all-to-all-start = ((f32[32,8,128]{2,1,0:T(8,128)}), f32[32,8,128]{2,1,0:T(8,128)S(1)}, u32[]{:S(2)}, u32[]{:S(2)}) async-start(f32[32,8,128]{2,1,0:T(8,128)} %get-tuple-element.8), calls=%async_computation | async-start | bytes 262144 | tf_op jit(solution)/shard_map/all_to_all | solution.py:682
  13.8 0.1 pad_add_fusion.refs_0_
  13.9 0.0 copy-start
  13.9 0.0 copy-start.1
  13.9 0.0 copy-start.2
  13.9 0.0 copy-start.4
  13.9 0.0 collective-permute-done.4.refs_5_.refs_6_
  13.9 0.0 collective-permute-done.3.refs_4_.refs_5_
  13.9 0.0 collective-permute-done.2.refs_3_.refs_4_
  13.9 0.0 collective-permute-done.1.refs_2_.refs_3_
  13.9 0.0 collective-permute-done.refs_1_.refs_2_
  13.9 0.0 copy-done.3
  13.9 11.2 %shard_map.74.refs_8_ = f32[16,384]{1,0:T(8,128)S(1)} custom-call(f32[32,384]{1,0:T(8,128)S(1)} %copy-done.3, f32[32,384]{1,0:T(8,128)S(1)} %collective-permute-done.refs_1_.refs_2_, f32[32,384]{1,0:T(8,128)S(1)} %collective-permute-done.1.refs_2_.refs_3_, f32[32,384]{1,0:T(8,128)S(1)} %collective-permute-done.2.refs_3_.refs_4_, ...), custom_call_target="tpu_custom_call" | custom-call | flops 10000000000 | bytes 100000 | tf_op jit(solution)/shard_map/pallas_call | solution.py:619
  25.1 0.0 all-to-all-done
  25.1 0.0 copy-done
  25.2 0.0 copy-done.1
  25.2 0.0 copy-done.2
  25.2 0.0 copy-done.4
  25.2 2.4 %shard_map.75 = f32[3,2,3,2,128]{4,3,2,1,0:T(2,128)} custom-call(s32[2]{0:T(128)S(1)} %pad_add_fusion.refs_0_, f32[32,384]{1,0:T(8,128)S(1)} %copy-done.3, f32[32,384]{1,0:T(8,128)S(1)} %collective-permute-done.refs_1_.refs_2_, f32[32,384]{1,0:T(8,128)S(1)} %collective-permute-done.1.refs_2_.refs_3_, f32[32,384]{1,0:T(8,128)S(1)} %collective-permute-done.2.refs_3_.refs_4_, ...), custom_call_target="tpu_custom_call" | custom-call | flops 100000000 | bytes 100000 | tf_op jit(solution)/shard_map/pallas_call | solution.py:619
Async XLA Ops:
  2.0 11.8 %collective-permute-start.4 = (f32[32,384]{1,0:T(8,128)}, f32[32,384]{1,0:T(8,128)S(1)}, u32[]{:S(2)}, u32[]{:S(2)}) collective-permute-start(f32[32,384]{1,0:T(8,128)} %get-tuple-element.7.refs_0_.refs_1_), channel_id=1, source_target_pairs={{31,0},{30,1},{1,2},{0,3},{3,4},{2,5},{5,6},{4,7},{7,8},{6,9},{9,1... | collective-permute-start | bytes 147464 | tf_op jit(solution)/shard_map/ppermute | solution.py:647
  4.5 9.4 %collective-permute-start.3 = (f32[32,384]{1,0:T(8,128)}, f32[32,384]{1,0:T(8,128)S(1)}, u32[]{:S(2)}, u32[]{:S(2)}) collective-permute-start(f32[32,384]{1,0:T(8,128)} %get-tuple-element.7.refs_0_.refs_1_), channel_id=1, source_target_pairs={{30,0},{31,1},{0,2},{1,3},{2,4},{3,5},{4,6},{5,7},{6,8},{7,9},{8,1... | collective-permute-start | bytes 147464 | tf_op jit(solution)/shard_map/ppermute | solution.py:647
  6.1 7.8 %collective-permute-start.2 = (f32[32,384]{1,0:T(8,128)}, f32[32,384]{1,0:T(8,128)S(1)}, u32[]{:S(2)}, u32[]{:S(2)}) collective-permute-start(f32[32,384]{1,0:T(8,128)} %get-tuple-element.7.refs_0_.refs_1_), channel_id=1, source_target_pairs={{1,0},{0,1},{3,2},{2,3},{5,4},{4,5},{7,6},{6,7},{9,8},{8,9},{11,10... | collective-permute-start | bytes 147464 | tf_op jit(solution)/shard_map/ppermute | solution.py:647
  6.6 7.3 %collective-permute-start.1 = (f32[32,384]{1,0:T(8,128)}, f32[32,384]{1,0:T(8,128)S(1)}, u32[]{:S(2)}, u32[]{:S(2)}) collective-permute-start(f32[32,384]{1,0:T(8,128)} %get-tuple-element.7.refs_0_.refs_1_), channel_id=1, source_target_pairs={{3,0},{2,1},{5,2},{4,3},{7,4},{6,5},{9,6},{8,7},{11,8},{10,9},{13,... | collective-permute-start | bytes 147464 | tf_op jit(solution)/shard_map/ppermute | solution.py:647
  10.1 3.8 %collective-permute-start = (f32[32,384]{1,0:T(8,128)}, f32[32,384]{1,0:T(8,128)S(1)}, u32[]{:S(2)}, u32[]{:S(2)}) collective-permute-start(f32[32,384]{1,0:T(8,128)} %get-tuple-element.7.refs_0_.refs_1_), channel_id=1, source_target_pairs={{2,0},{3,1},{4,2},{5,3},{6,4},{7,5},{8,6},{9,7},{10,8},{11,9},{12,... | collective-permute-start | bytes 147464 | tf_op jit(solution)/shard_map/ppermute | solution.py:647
  11.1 2.8 %copy-start.3 = (f32[32,384]{1,0:T(8,128)S(1)}, f32[32,384]{1,0:T(8,128)}, u32[]{:S(2)}) copy-start(f32[32,384]{1,0:T(8,128)} %get-tuple-element.7.refs_0_.refs_1_) | copy-start | bytes 147460
  11.1 14.1 %all-to-all-start = ((f32[32,8,128]{2,1,0:T(8,128)}), f32[32,8,128]{2,1,0:T(8,128)S(1)}, u32[]{:S(2)}, u32[]{:S(2)}) async-start(f32[32,8,128]{2,1,0:T(8,128)} %get-tuple-element.8), calls=%async_computation | async-start | bytes 262144 | tf_op jit(solution)/shard_map/all_to_all | solution.py:682
  13.9 11.3 %copy-start = (bf16[384,512]{1,0:T(8,128)(2,1)S(1)}, bf16[384,512]{1,0:T(8,128)(2,1)}, u32[]{:S(2)}) copy-start(bf16[384,512]{1,0:T(8,128)(2,1)} %constant.19.clone.refs_10_) | copy-start | bytes 1179652
  13.9 11.3 %copy-start.1 = (bf16[384,512]{1,0:T(8,128)(2,1)S(1)}, bf16[384,512]{1,0:T(8,128)(2,1)}, u32[]{:S(2)}) copy-start(bf16[384,512]{1,0:T(8,128)(2,1)} %constant.18.clone.refs_9_) | copy-start | bytes 1179652
  13.9 11.3 %copy-start.2 = (f32[256,128]{1,0:T(8,128)S(1)}, f32[256,128]{1,0:T(8,128)}, u32[]{:S(2)}) copy-start(f32[256,128]{1,0:T(8,128)} %constant.17.clone.refs_12_) | copy-start | bytes 393220
  13.9 11.3 %copy-start.4 = (f32[16,48]{1,0:T(8,128)S(1)}, f32[16,48]{1,0:T(8,128)}, u32[]{:S(2)}) copy-start(f32[16,48]{1,0:T(8,128)} %constant.16.clone.refs_11_) | copy-start | bytes 9220

commit v8 on v7

--- a/solution.py
+++ b/solution.py
@@ -128,8 +128,8 @@
 
 
 def spread_kernel(brick, *refs):
-    inputs, (msg_ref, coarse_ref), held = refs[0:3], refs[3:5], refs[5:8]
-    grid_ref, arrived = refs[8:]
+    inputs, outputs, held = refs[0:3], refs[3:5], refs[5:8]
+    msg_ref, coarse_ref, grid_ref, arrived, sent = refs[8:]
     counts_ref, pos_ref, charge_ref = held
     copies = [
         pltpu.make_async_copy(source, target, arrived.at[number])
@@ -184,6 +184,8 @@
                 plane = grid_ref[x]
                 total = total + (pltpu.roll(plane, spot * brick.zpad, 1) if spot else plane)
         msg_ref[brick.grid_row :, block * 128 : (block + 1) * 128] = total
+    send_msg = pltpu.make_async_copy(msg_ref, outputs[0], sent.at[0])
+    send_msg.start()
     planes = []
     for idx in range(brick.ci):
         inside = [x for x in (2 * idx - 1, 2 * idx) if 0 <= x < brick.px]
@@ -206,33 +208,31 @@
     if brick.coarse_rows > brick.ci:
         sums.append(jnp.zeros((brick.coarse_rows - brick.ci, brick.coarse_lanes), F32))
     coarse_ref[...] = jnp.broadcast_to(jnp.concatenate(sums, axis=0)[None], coarse_ref.shape)
-
-
-def store_pieces(piece_ref, rows, arrays):
-    for number, value in enumerate(arrays):
+    send_coarse = pltpu.make_async_copy(coarse_ref, outputs[1], sent.at[1])
+    send_coarse.start()
+    send_msg.wait()
+    send_coarse.wait()
+
+
+def store_pieces(piece_ref, rows, arrays, first=0):
+    for number, value in enumerate(arrays, first):
         for block in range(piece_ref.shape[0]):
             piece_ref[block, number * rows : (number + 1) * rows, :] = value[
                 :, block * 128 : (block + 1) * 128
             ]
 
 
-def load_pieces(piece_ref, rows, row, count):
+def load_pieces(piece_ref, rows, row, count, first=0):
     parts = [
-        piece_ref[block, pl.ds(row, count, stride=rows), :] for block in range(piece_ref.shape[0])
+        piece_ref[block, pl.ds(first * rows + row, count, stride=rows), :]
+        for block in range(piece_ref.shape[0])
     ]
     return jnp.concatenate(parts, axis=1)
 
 
-def feature_arrays(coords, square, order, square_first):
-    rows = coords[0].shape
-    arrays = []
-    for value in coords:
-        pieces = split(value, 3)
-        arrays += [pieces[piece] for piece in order]
-    squares = split(square, 3)
-    ones = [jnp.ones(rows, F32)] * 3
-    arrays += squares + ones if square_first else ones + squares
-    return arrays + [jnp.zeros(rows, F32)] * (FEATURES - len(arrays))
+def product_pieces(value, order):
+    pieces = split(value, 3)
+    return [pieces[piece] for piece in order]
 
 
 def source_arrays(coords, charge):
@@ -307,11 +307,13 @@
         (row_ref[2 * rows : 3 * rows, :] + (lane_z - half)) * SCALE,
     ]
     charge = row_ref[3 * rows : 4 * rows, :]
-    store_pieces(
-        other_piece_ref,
-        rows,
-        feature_arrays(coords, minus_square(coords), (0, 1, 2, 0, 1, 0), False),
-    )
+    order = (0, 1, 2, 0, 1, 0)
+    zero = jnp.zeros((rows, lanes), F32)
+    one = jnp.ones((rows, lanes), F32)
+    arrays = product_pieces(coords[0], order) + product_pieces(coords[1], order)
+    arrays += split(minus_square(coords), 3) + [zero]
+    arrays += product_pieces(coords[2], order) + [one] * 3
+    store_pieces(other_piece_ref, rows, arrays + [zero] * (FEATURES - len(arrays)))
     store_pieces(source_piece_ref, rows, source_arrays(coords, charge))
     level_sums = {}
     for place in range(len(brick.columns)):
@@ -334,20 +336,36 @@
     index = lax.broadcasted_iota(jnp.int32, (rows, 1), 0)
     own_x = (own[0] + ((index // brick.by).astype(F32) - 0.5 * brick.bx)) * SCALE
     own_y = (own[1] + ((index % brick.by).astype(F32) - 0.5 * brick.by)) * SCALE
+    order = (0, 0, 0, 1, 1, 2)
+    zero = jnp.zeros((rows, lanes), F32)
+    one = jnp.ones((rows, lanes), F32)
+    fixed = product_pieces(2.0 * own_x, order) + product_pieces(2.0 * own_y, order)
+    fixed += [one] * 3 + [zero]
+    own_half = len(fixed)
+    store_pieces(own_piece_ref, rows, fixed)
+    store_pieces(own_piece_ref, rows, [zero] * (FEATURES - own_half - 9), own_half + 9)
+    store_pieces(
+        own_source_ref, rows, split(own[3], 3) + split(own[3] * own_x, 3) + split(own[3] * own_y, 3)
+    )
+    store_pieces(own_source_ref, rows, [zero] * (SOURCES - 12), 12)
     own_z_coords = []
     for other_z in range(brick.bz):
         step = other_z - lane_z
         step = jnp.where(step > half, step - brick.bz, step)
         step = jnp.where(step < -half, step + brick.bz, step)
-        own_z_coords.append((own[2] + (other_z - step - half)) * SCALE)
-        coords = [own_x, own_y, own_z_coords[-1]]
-        arrays = feature_arrays(coords, minus_square(coords), (0, 0, 0, 1, 1, 2), True)
-        arrays = [2.0 * value for value in arrays[:18]] + arrays[18:]
-        store_pieces(own_piece_ref, rows, arrays)
-        store_pieces(own_source_ref, rows, source_arrays(coords, own[3]))
+        own_z = (own[2] + (other_z - step - half)) * SCALE
+        own_z_coords.append(own_z)
+        arrays = product_pieces(2.0 * own_z, order)
+        arrays += split(minus_square([own_x, own_y, own_z]), 3)
+        store_pieces(own_piece_ref, rows, arrays, own_half)
+        store_pieces(own_source_ref, rows, split(own[3] * own_z, 3), 9)
         for col in range(brick.cols):
-            part = load_pieces(own_piece_ref, rows, col, FEATURES)
-            right_ref[col, other_z] = part.astype(BF16)
+            if other_z == 0:
+                part = load_pieces(own_piece_ref, rows, col, own_half).astype(BF16)
+                for z in range(brick.bz):
+                    right_ref[col, z, 0:own_half] = part
+            part = load_pieces(own_piece_ref, rows, col, FEATURES - own_half, own_half)
+            right_ref[col, other_z, own_half:] = part.astype(BF16)
             part = load_pieces(own_source_ref, rows, col, SOURCES).astype(BF16)
             for z in range(brick.bz):
                 cell = part[:, z * atoms : (z + 1) * atoms]
@@ -390,10 +408,19 @@
             kept_ref[home, z, :, spot : spot + atoms] = high
             kept_ref[home, z, :, spot + atoms : spot + 2 * atoms] = low
     back_sums = {}
+    back_lifts = {}
     for (col, z), found in mirrors.items():
         back = jnp.concatenate([back_ref[c, z, own_z] for c, own_z in found], axis=1)
-        level = (-0.5 * LEVEL) * jnp.sum(back.astype(F32), axis=1, keepdims=True)
+        level = 0.0
+        lift = jnp.zeros((1, 1), F32)
+        for c, own_z in found:
+            value = level_sums[(brick.columns.index(cells[c]), own_z)]
+            level = level + value
+            turns = round((z - own_z) / brick.bz)
+            if turns:
+                lift = lift + (turns * brick.bz * SCALE) * moments(value, 0)
         back_sums[(col, z)] = mul_t(kept_ref[col, z, :, 0 : back.shape[1]], back).T + level
+        back_lifts[(col, z)] = jnp.broadcast_to(lift, (1, atoms))
 
     for col in range(brick.cols):
         forces = [0.0, 0.0, 0.0]
@@ -409,6 +436,10 @@
         for comp, coord in enumerate((own_x, own_y, home)):
             row = comp * brick.cols + col
             value = coord[col : col + 1] * weight - moments(total, 1 + comp)
+            if comp == 2:
+                value = value - jnp.concatenate(
+                    [back_lifts[(col, z)] for z in range(brick.bz)], axis=1
+                )
             value = value + forces[comp]
             force_ref[row : row + 1, :] = value * (own[3][col : col + 1] * (SCALE * SCALE))
 
@@ -632,7 +663,7 @@
     found = {}
     sender = {}
     msgs = []
-    for dx in (1, 0, -1):
+    for dx in (0, 1, -1):
         for dy in (0, -1, 1):
             if (dx, dy) == (0, 0):
                 continue
@@ -670,12 +701,16 @@
             pltpu.SMEM(counts.shape, jnp.int32),
             pltpu.VMEM(turned[0].shape, F32),
             pltpu.VMEM(turned[1].shape, F32),
+            pltpu.VMEM((brick.msg_rows, brick.msg_lanes), F32),
+            pltpu.VMEM((n_dev, brick.coarse_rows, brick.coarse_lanes), F32),
             pltpu.VMEM((brick.px, brick.py, 128), F32),
             pltpu.SemaphoreType.DMA((3,)),
+            pltpu.SemaphoreType.DMA((2,)),
         ],
         10**7,
         counts,
         *turned,
+        out_spec=ANY,
         grant=64,
     )
     sender, msgs = neighbours(brick, msg)

time: 27.8 us -> 27.8 us (level)
  no operation moved by 1% of the time
where the time goes in v8:
time: 27.8 us; the launch traced here: 27.5 us
  Pallas kernels  15.6 us (56%)
  starting transfers between devices  11.7 us (42%)
    pallas_call x3, Pallas kernels, call(): pl.pallas_call(kernel, out_shape=out_shape, in_specs=in_specs, out_specs=...  15.6 us
    ppermute x5, starting transfers between devices, neighbours(): msgs.append(lax.ppermute(msg, ('space', 'sub'), pairs))  9.04 us
    all_to_all x1, starting transfers between devices, body(): whole = lax.all_to_all(coarse, ('space', 'sub'), 0, 0, tiled=True)  2.69 us
  transfers between devices with their start and end apart: 6, of which 0 were waited for; matrix products, arithmetic and copies ran while one was open for 0% of the time, Pallas kernels for 41%

profile of v8, /device:TPU:0, one launch (start us, length us, event | category | flops | bytes accessed | tf_op | source)
XLA Modules:
  0.0 27.5 jit_solution(1339250447877391306)
XLA Ops:
  0.0 2.0 %shard_map.73 = (f32[32,384]{1,0:T(8,128)}, f32[32,8,128]{2,1,0:T(8,128)}) custom-call(s32[2,2,3]{2,1,0:T(2,128)} %refs_0_.1, f32[3,2,3,2,128]{4,3,2,1,0:T(2,128)} %bitcast.7, f32[2,3,2,128]{3,2,1,0:T(2,128)} %bitcast.8), custom_call_target="tpu_custom_call" | custom-call | flops 10000000 | bytes 100000 | tf_op jit(solution)/shard_map/pallas_call | solution.py:650
  2.0 2.5 %collective-permute-start.4 = (f32[32,384]{1,0:T(8,128)}, f32[32,384]{1,0:T(8,128)S(1)}, u32[]{:S(2)}, u32[]{:S(2)}) collective-permute-start(f32[32,384]{1,0:T(8,128)} %get-tuple-element.7.refs_0_.refs_1_), channel_id=1, source_target_pairs={{31,0},{30,1},{1,2},{0,3},{3,4},{2,5},{5,6},{4,7},{7,8},{6,9},{9,1... | collective-permute-start | bytes 147464 | tf_op jit(solution)/shard_map/ppermute | solution.py:678
  4.5 1.6 %collective-permute-start.3 = (f32[32,384]{1,0:T(8,128)}, f32[32,384]{1,0:T(8,128)S(1)}, u32[]{:S(2)}, u32[]{:S(2)}) collective-permute-start(f32[32,384]{1,0:T(8,128)} %get-tuple-element.7.refs_0_.refs_1_), channel_id=1, source_target_pairs={{30,0},{31,1},{0,2},{1,3},{2,4},{3,5},{4,6},{5,7},{6,8},{7,9},{8,1... | collective-permute-start | bytes 147464 | tf_op jit(solution)/shard_map/ppermute | solution.py:678
  6.1 2.9 %collective-permute-start.2 = (f32[32,384]{1,0:T(8,128)}, f32[32,384]{1,0:T(8,128)S(1)}, u32[]{:S(2)}, u32[]{:S(2)}) collective-permute-start(f32[32,384]{1,0:T(8,128)} %get-tuple-element.7.refs_0_.refs_1_), channel_id=1, source_target_pairs={{3,0},{2,1},{5,2},{4,3},{7,4},{6,5},{9,6},{8,7},{11,8},{10,9},{13,... | collective-permute-start | bytes 147464 | tf_op jit(solution)/shard_map/ppermute | solution.py:678
  9.0 0.4 %collective-permute-start.1 = (f32[32,384]{1,0:T(8,128)}, f32[32,384]{1,0:T(8,128)S(1)}, u32[]{:S(2)}, u32[]{:S(2)}) collective-permute-start(f32[32,384]{1,0:T(8,128)} %get-tuple-element.7.refs_0_.refs_1_), channel_id=1, source_target_pairs={{2,0},{3,1},{4,2},{5,3},{6,4},{7,5},{8,6},{9,7},{10,8},{11,9},{12,... | collective-permute-start | bytes 147464 | tf_op jit(solution)/shard_map/ppermute | solution.py:678
  9.4 1.6 %collective-permute-start = (f32[32,384]{1,0:T(8,128)}, f32[32,384]{1,0:T(8,128)S(1)}, u32[]{:S(2)}, u32[]{:S(2)}) collective-permute-start(f32[32,384]{1,0:T(8,128)} %get-tuple-element.7.refs_0_.refs_1_), channel_id=1, source_target_pairs={{1,0},{0,1},{3,2},{2,3},{5,4},{4,5},{7,6},{6,7},{9,8},{8,9},{11,10... | collective-permute-start | bytes 147464 | tf_op jit(solution)/shard_map/ppermute | solution.py:678
  11.1 0.0 copy-start.3
  11.1 2.7 %all-to-all-start = ((f32[32,8,128]{2,1,0:T(8,128)}), f32[32,8,128]{2,1,0:T(8,128)S(1)}, u32[]{:S(2)}, u32[]{:S(2)}) async-start(f32[32,8,128]{2,1,0:T(8,128)} %get-tuple-element.8), calls=%async_computation | async-start | bytes 262144 | tf_op jit(solution)/shard_map/all_to_all | solution.py:717
  13.8 0.1 pad_add_fusion.refs_0_
  13.9 0.0 copy-start
  13.9 0.0 copy-start.1
  13.9 0.0 copy-start.2
  13.9 0.0 copy-start.4
  13.9 0.0 collective-permute-done.4.refs_5_.refs_6_
  13.9 0.0 collective-permute-done.3.refs_4_.refs_5_
  13.9 0.0 collective-permute-done.2.refs_3_.refs_4_
  13.9 0.0 collective-permute-done.1.refs_2_.refs_3_
  13.9 0.0 collective-permute-done.refs_1_.refs_2_
  13.9 0.0 copy-done.3
  13.9 11.2 %shard_map.74.refs_8_ = f32[16,384]{1,0:T(8,128)S(1)} custom-call(f32[32,384]{1,0:T(8,128)S(1)} %copy-done.3, f32[32,384]{1,0:T(8,128)S(1)} %collective-permute-done.refs_1_.refs_2_, f32[32,384]{1,0:T(8,128)S(1)} %collective-permute-done.1.refs_2_.refs_3_, f32[32,384]{1,0:T(8,128)S(1)} %collective-permute-done.2.refs_3_.refs_4_, ...), custom_call_target="tpu_custom_call" | custom-call | flops 10000000000 | bytes 100000 | tf_op jit(solution)/shard_map/pallas_call | solution.py:650
  25.1 0.0 all-to-all-done
  25.1 0.0 copy-done
  25.1 0.0 copy-done.1
  25.1 0.0 copy-done.2
  25.2 0.0 copy-done.4
  25.2 2.4 %shard_map.75 = f32[3,2,3,2,128]{4,3,2,1,0:T(2,128)} custom-call(s32[2]{0:T(128)S(1)} %pad_add_fusion.refs_0_, f32[32,384]{1,0:T(8,128)S(1)} %copy-done.3, f32[32,384]{1,0:T(8,128)S(1)} %collective-permute-done.refs_1_.refs_2_, f32[32,384]{1,0:T(8,128)S(1)} %collective-permute-done.1.refs_2_.refs_3_, f32[32,384]{1,0:T(8,128)S(1)} %collective-permute-done.2.refs_3_.refs_4_, ...), custom_call_target="tpu_custom_call" | custom-call | flops 100000000 | bytes 100000 | tf_op jit(solution)/shard_map/pallas_call | solution.py:650
Async XLA Ops:
  2.0 11.8 %collective-permute-start.4 = (f32[32,384]{1,0:T(8,128)}, f32[32,384]{1,0:T(8,128)S(1)}, u32[]{:S(2)}, u32[]{:S(2)}) collective-permute-start(f32[32,384]{1,0:T(8,128)} %get-tuple-element.7.refs_0_.refs_1_), channel_id=1, source_target_pairs={{31,0},{30,1},{1,2},{0,3},{3,4},{2,5},{5,6},{4,7},{7,8},{6,9},{9,1... | collective-permute-start | bytes 147464 | tf_op jit(solution)/shard_map/ppermute | solution.py:678
  4.5 9.4 %collective-permute-start.3 = (f32[32,384]{1,0:T(8,128)}, f32[32,384]{1,0:T(8,128)S(1)}, u32[]{:S(2)}, u32[]{:S(2)}) collective-permute-start(f32[32,384]{1,0:T(8,128)} %get-tuple-element.7.refs_0_.refs_1_), channel_id=1, source_target_pairs={{30,0},{31,1},{0,2},{1,3},{2,4},{3,5},{4,6},{5,7},{6,8},{7,9},{8,1... | collective-permute-start | bytes 147464 | tf_op jit(solution)/shard_map/ppermute | solution.py:678
  6.1 7.8 %collective-permute-start.2 = (f32[32,384]{1,0:T(8,128)}, f32[32,384]{1,0:T(8,128)S(1)}, u32[]{:S(2)}, u32[]{:S(2)}) collective-permute-start(f32[32,384]{1,0:T(8,128)} %get-tuple-element.7.refs_0_.refs_1_), channel_id=1, source_target_pairs={{3,0},{2,1},{5,2},{4,3},{7,4},{6,5},{9,6},{8,7},{11,8},{10,9},{13,... | collective-permute-start | bytes 147464 | tf_op jit(solution)/shard_map/ppermute | solution.py:678
  9.0 4.9 %collective-permute-start.1 = (f32[32,384]{1,0:T(8,128)}, f32[32,384]{1,0:T(8,128)S(1)}, u32[]{:S(2)}, u32[]{:S(2)}) collective-permute-start(f32[32,384]{1,0:T(8,128)} %get-tuple-element.7.refs_0_.refs_1_), channel_id=1, source_target_pairs={{2,0},{3,1},{4,2},{5,3},{6,4},{7,5},{8,6},{9,7},{10,8},{11,9},{12,... | collective-permute-start | bytes 147464 | tf_op jit(solution)/shard_map/ppermute | solution.py:678
  9.4 4.5 %collective-permute-start = (f32[32,384]{1,0:T(8,128)}, f32[32,384]{1,0:T(8,128)S(1)}, u32[]{:S(2)}, u32[]{:S(2)}) collective-permute-start(f32[32,384]{1,0:T(8,128)} %get-tuple-element.7.refs_0_.refs_1_), channel_id=1, source_target_pairs={{1,0},{0,1},{3,2},{2,3},{5,4},{4,5},{7,6},{6,7},{9,8},{8,9},{11,10... | collective-permute-start | bytes 147464 | tf_op jit(solution)/shard_map/ppermute | solution.py:678
  11.1 2.8 %copy-start.3 = (f32[32,384]{1,0:T(8,128)S(1)}, f32[32,384]{1,0:T(8,128)}, u32[]{:S(2)}) copy-start(f32[32,384]{1,0:T(8,128)} %get-tuple-element.7.refs_0_.refs_1_) | copy-start | bytes 147460
  11.1 14.0 %all-to-all-start = ((f32[32,8,128]{2,1,0:T(8,128)}), f32[32,8,128]{2,1,0:T(8,128)S(1)}, u32[]{:S(2)}, u32[]{:S(2)}) async-start(f32[32,8,128]{2,1,0:T(8,128)} %get-tuple-element.8), calls=%async_computation | async-start | bytes 262144 | tf_op jit(solution)/shard_map/all_to_all | solution.py:717
  13.9 11.3 %copy-start = (bf16[384,512]{1,0:T(8,128)(2,1)S(1)}, bf16[384,512]{1,0:T(8,128)(2,1)}, u32[]{:S(2)}) copy-start(bf16[384,512]{1,0:T(8,128)(2,1)} %constant.19.clone.refs_10_) | copy-start | bytes 1179652
  13.9 11.3 %copy-start.1 = (bf16[384,512]{1,0:T(8,128)(2,1)S(1)}, bf16[384,512]{1,0:T(8,128)(2,1)}, u32[]{:S(2)}) copy-start(bf16[384,512]{1,0:T(8,128)(2,1)} %constant.18.clone.refs_9_) | copy-start | bytes 1179652
  13.9 11.3 %copy-start.2 = (f32[256,128]{1,0:T(8,128)S(1)}, f32[256,128]{1,0:T(8,128)}, u32[]{:S(2)}) copy-start(f32[256,128]{1,0:T(8,128)} %constant.17.clone.refs_12_) | copy-start | bytes 393220
  13.9 11.3 %copy-start.4 = (f32[16,48]{1,0:T(8,128)S(1)}, f32[16,48]{1,0:T(8,128)}, u32[]{:S(2)}) copy-start(f32[16,48]{1,0:T(8,128)} %constant.16.clone.refs_11_) | copy-start | bytes 9220

commit v9 on v7

--- a/solution.py
+++ b/solution.py
@@ -551,7 +551,9 @@
                 done = lefts[number][x]
                 lefts[number][x] = value if done is None else done + value
     left = jnp.concatenate([jnp.concatenate(rows, axis=0) for rows in lefts], axis=1)
-    coarse = mul(left, coarse_z_ref[...], HIGHEST)
+    parts = mul(jnp.concatenate(split(left, 2), axis=0).astype(BF16), coarse_z_ref[...])
+    count = left.shape[0]
+    coarse = parts[:count] + pltpu.roll(parts[:count], 128 - brick.zpad, 1) + parts[count:]
     lane = lax.broadcasted_iota(jnp.int32, (brick.py, 128), 1)
     for x in range(brick.px):
         block, shift = divmod(x, brick.group)
@@ -632,7 +634,7 @@
     found = {}
     sender = {}
     msgs = []
-    for dx in (1, 0, -1):
+    for dx in (1, -1, 0):
         for dy in (0, -1, 1):
             if (dx, dy) == (0, 0):
                 continue
@@ -656,6 +658,10 @@
     xz_high = along_xz.astype(BF16)
     xz_low = (along_xz - xz_high.astype(np.float32)).astype(BF16)
     coarse_z = coarse_table(brick)
+    coarse_high = coarse_z.astype(BF16)
+    coarse_low = (coarse_z - coarse_high.astype(np.float32)).astype(BF16)
+    coarse_pair = coarse_high.copy()
+    coarse_pair[:, brick.zpad : 2 * brick.zpad] = coarse_low[:, : brick.zpad]
     place = jnp.stack([lax.axis_index("space"), lax.axis_index("sub")]).astype(jnp.int32)
 
     turned = (positions.transpose(0, 1, 3, 2, 4), charges.transpose(0, 2, 1, 3))
@@ -721,7 +727,7 @@
         xz_high,
         xz_low,
         jnp.asarray(along_y),
-        jnp.asarray(coarse_z),
+        coarse_pair,
         out_spec=WHOLE,
     )
     return forces.transpose(0, 1, 3, 2, 4)

time: 27.8 us -> 27.8 us (level)
  no operation moved by 1% of the time
where the time goes in v9:
time: 27.8 us; the launch traced here: 27.5 us
  Pallas kernels  15.5 us (56%)
  starting transfers between devices  11.7 us (42%)
    pallas_call x3, Pallas kernels, call(): pl.pallas_call(kernel, out_shape=out_shape, in_specs=in_specs, out_specs=...  15.5 us
    ppermute x5, starting transfers between devices, neighbours(): msgs.append(lax.ppermute(msg, ('space', 'sub'), pairs))  9.05 us
    all_to_all x1, starting transfers between devices, body(): whole = lax.all_to_all(coarse, ('space', 'sub'), 0, 0, tiled=True)  2.69 us
  transfers between devices with their start and end apart: 6, of which 0 were waited for; matrix products, arithmetic and copies ran while one was open for 0% of the time, Pallas kernels for 41%

profile of v9, /device:TPU:0, one launch (start us, length us, event | category | flops | bytes accessed | tf_op | source)
XLA Modules:
  0.0 27.5 jit_solution(589586746666473544)
XLA Ops:
  0.0 2.0 %shard_map.73 = (f32[32,384]{1,0:T(8,128)}, f32[32,8,128]{2,1,0:T(8,128)}) custom-call(s32[2,2,3]{2,1,0:T(2,128)} %refs_0_.1, f32[3,2,3,2,128]{4,3,2,1,0:T(2,128)} %bitcast.7, f32[2,3,2,128]{3,2,1,0:T(2,128)} %bitcast.8), custom_call_target="tpu_custom_call" | custom-call | flops 10000000 | bytes 100000 | tf_op jit(solution)/shard_map/pallas_call | solution.py:621
  2.0 3.0 %collective-permute-start.4 = (f32[32,384]{1,0:T(8,128)}, f32[32,384]{1,0:T(8,128)S(1)}, u32[]{:S(2)}, u32[]{:S(2)}) collective-permute-start(f32[32,384]{1,0:T(8,128)} %get-tuple-element.7.refs_0_.refs_1_), channel_id=1, source_target_pairs={{1,0},{0,1},{3,2},{2,3},{5,4},{4,5},{7,6},{6,7},{9,8},{8,9},{11,10... | collective-permute-start | bytes 147464 | tf_op jit(solution)/shard_map/ppermute | solution.py:649
  5.1 0.0 collective-permute-start.3
  5.1 1.5 %collective-permute-start.2 = (f32[32,384]{1,0:T(8,128)}, f32[32,384]{1,0:T(8,128)S(1)}, u32[]{:S(2)}, u32[]{:S(2)}) collective-permute-start(f32[32,384]{1,0:T(8,128)} %get-tuple-element.7.refs_0_.refs_1_), channel_id=1, source_target_pairs={{30,0},{31,1},{0,2},{1,3},{2,4},{3,5},{4,6},{5,7},{6,8},{7,9},{8,1... | collective-permute-start | bytes 147464 | tf_op jit(solution)/shard_map/ppermute | solution.py:649
  6.6 3.8 %collective-permute-start.1 = (f32[32,384]{1,0:T(8,128)}, f32[32,384]{1,0:T(8,128)S(1)}, u32[]{:S(2)}, u32[]{:S(2)}) collective-permute-start(f32[32,384]{1,0:T(8,128)} %get-tuple-element.7.refs_0_.refs_1_), channel_id=1, source_target_pairs={{3,0},{2,1},{5,2},{4,3},{7,4},{6,5},{9,6},{8,7},{11,8},{10,9},{13,... | collective-permute-start | bytes 147464 | tf_op jit(solution)/shard_map/ppermute | solution.py:649
  10.4 0.7 %collective-permute-start = (f32[32,384]{1,0:T(8,128)}, f32[32,384]{1,0:T(8,128)S(1)}, u32[]{:S(2)}, u32[]{:S(2)}) collective-permute-start(f32[32,384]{1,0:T(8,128)} %get-tuple-element.7.refs_0_.refs_1_), channel_id=1, source_target_pairs={{2,0},{3,1},{4,2},{5,3},{6,4},{7,5},{8,6},{9,7},{10,8},{11,9},{12,... | collective-permute-start | bytes 147464 | tf_op jit(solution)/shard_map/ppermute | solution.py:649
  11.1 0.0 copy-start.3
  11.1 2.7 %all-to-all-start = ((f32[32,8,128]{2,1,0:T(8,128)}), f32[32,8,128]{2,1,0:T(8,128)S(1)}, u32[]{:S(2)}, u32[]{:S(2)}) async-start(f32[32,8,128]{2,1,0:T(8,128)} %get-tuple-element.8), calls=%async_computation | async-start | bytes 262144 | tf_op jit(solution)/shard_map/all_to_all | solution.py:688
  13.8 0.1 pad_add_fusion.refs_0_
  13.9 0.0 copy-start
  13.9 0.0 copy-start.1
  13.9 0.0 copy-start.2
  13.9 0.0 copy-start.4
  13.9 0.0 collective-permute-done.4.refs_5_.refs_6_
  13.9 0.0 collective-permute-done.3.refs_4_.refs_5_
  13.9 0.0 collective-permute-done.2.refs_3_.refs_4_
  13.9 0.0 collective-permute-done.1.refs_2_.refs_3_
  13.9 0.0 collective-permute-done.refs_1_.refs_2_
  13.9 0.0 copy-done.3
  13.9 11.2 %shard_map.74.refs_8_ = f32[16,384]{1,0:T(8,128)S(1)} custom-call(f32[32,384]{1,0:T(8,128)S(1)} %copy-done.3, f32[32,384]{1,0:T(8,128)S(1)} %collective-permute-done.refs_1_.refs_2_, f32[32,384]{1,0:T(8,128)S(1)} %collective-permute-done.1.refs_2_.refs_3_, f32[32,384]{1,0:T(8,128)S(1)} %collective-permute-done.2.refs_3_.refs_4_, ...), custom_call_target="tpu_custom_call" | custom-call | flops 10000000000 | bytes 100000 | tf_op jit(solution)/shard_map/pallas_call | solution.py:621
  25.1 0.0 all-to-all-done
  25.2 0.0 copy-done
  25.2 0.0 copy-done.1
  25.2 0.0 copy-done.2
  25.2 0.0 copy-done.4
  25.2 2.3 %shard_map.75 = f32[3,2,3,2,128]{4,3,2,1,0:T(2,128)} custom-call(s32[2]{0:T(128)S(1)} %pad_add_fusion.refs_0_, f32[32,384]{1,0:T(8,128)S(1)} %copy-done.3, f32[32,384]{1,0:T(8,128)S(1)} %collective-permute-done.refs_1_.refs_2_, f32[32,384]{1,0:T(8,128)S(1)} %collective-permute-done.1.refs_2_.refs_3_, f32[32,384]{1,0:T(8,128)S(1)} %collective-permute-done.2.refs_3_.refs_4_, ...), custom_call_target="tpu_custom_call" | custom-call | flops 100000000 | bytes 100000 | tf_op jit(solution)/shard_map/pallas_call | solution.py:621
Async XLA Ops:
  2.0 11.8 %collective-permute-start.4 = (f32[32,384]{1,0:T(8,128)}, f32[32,384]{1,0:T(8,128)S(1)}, u32[]{:S(2)}, u32[]{:S(2)}) collective-permute-start(f32[32,384]{1,0:T(8,128)} %get-tuple-element.7.refs_0_.refs_1_), channel_id=1, source_target_pairs={{1,0},{0,1},{3,2},{2,3},{5,4},{4,5},{7,6},{6,7},{9,8},{8,9},{11,10... | collective-permute-start | bytes 147464 | tf_op jit(solution)/shard_map/ppermute | solution.py:649
  5.1 8.8 %collective-permute-start.3 = (f32[32,384]{1,0:T(8,128)}, f32[32,384]{1,0:T(8,128)S(1)}, u32[]{:S(2)}, u32[]{:S(2)}) collective-permute-start(f32[32,384]{1,0:T(8,128)} %get-tuple-element.7.refs_0_.refs_1_), channel_id=1, source_target_pairs={{31,0},{30,1},{1,2},{0,3},{3,4},{2,5},{5,6},{4,7},{7,8},{6,9},{9,1... | collective-permute-start | bytes 147464 | tf_op jit(solution)/shard_map/ppermute | solution.py:649
  5.1 8.8 %collective-permute-start.2 = (f32[32,384]{1,0:T(8,128)}, f32[32,384]{1,0:T(8,128)S(1)}, u32[]{:S(2)}, u32[]{:S(2)}) collective-permute-start(f32[32,384]{1,0:T(8,128)} %get-tuple-element.7.refs_0_.refs_1_), channel_id=1, source_target_pairs={{30,0},{31,1},{0,2},{1,3},{2,4},{3,5},{4,6},{5,7},{6,8},{7,9},{8,1... | collective-permute-start | bytes 147464 | tf_op jit(solution)/shard_map/ppermute | solution.py:649
  6.6 7.3 %collective-permute-start.1 = (f32[32,384]{1,0:T(8,128)}, f32[32,384]{1,0:T(8,128)S(1)}, u32[]{:S(2)}, u32[]{:S(2)}) collective-permute-start(f32[32,384]{1,0:T(8,128)} %get-tuple-element.7.refs_0_.refs_1_), channel_id=1, source_target_pairs={{3,0},{2,1},{5,2},{4,3},{7,4},{6,5},{9,6},{8,7},{11,8},{10,9},{13,... | collective-permute-start | bytes 147464 | tf_op jit(solution)/shard_map/ppermute | solution.py:649
  10.4 3.5 %collective-permute-start = (f32[32,384]{1,0:T(8,128)}, f32[32,384]{1,0:T(8,128)S(1)}, u32[]{:S(2)}, u32[]{:S(2)}) collective-permute-start(f32[32,384]{1,0:T(8,128)} %get-tuple-element.7.refs_0_.refs_1_), channel_id=1, source_target_pairs={{2,0},{3,1},{4,2},{5,3},{6,4},{7,5},{8,6},{9,7},{10,8},{11,9},{12,... | collective-permute-start | bytes 147464 | tf_op jit(solution)/shard_map/ppermute | solution.py:649
  11.1 2.8 %copy-start.3 = (f32[32,384]{1,0:T(8,128)S(1)}, f32[32,384]{1,0:T(8,128)}, u32[]{:S(2)}) copy-start(f32[32,384]{1,0:T(8,128)} %get-tuple-element.7.refs_0_.refs_1_) | copy-start | bytes 147460
  11.1 14.1 %all-to-all-start = ((f32[32,8,128]{2,1,0:T(8,128)}), f32[32,8,128]{2,1,0:T(8,128)S(1)}, u32[]{:S(2)}, u32[]{:S(2)}) async-start(f32[32,8,128]{2,1,0:T(8,128)} %get-tuple-element.8), calls=%async_computation | async-start | bytes 262144 | tf_op jit(solution)/shard_map/all_to_all | solution.py:688
  13.9 11.3 %copy-start = (bf16[384,512]{1,0:T(8,128)(2,1)S(1)}, bf16[384,512]{1,0:T(8,128)(2,1)}, u32[]{:S(2)}) copy-start(bf16[384,512]{1,0:T(8,128)(2,1)} %constant.18.clone.refs_10_) | copy-start | bytes 1179652
  13.9 11.3 %copy-start.1 = (bf16[384,512]{1,0:T(8,128)(2,1)S(1)}, bf16[384,512]{1,0:T(8,128)(2,1)}, u32[]{:S(2)}) copy-start(bf16[384,512]{1,0:T(8,128)(2,1)} %constant.17.clone.refs_9_) | copy-start | bytes 1179652
  13.9 11.3 %copy-start.2 = (bf16[256,128]{1,0:T(8,128)(2,1)S(1)}, bf16[256,128]{1,0:T(8,128)(2,1)}, u32[]{:S(2)}) copy-start(bf16[256,128]{1,0:T(8,128)(2,1)} %constant.19.clone.refs_12_) | copy-start | bytes 196612
  13.9 11.3 %copy-start.4 = (f32[16,48]{1,0:T(8,128)S(1)}, f32[16,48]{1,0:T(8,128)}, u32[]{:S(2)}) copy-start(f32[16,48]{1,0:T(8,128)} %constant.16.clone.refs_11_) | copy-start | bytes 9220

commit v10 on v9

--- a/solution.py
+++ b/solution.py
@@ -465,8 +465,8 @@
 
 def potential_kernel(brick, sender, n_msgs, *refs):
     atoms = brick.atoms
-    place_ref, msg_ref = refs[0:2]
-    other_msgs = refs[2 : 2 + n_msgs]
+    msg_ref = refs[0]
+    other_msgs = refs[1 : 1 + n_msgs]
     (
         whole_ref,
         short_ref,
@@ -476,7 +476,7 @@
         coarse_z_ref,
         out_ref,
         pot_ref,
-    ) = refs[2 + n_msgs :]
+    ) = refs[1 + n_msgs :]
     step_y = POINTS * brick.by
     rows_y = brick.py + step_y
     in_lanes = xz_high_ref.shape[0]
@@ -515,8 +515,8 @@
 
     total_x = 2 * brick.bx * brick.n_space
     total_y = 2 * brick.by * brick.n_sub
-    first_x = place_ref[0] * (2 * brick.bx)
-    first_y = place_ref[1] * (2 * brick.by)
+    first_x = lax.axis_index("space") * (2 * brick.bx)
+    first_y = lax.axis_index("sub") * (2 * brick.by)
     out_rows = round_up(brick.px, 8)
     shape = (out_rows, brick.n_space * brick.coarse_rows)
     point = lax.broadcasted_iota(jnp.int32, shape, 0)
@@ -634,7 +634,7 @@
     found = {}
     sender = {}
     msgs = []
-    for dx in (1, -1, 0):
+    for dx in (1, 0, -1):
         for dy in (0, -1, 1):
             if (dx, dy) == (0, 0):
                 continue
@@ -662,7 +662,6 @@
     coarse_low = (coarse_z - coarse_high.astype(np.float32)).astype(BF16)
     coarse_pair = coarse_high.copy()
     coarse_pair[:, brick.zpad : 2 * brick.zpad] = coarse_low[:, : brick.zpad]
-    place = jnp.stack([lax.axis_index("space"), lax.axis_index("sub")]).astype(jnp.int32)
 
     turned = (positions.transpose(0, 1, 3, 2, 4), charges.transpose(0, 2, 1, 3))
     msg, coarse = call(
@@ -714,12 +713,11 @@
     forces = call(
         functools.partial(potential_kernel, brick, sender, len(msgs)),
         jax.ShapeDtypeStruct((comps, size_x, size_z, size_y, atoms), F32),
-        [SMEM] + [VMEM] * (7 + len(msgs)),
+        [VMEM] * (7 + len(msgs)),
         [
             pltpu.VMEM((brick.px, brick.py, 128), F32),
         ],
         10**8,
-        place,
         msg,
         *msgs,
         whole,

time: 27.8 us -> 27.2 us (0.978)
  Pallas kernels: 15.5 us -> 15 us
    pallas_call x3, Pallas kernels: 15.5 us -> 15 us  [call(): pl.pallas_call(kernel, out_shape=out_shape, in_specs=in_specs, out_specs=...]
  transfers between devices with their start and end apart: 6 -> 6, of which waited for: 0 -> 0; matrix products, arithmetic and copies ran while one was open for 0% -> 0% of each run, Pallas kernels for 41% -> 42%
where the time goes in v10:
time: 27.2 us; the launch traced here: 26.9 us
  Pallas kernels  15 us (55%)
  starting transfers between devices  11.7 us (43%)
    pallas_call x3, Pallas kernels, call(): pl.pallas_call(kernel, out_shape=out_shape, in_specs=in_specs, out_specs=...  15 us
    ppermute x5, starting transfers between devices, neighbours(): msgs.append(lax.ppermute(msg, ('space', 'sub'), pairs))  9.04 us
    all_to_all x1, starting transfers between devices, body(): whole = lax.all_to_all(coarse, ('space', 'sub'), 0, 0, tiled=True)  2.69 us
  transfers between devices with their start and end apart: 6, of which 0 were waited for; matrix products, arithmetic and copies ran while one was open for 0% of the time, Pallas kernels for 42%

profile of v10, /device:TPU:0, one launch (start us, length us, event | category | flops | bytes accessed | tf_op | source)
XLA Modules:
  0.0 26.9 jit_solution(2840271040185125269)
XLA Ops:
  0.0 2.0 %shard_map.73 = (f32[32,384]{1,0:T(8,128)}, f32[32,8,128]{2,1,0:T(8,128)}) custom-call(s32[2,2,3]{2,1,0:T(2,128)} %refs_0_.1, f32[3,2,3,2,128]{4,3,2,1,0:T(2,128)} %bitcast.5, f32[2,3,2,128]{3,2,1,0:T(2,128)} %bitcast.6), custom_call_target="tpu_custom_call" | custom-call | flops 10000000 | bytes 100000 | tf_op jit(solution)/shard_map/pallas_call | solution.py:621
  2.0 2.5 %collective-permute-start.4 = (f32[32,384]{1,0:T(8,128)}, f32[32,384]{1,0:T(8,128)S(1)}, u32[]{:S(2)}, u32[]{:S(2)}) collective-permute-start(f32[32,384]{1,0:T(8,128)} %get-tuple-element.7.refs_0_), channel_id=1, source_target_pairs={{31,0},{30,1},{1,2},{0,3},{3,4},{2,5},{5,6},{4,7},{7,8},{6,9},{9,1... | collective-permute-start | bytes 147464 | tf_op jit(solution)/shard_map/ppermute | solution.py:649
  4.5 1.6 %collective-permute-start.3 = (f32[32,384]{1,0:T(8,128)}, f32[32,384]{1,0:T(8,128)S(1)}, u32[]{:S(2)}, u32[]{:S(2)}) collective-permute-start(f32[32,384]{1,0:T(8,128)} %get-tuple-element.7.refs_0_), channel_id=1, source_target_pairs={{30,0},{31,1},{0,2},{1,3},{2,4},{3,5},{4,6},{5,7},{6,8},{7,9},{8,1... | collective-permute-start | bytes 147464 | tf_op jit(solution)/shard_map/ppermute | solution.py:649
  6.1 0.5 %collective-permute-start.2 = (f32[32,384]{1,0:T(8,128)}, f32[32,384]{1,0:T(8,128)S(1)}, u32[]{:S(2)}, u32[]{:S(2)}) collective-permute-start(f32[32,384]{1,0:T(8,128)} %get-tuple-element.7.refs_0_), channel_id=1, source_target_pairs={{1,0},{0,1},{3,2},{2,3},{5,4},{4,5},{7,6},{6,7},{9,8},{8,9},{11,10... | collective-permute-start | bytes 147464 | tf_op jit(solution)/shard_map/ppermute | solution.py:649
  6.6 3.5 %collective-permute-start.1 = (f32[32,384]{1,0:T(8,128)}, f32[32,384]{1,0:T(8,128)S(1)}, u32[]{:S(2)}, u32[]{:S(2)}) collective-permute-start(f32[32,384]{1,0:T(8,128)} %get-tuple-element.7.refs_0_), channel_id=1, source_target_pairs={{3,0},{2,1},{5,2},{4,3},{7,4},{6,5},{9,6},{8,7},{11,8},{10,9},{13,... | collective-permute-start | bytes 147464 | tf_op jit(solution)/shard_map/ppermute | solution.py:649
  10.1 1.0 %collective-permute-start = (f32[32,384]{1,0:T(8,128)}, f32[32,384]{1,0:T(8,128)S(1)}, u32[]{:S(2)}, u32[]{:S(2)}) collective-permute-start(f32[32,384]{1,0:T(8,128)} %get-tuple-element.7.refs_0_), channel_id=1, source_target_pairs={{2,0},{3,1},{4,2},{5,3},{6,4},{7,5},{8,6},{9,7},{10,8},{11,9},{12,... | collective-permute-start | bytes 147464 | tf_op jit(solution)/shard_map/ppermute | solution.py:649
  11.1 0.0 copy-start.3
  11.1 2.7 %all-to-all-start = ((f32[32,8,128]{2,1,0:T(8,128)}), f32[32,8,128]{2,1,0:T(8,128)S(1)}, u32[]{:S(2)}, u32[]{:S(2)}) async-start(f32[32,8,128]{2,1,0:T(8,128)} %get-tuple-element.8), calls=%async_computation | async-start | bytes 262144 | tf_op jit(solution)/shard_map/all_to_all | solution.py:687
  13.8 0.0 copy-start
  13.8 0.0 copy-start.1
  13.8 0.0 copy-start.2
  13.8 0.0 copy-start.4
  13.8 0.0 collective-permute-done.4.refs_5_
  13.8 0.0 collective-permute-done.3.refs_4_
  13.8 0.0 collective-permute-done.2.refs_3_
  13.9 0.0 collective-permute-done.1.refs_2_
  13.9 0.0 collective-permute-done.refs_1_
  13.9 0.0 copy-done.3
  13.9 11.2 %shard_map.74.refs_7_ = f32[16,384]{1,0:T(8,128)S(1)} custom-call(f32[32,384]{1,0:T(8,128)S(1)} %copy-done.3, f32[32,384]{1,0:T(8,128)S(1)} %collective-permute-done.refs_1_, f32[32,384]{1,0:T(8,128)S(1)} %collective-permute-done.1.refs_2_, f32[32,384]{1,0:T(8,128)S(1)} %collective-permute-done.2.refs_3_, f32[32,384]{1,0:T(8,128)S(1)} %collective-permute-done.3.refs_4_, ...), custom_call_target="tpu_custom_call" | custom-call | flops 10000000000 | bytes 100000 | tf_op jit(solution)/shard_map/pallas_call | solution.py:621
  25.1 0.0 all-to-all-done
  25.1 0.0 copy-done
  25.1 0.0 copy-done.1
  25.1 0.0 copy-done.2
  25.1 0.0 copy-done.4
  25.1 1.8 %shard_map.75 = f32[3,2,3,2,128]{4,3,2,1,0:T(2,128)} custom-call(f32[32,384]{1,0:T(8,128)S(1)} %copy-done.3, f32[32,384]{1,0:T(8,128)S(1)} %collective-permute-done.refs_1_, f32[32,384]{1,0:T(8,128)S(1)} %collective-permute-done.1.refs_2_, f32[32,384]{1,0:T(8,128)S(1)} %collective-permute-done.2.refs_3_, f32[32,384]{1,0:T(8,128)S(1)} %collective-permute-done.3.refs_4_, ...), custom_call_target="tpu_custom_call" | custom-call | flops 100000000 | bytes 100000 | tf_op jit(solution)/shard_map/pallas_call | solution.py:621
Async XLA Ops:
  2.0 11.8 %collective-permute-start.4 = (f32[32,384]{1,0:T(8,128)}, f32[32,384]{1,0:T(8,128)S(1)}, u32[]{:S(2)}, u32[]{:S(2)}) collective-permute-start(f32[32,384]{1,0:T(8,128)} %get-tuple-element.7.refs_0_), channel_id=1, source_target_pairs={{31,0},{30,1},{1,2},{0,3},{3,4},{2,5},{5,6},{4,7},{7,8},{6,9},{9,1... | collective-permute-start | bytes 147464 | tf_op jit(solution)/shard_map/ppermute | solution.py:649
  4.5 9.3 %collective-permute-start.3 = (f32[32,384]{1,0:T(8,128)}, f32[32,384]{1,0:T(8,128)S(1)}, u32[]{:S(2)}, u32[]{:S(2)}) collective-permute-start(f32[32,384]{1,0:T(8,128)} %get-tuple-element.7.refs_0_), channel_id=1, source_target_pairs={{30,0},{31,1},{0,2},{1,3},{2,4},{3,5},{4,6},{5,7},{6,8},{7,9},{8,1... | collective-permute-start | bytes 147464 | tf_op jit(solution)/shard_map/ppermute | solution.py:649
  6.1 7.8 %collective-permute-start.2 = (f32[32,384]{1,0:T(8,128)}, f32[32,384]{1,0:T(8,128)S(1)}, u32[]{:S(2)}, u32[]{:S(2)}) collective-permute-start(f32[32,384]{1,0:T(8,128)} %get-tuple-element.7.refs_0_), channel_id=1, source_target_pairs={{1,0},{0,1},{3,2},{2,3},{5,4},{4,5},{7,6},{6,7},{9,8},{8,9},{11,10... | collective-permute-start | bytes 147464 | tf_op jit(solution)/shard_map/ppermute | solution.py:649
  6.6 7.3 %collective-permute-start.1 = (f32[32,384]{1,0:T(8,128)}, f32[32,384]{1,0:T(8,128)S(1)}, u32[]{:S(2)}, u32[]{:S(2)}) collective-permute-start(f32[32,384]{1,0:T(8,128)} %get-tuple-element.7.refs_0_), channel_id=1, source_target_pairs={{3,0},{2,1},{5,2},{4,3},{7,4},{6,5},{9,6},{8,7},{11,8},{10,9},{13,... | collective-permute-start | bytes 147464 | tf_op jit(solution)/shard_map/ppermute | solution.py:649
  10.1 3.8 %collective-permute-start = (f32[32,384]{1,0:T(8,128)}, f32[32,384]{1,0:T(8,128)S(1)}, u32[]{:S(2)}, u32[]{:S(2)}) collective-permute-start(f32[32,384]{1,0:T(8,128)} %get-tuple-element.7.refs_0_), channel_id=1, source_target_pairs={{2,0},{3,1},{4,2},{5,3},{6,4},{7,5},{8,6},{9,7},{10,8},{11,9},{12,... | collective-permute-start | bytes 147464 | tf_op jit(solution)/shard_map/ppermute | solution.py:649
  11.1 2.8 %copy-start.3 = (f32[32,384]{1,0:T(8,128)S(1)}, f32[32,384]{1,0:T(8,128)}, u32[]{:S(2)}) copy-start(f32[32,384]{1,0:T(8,128)} %get-tuple-element.7.refs_0_) | copy-start | bytes 147460
  11.1 14.0 %all-to-all-start = ((f32[32,8,128]{2,1,0:T(8,128)}), f32[32,8,128]{2,1,0:T(8,128)S(1)}, u32[]{:S(2)}, u32[]{:S(2)}) async-start(f32[32,8,128]{2,1,0:T(8,128)} %get-tuple-element.8), calls=%async_computation | async-start | bytes 262144 | tf_op jit(solution)/shard_map/all_to_all | solution.py:687
  13.8 11.3 %copy-start = (bf16[384,512]{1,0:T(8,128)(2,1)S(1)}, bf16[384,512]{1,0:T(8,128)(2,1)}, u32[]{:S(2)}) copy-start(bf16[384,512]{1,0:T(8,128)(2,1)} %constant.10.clone.refs_9_) | copy-start | bytes 1179652
  13.8 11.3 %copy-start.1 = (bf16[384,512]{1,0:T(8,128)(2,1)S(1)}, bf16[384,512]{1,0:T(8,128)(2,1)}, u32[]{:S(2)}) copy-start(bf16[384,512]{1,0:T(8,128)(2,1)} %constant.9.clone.refs_8_) | copy-start | bytes 1179652
  13.8 11.3 %copy-start.2 = (bf16[256,128]{1,0:T(8,128)(2,1)S(1)}, bf16[256,128]{1,0:T(8,128)(2,1)}, u32[]{:S(2)}) copy-start(bf16[256,128]{1,0:T(8,128)(2,1)} %constant.11.clone.refs_11_) | copy-start | bytes 196612
  13.8 11.3 %copy-start.4 = (f32[16,48]{1,0:T(8,128)S(1)}, f32[16,48]{1,0:T(8,128)}, u32[]{:S(2)}) copy-start(f32[16,48]{1,0:T(8,128)} %constant.8.clone.refs_10_) | copy-start | bytes 9220
